TPU v7x, 32 devices: a whole 2x2x4 slice. The times are simulated.
32 devices in a mesh: dp: 16 (over z, y, x), tensor: 2 (over core).
Axes of the slice: x: 2, y: 2, z: 4, core: 2. Of those that a mesh axis runs over, the one named last changes fastest.
Arguments:
- enc_params: float32 [2, 7077888], P('tensor', 'dp'), may hold values from -2.44948974 to 2.44948974, as said below
- enc_m1: float32 [2, 7077888], P('tensor', 'dp'), may hold values from -7.4505806e-08 to 7.4505806e-08
- enc_m2: float32 [2, 7077888], P('tensor', 'dp'), may hold values from 2.3901121e-18 to 9.5604485e-18
- pred_params: float32 [2, 1277952], P('tensor', 'dp'), may hold values from -2.44948974 to 2.44948974, as said below
- pred_m1: float32 [2, 1277952], P('tensor', 'dp'), may hold values from -7.4505806e-08 to 7.4505806e-08
- pred_m2: float32 [2, 1277952], P('tensor', 'dp'), may hold values from 2.3901121e-18 to 9.5604485e-18
- target_params: float32 [2, 7077888], P('tensor', 'dp'), may hold values from -2.44948974 to 2.44948974, as said below
- vecs: float32 [23936], replicated, may hold values from -6 to 6, as said below
- vec_m1: float32 [23936], replicated, may hold values from -2.9802322e-07 to 2.9802322e-07
- vec_m2: float32 [23936], replicated, may hold values from 3.8241794e-17 to 1.5535729e-16
- target_vecs: float32 [16384], replicated, may hold values from -6 to 6, as said below
- patches: bfloat16 [18816, 1536], P('dp', 'tensor'), may hold values from -6 to 6
- segment: int32 [18816], P('dp'), may hold values from 0 to 4, as said below
- context: int32 [18816], P('dp'), may hold values from 0 to 1, as said below
- step_count: int32 [1], replicated, may hold values from 1 to 20
Outputs:
- new_enc_params: float32 [2, 7077888], P('tensor', 'dp')
- new_enc_m1: float32 [2, 7077888], P('tensor', 'dp')
- new_enc_m2: float32 [2, 7077888], P('tensor', 'dp')
- enc_bf16: bfloat16 [2, 7077888], P('tensor', 'dp')
- new_pred_params: float32 [2, 1277952], P('tensor', 'dp')
- new_pred_m1: float32 [2, 1277952], P('tensor', 'dp')
- new_pred_m2: float32 [2, 1277952], P('tensor', 'dp')
- pred_bf16: bfloat16 [2, 1277952], P('tensor', 'dp')
- new_target_params: float32 [2, 7077888], P('tensor', 'dp')
- new_vecs: float32 [23936], replicated
- new_vec_m1: float32 [23936], replicated
- new_vec_m2: float32 [23936], replicated
- new_target_vecs: float32 [16384], replicated
- loss: float32 [], replicated
- grad_norm: float32 [], replicated
Inputs may be any that keep to these rules, and one draw needn't show every extreme that they name: `segment`: segment numbers count the samples of a pack from 0 and never fall within it. Sample 0 of a pack is a video of 2 to 6 frame pairs of 196 tokens; every later sample is an image of 196 tokens. In every draw some pack holds a video of 1176 tokens. The first token of every sample is a context token. `enc_params`: entries of each matrix block are normal with a deviation of a fixed multiple of one over the root of its fan-in. `pred_params`: as for enc_params. `target_params`: as for enc_params. `vecs`: gains near 1, biases and the mask token of both signs. `target_vecs`: gains near 1, biases of both signs.
All inputs are finite; a program needn't handle non-finite values.
Results may differ from a plain program's by a relative error of at most 0.0034.
Values may be sent and summed in bfloat16 or wider, within the bound.
No kernel may reach another device: no remote copies, remote signals or barrier semaphores. Data moves between devices by JAX's collectives and lax.ppermute only.
A program may use at most 1.0625 GiB of HBM per device.

v0:
```python
import math

import jax
import jax.numpy as jnp
from jax import lax
from jax.sharding import PartitionSpec as P

D = 1024
HEADS = 16
HEAD_DIM = 64
MLP = 4096
PATCH = 1536
PD = 384
PHEADS = 12
PHEAD_DIM = 32
PMLP = 1536


BETA_ONE = 0.9
BETA_TWO = 0.999
ADAM_EPS = 1e-08
RATE_MAT = 0.01
RATE_VEC = 0.05
DECAY = 0.05
CLIP = 0.0002
TAU = 0.75
NORM_EPS = 1e-06
VAR_EPS = 0.0001
LOCAL_BIAS = {
    "b_qkv": True,
    "b_pqkv": True,
    "b_up": False,
    "b_pup": False,
    "b_pin": False,
    "b_pproj": False,
}
ROW_GAINS = ("ln2_g", "ln2_b", "pln2_g", "pln2_b")


def enc_shapes(ways):
    return [
        ("w_patch", PATCH // ways, D),
        ("w_qkv", D, 3 * D // ways),
        ("w_out", D // ways, D),
        ("w_up", D, MLP // ways),
        ("w_down", MLP // ways, D),
    ]


def pred_shapes(ways):
    return [
        ("w_pin", D, PD // ways),
        ("w_pqkv", PD, 3 * PD // ways),
        ("w_pout", PD // ways, PD),
        ("w_pup", PD, PMLP // ways),
        ("w_pdown", PMLP // ways, PD),
        ("w_pproj", PD, D // ways),
    ]


def enc_vectors():
    return [
        ("b_patch", D),
        ("ln1_g", D),
        ("ln1_b", D),
        ("b_qkv", 3 * D),
        ("b_out", D),
        ("ln2_g", D),
        ("ln2_b", D),
        ("b_up", MLP),
        ("b_down", D),
        ("lnf_g", D),
        ("lnf_b", D),
    ]


def pred_vectors():
    return [
        ("b_pin", PD),
        ("mask_tok", PD),
        ("pln1_g", PD),
        ("pln1_b", PD),
        ("b_pqkv", 3 * PD),
        ("b_pout", PD),
        ("pln2_g", PD),
        ("pln2_b", PD),
        ("b_pup", PMLP),
        ("b_pdown", PD),
        ("plnf_g", PD),
        ("plnf_b", PD),
        ("b_pproj", D),
    ]


def unflat(flat_row, shapes):
    result = {}
    offset = 0
    for label, height, breadth in shapes:
        result[label] = flat_row[offset : offset + height * breadth].reshape(height, breadth)
        offset += height * breadth
    return result


def split_vector(vector, sections):
    result = {}
    offset = 0
    for label, length in sections:
        result[label] = vector[offset : offset + length]
        offset += length
    return result


def positions(segment_row):
    earlier = jnp.sum((segment_row[None, :] < segment_row[:, None]).astype(jnp.int32), axis=1)
    return (jnp.arange(segment_row.shape[0], dtype=jnp.int32) - earlier).astype(jnp.float32)


def sincos(places, width):
    half_width = width // 2
    freqs = jnp.exp(-math.log(10000.0) * jnp.arange(half_width).astype(jnp.float32) / half_width)
    angles = places[:, None] * freqs[None, :]
    return jnp.concatenate([jnp.sin(angles), jnp.cos(angles)], axis=1)


def layer_norm(values, gain, shift):
    centered = values - jnp.mean(values, axis=-1, keepdims=True)
    spread = jnp.mean(centered * centered, axis=-1, keepdims=True)
    return centered * lax.rsqrt(spread + NORM_EPS) * gain + shift


def plain_norm(values):
    centered = values - jnp.mean(values, axis=-1, keepdims=True)
    return centered * lax.rsqrt(jnp.mean(centered * centered, axis=-1, keepdims=True) + NORM_EPS)


def norm_backward(values, gain, shift, cotangent):
    return jax.vjp(layer_norm, values, gain, shift)[1](cotangent)


def matmul(left, right):
    return jnp.dot(left, right, preferred_element_type=jnp.float32)


def matmul_tn(left, right):
    return lax.dot_general(
        left, right, (((0,), (0,)), ((), ())), preferred_element_type=jnp.float32
    )


def matmul_nt(left, right):
    return lax.dot_general(
        left, right, (((1,), (1,)), ((), ())), preferred_element_type=jnp.float32
    )


def tensor_total(partial_sum):
    return lax.psum(partial_sum, "tensor")


def layer_total(partial_sum):
    return lax.psum(partial_sum, "tensor")


def tensor_back(partial_sum):
    return lax.psum(partial_sum.astype(jnp.bfloat16), "tensor").astype(jnp.float32)


def local_columns(vector, thirds, ways, member):
    if thirds:
        width = vector.shape[0] // 3
        slab = vector.reshape(3, width)
        return lax.dynamic_slice_in_dim(slab, member * (width // ways), width // ways, 1).reshape(
            -1
        )
    return lax.dynamic_slice_in_dim(
        vector, member * (vector.shape[0] // ways), vector.shape[0] // ways, 0
    )


def place_columns(local, length, thirds, ways, member):
    if thirds:
        slab = jnp.zeros((3, length // 3), jnp.float32)
        placed = lax.dynamic_update_slice_in_dim(
            slab, local.reshape(3, -1), member * (length // 3 // ways), 1
        )
        return placed.reshape(-1)
    return lax.dynamic_update_slice_in_dim(
        jnp.zeros((length,), jnp.float32), local, member * (length // ways), 0
    )


def attend_heads(queries, keys_all, values, allowed, head_dim):

    def attend_one_head(inputs):
        query_h, key_h, value_h = inputs
        scores = jnp.where(allowed, matmul_nt(query_h, key_h) * head_dim ** (-0.5), -1e30)
        peak = jnp.max(scores, axis=1, keepdims=True)
        expo = jnp.exp(scores - peak)
        total = jnp.sum(expo, axis=1, keepdims=True)
        mixed = matmul((expo / total).astype(jnp.bfloat16), value_h)
        return (mixed.astype(jnp.bfloat16), (peak + jnp.log(total))[:, 0])

    return lax.map(attend_one_head, (queries, keys_all, values))


def layer_forward(stream, mats, vectors, tag, heads, head_dim, allowed, ways, member):
    row_count = stream.shape[0]
    local_heads = heads // ways
    normed_low = layer_norm(stream, vectors[tag + "ln1_g"], vectors[tag + "ln1_b"]).astype(
        jnp.bfloat16
    )
    packed = matmul(normed_low, mats["w_" + tag + "qkv"]) + local_columns(
        vectors["b_" + tag + "qkv"], True, ways, member
    )
    heads_first = (
        packed.astype(jnp.bfloat16)
        .reshape(row_count, 3, local_heads, head_dim)
        .transpose(1, 2, 0, 3)
    )
    mixed, log_totals = attend_heads(
        heads_first[0], heads_first[1], heads_first[2], allowed, head_dim
    )
    mixed_rows = mixed.transpose(1, 0, 2).reshape(row_count, local_heads * head_dim)
    attn_part = matmul(mixed_rows, mats["w_" + tag + "out"])
    middle = stream + layer_total(attn_part) + vectors["b_" + tag + "out"]
    normed_two = layer_norm(middle, vectors[tag + "ln2_g"], vectors[tag + "ln2_b"]).astype(
        jnp.bfloat16
    )
    hidden = matmul(normed_two, mats["w_" + tag + "up"]) + local_columns(
        vectors["b_" + tag + "up"], False, ways, member
    )
    activated = jax.nn.gelu(hidden).astype(jnp.bfloat16)
    down_part = matmul(activated, mats["w_" + tag + "down"])
    result = middle + layer_total(down_part) + vectors["b_" + tag + "down"]
    kept = (
        stream,
        normed_low,
        heads_first,
        mixed_rows,
        log_totals,
        middle,
        normed_two,
        hidden,
        activated,
    )
    return (result, kept)


def layer_backward(grad_out, kept, mats, vectors, tag, heads, head_dim, allowed, ways):
    (
        stream,
        normed_low,
        heads_first,
        mixed_rows,
        log_totals,
        middle,
        normed_two,
        hidden,
        activated,
    ) = kept
    row_count = stream.shape[0]
    local_heads = heads // ways
    grads = {}
    grad_low = grad_out.astype(jnp.bfloat16)
    grads["w_" + tag + "down"] = matmul_tn(activated, grad_low)
    grads["b_" + tag + "down"] = jnp.sum(grad_out, axis=0)
    grad_act = matmul_nt(grad_low, mats["w_" + tag + "down"])
    grad_hidden = jax.vjp(jax.nn.gelu, hidden)[1](grad_act)[0].astype(jnp.bfloat16)
    grads["w_" + tag + "up"] = matmul_tn(normed_two, grad_hidden)
    grads["b_" + tag + "up"] = jnp.sum(grad_hidden.astype(jnp.float32), axis=0)
    normed_part = matmul_nt(grad_hidden, mats["w_" + tag + "up"])
    grad_normed = lax.psum(normed_part.astype(jnp.bfloat16), "tensor").astype(jnp.float32)
    grad_middle, grads[tag + "ln2_g"], grads[tag + "ln2_b"] = norm_backward(
        middle, vectors[tag + "ln2_g"], vectors[tag + "ln2_b"], grad_normed
    )
    grad_middle = grad_middle + grad_out
    grad_mid_low = grad_middle.astype(jnp.bfloat16)
    grads["w_" + tag + "out"] = matmul_tn(mixed_rows, grad_mid_low)
    grads["b_" + tag + "out"] = jnp.sum(grad_middle, axis=0)
    grad_mixed = matmul_nt(grad_mid_low, mats["w_" + tag + "out"]).astype(jnp.bfloat16)
    grad_heads = grad_mixed.reshape(row_count, local_heads, head_dim).transpose(1, 0, 2)

    def layer_one_head(inputs):
        query_h, key_h, value_h, total_h, grad_h = inputs
        scores = jnp.where(allowed, matmul_nt(query_h, key_h) * head_dim ** (-0.5), -1e30)
        probs = jnp.exp(scores - total_h[:, None])
        grad_probs = matmul_nt(grad_h, value_h)
        grad_value = matmul_tn(probs.astype(jnp.bfloat16), grad_h)
        grad_scores = probs * (grad_probs - jnp.sum(probs * grad_probs, axis=1, keepdims=True))
        grad_scores = grad_scores.astype(jnp.bfloat16)
        grad_query = matmul(grad_scores, key_h) * head_dim ** (-0.5)
        grad_key = matmul_tn(grad_scores, query_h) * head_dim ** (-0.5)
        return jnp.stack([grad_query, grad_key, grad_value])

    grad_qkv = lax.map(
        layer_one_head, (heads_first[0], heads_first[1], heads_first[2], log_totals, grad_heads)
    )
    grad_packed = (
        grad_qkv.transpose(2, 1, 0, 3)
        .reshape(row_count, 3 * local_heads * head_dim)
        .astype(jnp.bfloat16)
    )
    grads["w_" + tag + "qkv"] = matmul_tn(normed_low, grad_packed)
    grads["b_" + tag + "qkv"] = jnp.sum(grad_packed.astype(jnp.float32), axis=0)
    grad_first = tensor_back(matmul_nt(grad_packed, mats["w_" + tag + "qkv"]))
    grad_stream, grads[tag + "ln1_g"], grads[tag + "ln1_b"] = norm_backward(
        stream, vectors[tag + "ln1_g"], vectors[tag + "ln1_b"], grad_first
    )
    return (grad_stream + grad_middle, grads)


def adam(weight, first, second, grad, rate, decay, count):
    first_new = BETA_ONE * first + (1 - BETA_ONE) * grad
    second_new = BETA_TWO * second + (1 - BETA_TWO) * grad * grad
    first_hat = first_new / (1 - BETA_ONE**count)
    second_hat = second_new / (1 - BETA_TWO**count)
    weight_new = weight - rate * (first_hat / (jnp.sqrt(second_hat) + ADAM_EPS) + decay * weight)
    return (weight_new, first_new, second_new)


def shards(
    enc_params,
    enc_m1,
    enc_m2,
    pred_params,
    pred_m1,
    pred_m2,
    target_params,
    vecs,
    vec_m1,
    vec_m2,
    target_vecs,
    patches,
    segment,
    context,
    step_count,
):
    ways = lax.axis_size("tensor")
    member = lax.axis_index("tensor")
    dp_count = lax.axis_size("dp")
    enc_low = enc_params.astype(jnp.bfloat16)
    pred_low = pred_params.astype(jnp.bfloat16)
    enc_full, pred_full, target_full = (
        lax.all_gather(enc_low, "dp", axis=1, tiled=True),
        lax.all_gather(pred_low, "dp", axis=1, tiled=True),
        lax.all_gather(target_params.astype(jnp.bfloat16), "dp", axis=1, tiled=True),
    )
    mats = unflat(enc_full[0], enc_shapes(ways))
    mats.update(unflat(pred_full[0], pred_shapes(ways)))
    target_mats = unflat(target_full[0], enc_shapes(ways))
    vectors = split_vector(vecs, enc_vectors() + pred_vectors())
    target_vectors = split_vector(target_vecs, enc_vectors())
    places = positions(segment)
    same_sample = segment[:, None] == segment[None, :]
    context_mask = context > 0
    online_allowed = same_sample & context_mask[None, :]
    embed_pos = sincos(places, D)

    def embed(weight_set, vector_set):
        return (
            tensor_total(matmul(patches, weight_set["w_patch"])) + vector_set["b_patch"] + embed_pos
        )

    online_mid, online_kept = layer_forward(
        embed(mats, vectors), mats, vectors, "", HEADS, HEAD_DIM, online_allowed, ways, member
    )
    encoded_low = layer_norm(online_mid, vectors["lnf_g"], vectors["lnf_b"]).astype(jnp.bfloat16)
    target_mid, _ = layer_forward(
        embed(target_mats, target_vectors),
        target_mats,
        target_vectors,
        "",
        HEADS,
        HEAD_DIM,
        same_sample,
        ways,
        member,
    )
    targets = plain_norm(layer_norm(target_mid, target_vectors["lnf_g"], target_vectors["lnf_b"]))
    target_cols = lax.dynamic_slice_in_dim(targets, member * (D // ways), D // ways, 1)
    pin_local = matmul(encoded_low, mats["w_pin"]) + local_columns(
        vectors["b_pin"], False, ways, member
    )
    pin_full = lax.all_gather(pin_local, "tensor", axis=1, tiled=True)
    pred_in = jnp.where(context_mask[:, None], pin_full, vectors["mask_tok"][None, :]) + sincos(
        places, PD
    )
    pred_mid, pred_kept = layer_forward(
        pred_in, mats, vectors, "p", PHEADS, PHEAD_DIM, same_sample, ways, member
    )
    pred_rows = layer_norm(pred_mid, vectors["plnf_g"], vectors["plnf_b"]).astype(jnp.bfloat16)
    predicted = matmul(pred_rows, mats["w_pproj"]) + local_columns(
        vectors["b_pproj"], False, ways, member
    )
    target_mask = (1 - context).astype(jnp.float32)
    count_all, sum_all, square_all = lax.psum(
        (
            jnp.sum(target_mask),
            jnp.sum(target_mask[:, None] * predicted, axis=0),
            jnp.sum(target_mask[:, None] * predicted * predicted, axis=0),
        ),
        "dp",
    )
    difference = predicted - target_cols
    error = jnp.sum(target_mask[:, None] * jnp.abs(difference)) / (count_all * D)
    column_mean = sum_all / count_all
    column_var = square_all / count_all - column_mean * column_mean
    spread = jnp.sqrt(column_var + VAR_EPS)
    local_loss = error + jnp.sum((spread - 1.0) ** 2) / D / dp_count
    grad_var = (spread - 1.0) / (D * spread)
    grad_pred = target_mask[:, None] * (
        jnp.sign(difference) / (count_all * D)
        + 2.0 * grad_var * (predicted - column_mean) / count_all
    )
    enc_again, pred_again = (
        lax.all_gather(enc_low, "dp", axis=1, tiled=True),
        lax.all_gather(pred_low, "dp", axis=1, tiled=True),
    )
    mats = unflat(enc_again[0], enc_shapes(ways))
    mats.update(unflat(pred_again[0], pred_shapes(ways)))
    grads = {}
    grad_low = grad_pred.astype(jnp.bfloat16)
    grads["w_pproj"] = matmul_tn(pred_rows, grad_low)
    grads["b_pproj"] = jnp.sum(grad_pred, axis=0)
    grad_normed = tensor_back(matmul_nt(grad_low, mats["w_pproj"]))
    grad_mid, grads["plnf_g"], grads["plnf_b"] = norm_backward(
        pred_mid, vectors["plnf_g"], vectors["plnf_b"], grad_normed
    )
    grad_in, layer_grads = layer_backward(
        grad_mid, pred_kept, mats, vectors, "p", PHEADS, PHEAD_DIM, same_sample, ways
    )
    grads.update(layer_grads)
    grads["mask_tok"] = jnp.sum(jnp.where(context_mask[:, None], 0.0, grad_in), axis=0)
    grad_pin = lax.dynamic_slice_in_dim(
        jnp.where(context_mask[:, None], grad_in, 0.0), member * (PD // ways), PD // ways, 1
    )
    grad_pin_low = grad_pin.astype(jnp.bfloat16)
    grads["w_pin"] = matmul_tn(encoded_low, grad_pin_low)
    grads["b_pin"] = jnp.sum(grad_pin, axis=0)
    grad_encoded = tensor_back(matmul_nt(grad_pin_low, mats["w_pin"]))
    grad_mid, grads["lnf_g"], grads["lnf_b"] = norm_backward(
        online_mid, vectors["lnf_g"], vectors["lnf_b"], grad_encoded
    )
    grad_in, layer_grads = layer_backward(
        grad_mid, online_kept, mats, vectors, "", HEADS, HEAD_DIM, online_allowed, ways
    )
    grads.update(layer_grads)
    grads["w_patch"] = matmul_tn(patches, grad_in.astype(jnp.bfloat16))
    grads["b_patch"] = jnp.sum(grad_in, axis=0)
    enc_grad = jnp.concatenate([grads[label].reshape(-1) for label, _, _ in enc_shapes(ways)])[
        None, :
    ]
    pred_grad = jnp.concatenate([grads[label].reshape(-1) for label, _, _ in pred_shapes(ways)])[
        None, :
    ]
    enc_share, pred_share = (
        lax.psum_scatter(enc_grad, "dp", scatter_dimension=1, tiled=True),
        lax.psum_scatter(pred_grad, "dp", scatter_dimension=1, tiled=True),
    )
    gain_weight = 0.5
    halves = []
    for label, length in enc_vectors() + pred_vectors():
        if label in LOCAL_BIAS:
            halves.append(place_columns(grads[label], length, LOCAL_BIAS[label], ways, member))
        elif label in ROW_GAINS:
            halves.append(gain_weight * grads[label])
        else:
            halves.append(0.5 * grads[label])
    vector_part = jnp.concatenate(halves)
    square_sum = jnp.sum(enc_share * enc_share) + jnp.sum(pred_share * pred_share)
    square_total, vector_grad, loss_value = lax.psum(
        (square_sum, vector_part, local_loss), ("dp", "tensor")
    )
    grad_norm = jnp.sqrt(square_total + jnp.sum(vector_grad * vector_grad))
    factor = jnp.minimum(1.0, CLIP / (grad_norm + 1e-06))
    count = step_count[0].astype(jnp.float32)
    new_enc, enc_first, enc_second = adam(
        enc_params, enc_m1, enc_m2, enc_share * factor, RATE_MAT, DECAY, count
    )
    new_pred, pred_first, pred_second = adam(
        pred_params, pred_m1, pred_m2, pred_share * factor, RATE_MAT, DECAY, count
    )
    new_vec, vec_first, vec_second = adam(
        vecs, vec_m1, vec_m2, vector_grad * factor, RATE_VEC, 0.0, count
    )
    new_target = TAU * target_params + (1 - TAU) * new_enc
    new_target_vec = TAU * target_vecs + (1 - TAU) * new_vec[: target_vecs.shape[0]]
    return (
        new_enc,
        enc_first,
        enc_second,
        new_enc.astype(jnp.bfloat16),
        new_pred,
        pred_first,
        pred_second,
        new_pred.astype(jnp.bfloat16),
        new_target,
        new_vec,
        vec_first,
        vec_second,
        new_target_vec,
        loss_value,
        grad_norm,
    )


def solution(mesh):
    placed = (
        P("tensor", "dp"),
        P("tensor", "dp"),
        P("tensor", "dp"),
        P("tensor", "dp"),
        P("tensor", "dp"),
        P("tensor", "dp"),
        P("tensor", "dp"),
        P(),
        P(),
        P(),
        P(),
        P("dp", "tensor"),
        P("dp"),
        P("dp"),
        P(),
    )
    return jax.shard_map(
        shards,
        mesh=mesh,
        in_specs=placed,
        out_specs=(
            P("tensor", "dp"),
            P("tensor", "dp"),
            P("tensor", "dp"),
            P("tensor", "dp"),
            P("tensor", "dp"),
            P("tensor", "dp"),
            P("tensor", "dp"),
            P("tensor", "dp"),
            P("tensor", "dp"),
            P(),
            P(),
            P(),
            P(),
            P(),
            P(),
        ),
        check_vma=False,
    )
```

profile of v0, /device:TPU:0, one launch (start us, length us, event | category | flops | bytes accessed | tf_op | source)
XLA Modules:
  0.0 2844.7 jit_solution(11390692875327216479)
XLA Ops:
  11.6 304.1 %all-gather.5.cloned.1.call-done = bf16[1,7077888]{1,0:T(2,128)(2,1)} async-done(((bf16[1,442368]{1,0:T(2,128)(2,1)}), bf16[1,7077888]{1,0:T(2,128)(2,1)}) %all-gather.5.cloned.1.call-update) | async-done | bytes 14155792 | tf_op jit(solution)/shard_map/all_gather | solution.py:344
  315.7 27.3 slice_reduce_fusion.7
  345.1 5.7 fusion.245
  356.7 10.0 multiply_sine_fusion
  366.7 18.5 slice_reduce_fusion.9
  386.5 55.6 %slice_reduce_fusion.5 = bf16[1572864]{0:T(1024)(128)(2,1)} fusion(bf16[1,7077888]{1,0:T(2,128)(2,1)} %all-gather.5.cloned.1.call-done), kind=kLoop, calls=%fused_computation.173 | loop fusion | bytes 6291456 | tf_op jit(solution)/shard_map/slice | solution.py:99
  442.1 7.2 reshape.567
  457.6 5.9 fusion.129
  463.5 6.1 copy.164
  483.8 63.4 %while.59 = (s32[]{:T(128)}, bf16[8,1176,64]{1,2,0:T(8,128)(2,1)S(1)}, f32[8,1176]{1,0:T(8,128)}, bf16[8,1176,64]{2,1,0:T(8,128)(2,1)}, bf16[8,1176,64]{2,1,0:T(...) while((s32[]{:T(128)}, ...), condition=%wide.region_7.8_spmd.clone, body=%wide.region_4.7_spmd.clone.sunk | while | flops 367945696 | bytes 18235952 | solution.py:203
  547.7 5.0 fusion.246
  554.7 93.2 %slice_reduce_fusion.3 = (bf16[2097152]{0:T(1024)(128)(2,1)}, bf16[2097152]{0:T(1024)(128)(2,1)}) fusion(bf16[1,7077888]{1,0:T(2,128)(2,1)} %all-gather.5.cloned.1.call-done), kind=kLoop, calls=%fused_computation.156 | loop fusion | bytes 16777216 | tf_op jit(solution)/shard_map/slice | solution.py:99
  647.9 36.8 %all-gather.11.cloned.1.call-done = bf16[1,7077888]{1,0:T(2,128)(2,1)} async-done(((bf16[1,442368]{1,0:T(2,128)(2,1)}), bf16[1,7077888]{1,0:T(2,128)(2,1)}) %all-gather.11.cloned.1.call-update) | async-done | bytes 14155792 | tf_op jit(solution)/shard_map/all_gather | solution.py:346
  684.7 27.3 slice_reduce_fusion.6
  714.0 7.5 reshape.572
  721.5 7.5 reshape.573
  741.6 5.8 convolution_add_fusion.2
  751.2 7.6 fusion.218
  761.2 6.0 multiply_sine_fusion.1
  767.3 35.8 %all-gather.7.cloned.1.call-done = bf16[1,1277952]{1,0:T(2,128)(2,1)} async-done(((bf16[1,79872]{1,0:T(2,128)(2,1)}), bf16[1,1277952]{1,0:T(2,128)(2,1)}) %all-gather.7.cloned.1.call-update) | async-done | bytes 2555920 | tf_op jit(solution)/shard_map/all_gather | solution.py:345
  805.6 8.4 slice_reduce_fusion.12
  815.2 10.3 slice_reduce_fusion.13
  825.9 19.7 slice_reduce_fusion.8
  847.9 55.2 %slice_reduce_fusion.4 = bf16[1572864]{0:T(1024)(128)(2,1)} fusion(bf16[1,7077888]{1,0:T(2,128)(2,1)} %all-gather.11.cloned.1.call-done), kind=kLoop, calls=%fused_computation.172 | loop fusion | bytes 6291456 | tf_op jit(solution)/shard_map/slice | solution.py:99
  903.1 7.0 reshape.584
  922.7 5.7 fusion.130
  928.4 6.1 copy.170
  943.1 39.9 %while.61 = (s32[]{:T(128)}, bf16[8,1176,64]{1,2,0:T(8,128)(2,1)S(1)}, bf16[8,1176,64]{1,2,0:T(8,128)(2,1)}, bf16[8,1176,64]{1,2,0:T(8,128)(2,1)}, bf16[8,1176,6...) while((s32[]{:T(128)}, bf16[8,1176,64]{1,2,0:T(8,128)(2,1)S(1)}, ...), condition=%wide.region_32.33_spmd.clone, body=%wide.region_29.32_spmd.clone.sunk | while | flops 366561536 | bytes 17789300 | solution.py:203
  999.6 5.1 slice_bitcast_fusion
  1004.7 32.0 %while.60 = (s32[]{:T(128)}, bf16[6,1176,32]{1,2,0:T(8,128)(2,1)S(1)}, f32[6,1176]{1,0:T(8,128)S(1)}, bf16[6,1176,32]{2,1,0:T(8,128)(2,1)}, bf16[6,1176,32]{2,1,...) while((s32[]{:T(128)}, ...), condition=%wide.region_19.20_spmd.clone, body=%wide.region_16.19_spmd.clone.sunk | while | flops 189504160 | bytes 18151976 | solution.py:203
  1039.5 14.1 slice_reduce_fusion.10
  1055.2 93.1 %slice_reduce_fusion.1 = (bf16[2097152]{0:T(1024)(128)(2,1)}, bf16[2097152]{0:T(1024)(128)(2,1)}) fusion(bf16[1,7077888]{1,0:T(2,128)(2,1)} %all-gather.11.cloned.1.call-done), kind=kLoop, calls=%fused_computation.154 | loop fusion | bytes 16777216 | tf_op jit(solution)/shard_map/slice | solution.py:99
  1148.3 7.3 reshape.588
  1155.6 7.4 reshape.589
  1176.5 19.4 fusion.183
  1197.6 30.0 %all-reduce.44.cloned.1.call-done = (f32[1176,384]{1,0:T(8,128)}, f32[1176,1024]{1,0:T(8,128)}) async-done(((f32[1176,384]{1,0:T(8,128)}, f32[1176,1024]{1,0:T(8,128)}), (f32[1176,384]{1,0:T(8,128)}, f32[1176,1024]{1,0:T(8,128)})) %all-reduce.44.cloned.1.call-update) | async-done | bytes 6623248 | tf_op jit(solution)/shard_map/psum | solution.py:161
  1241.0 43.1 %all-reduce.3 = (f32[]{:T(128)}, f32[512]{0:T(512)S(1)}, f32[512]{0:T(512)S(1)}) all-reduce(f32[]{:T(128)} %fusion.206, f32[512]{0:T(512)S(1)} %get-tuple-element.469, f32[512]{0:T(512)S(1)} %get-tuple-element.468), channel_id=1, replica_groups=mesh['dp'=16,'tensor'=2] {'dp'}, use_global_device_ids=true, to_apply=%region_42.43 | all-reduce | flops 1025 | bytes 8200 | tf_op jit(solution)/shard_map/psum | solution.py:396
  1292.6 15.4 all-reduce.26.cloned.1.call-done
  1328.6 12.7 all-reduce.28.cloned.1.call-done
  1352.3 76.9 %while.62 = (s32[]{:T(128)}, bf16[6,3,1176,32]{2,3,0,1:T(8,128)(2,1)}, bf16[6,1176,32]{2,1,0:T(8,128)(2,1)}, bf16[6,1176,32]{2,1,0:T(8,128)(2,1)}, f32[6,1176]{1...) while((s32[]{:T(128)}, ...), condition=%wide.region_55.56_spmd.clone, body=%wide.region_53.55_spmd.clone.sunk | while | flops 457208800 | bytes 44828792 | solution.py:295
  1475.5 16.4 all-reduce.32.cloned.1.call-done
  1491.9 5.5 fusion.140
  1501.6 16.8 convert_reduce_fusion
  1518.4 8.9 convolution_convert_fusion.1
  1528.7 21.7 all-reduce.34.cloned.1.call-done
  1550.4 5.3 convert_reduce_fusion.3
  1555.7 5.6 fusion.141
  1561.4 5.0 add_reduce_fusion
  1572.6 106.3 %while.63 = (s32[]{:T(128)}, bf16[8,3,1176,64]{2,3,1,0:T(8,128)(2,1)}, bf16[8,1176,64]{2,1,0:T(8,128)(2,1)}, bf16[8,1176,64]{2,1,0:T(8,128)(2,1)}, f32[8,1176]{1...) while((s32[]{:T(128)}, ...), condition=%wide.region_67.68_spmd.clone, body=%wide.region_65.67_spmd.clone.sunk | while | flops 901972032 | bytes 45742976 | solution.py:295
  1683.3 6.2 convolution_convert_fusion
  1690.7 10.6 convolution_bitcast_fusion
  1701.3 11.4 convolution_bitcast_fusion.1
  1712.8 5.3 copy.265
  1718.1 9.6 copy.264
  1729.9 8.1 fusion.217
  1739.7 7.0 reshape.593
  1746.8 4.9 fusion.142
  1770.6 6.1 constant_dynamic-update-slice_fusion.3
  1798.8 108.5 %all-reduce.42.cloned.1.call-done = f32[1,1277952]{1,0:T(1,128)} async-done(((f32[1,1277952]{1,0:T(1,128)}), f32[1,1277952]{1,0:T(1,128)}) %all-reduce.42.cloned.1.call-update) | async-done | bytes 5111824
  1915.3 726.4 %all-reduce.40.cloned.1.call-done = f32[1,7077888]{1,0:T(1,128)} async-done(((f32[1,7077888]{1,0:T(1,128)}), f32[1,7077888]{1,0:T(1,128)}) %all-reduce.40.cloned.1.call-update) | async-done | bytes 28311568
  2641.7 5.4 multiply_reduce_fusion.14
  2648.4 119.0 %all-reduce.38.cloned.1.call-done = f32[23936]{0:T(1024)} async-done(((f32[23936]{0:T(1024)}), f32[23936]{0:T(1024)}) %all-reduce.38.cloned.1.call-update) | async-done | bytes 95760 | tf_op jit(solution)/shard_map/psum | solution.py:471
  2768.9 41.0 %all-reduce.2 = (f32[]{:T(128)}, f32[]{:T(128)}) all-reduce(f32[]{:T(128)S(6)} %add.642, f32[]{:T(128)S(6)} %add.662), channel_id=1, replica_groups=mesh['dp'=16,'tensor'=2] {'dp','tensor'}, use_global_device_ids=true, to_apply=%region_75.76 | all-reduce | flops 2 | bytes 16 | tf_op jit(solution)/shard_map/psum | solution.py:471
  2813.7 16.2 multiply_add_fusion.1
  (847 shorter events, 615.0 us)
Async XLA Ops:
  7.2 337.9 %copy-start = (bf16[1176,768]{1,0:T(8,128)(2,1)S(1)}, bf16[1176,768]{1,0:T(8,128)(2,1)}, u32[]{:S(2)}) copy-start(bf16[1176,768]{1,0:T(8,128)(2,1)} %param.36) | copy-start | bytes 5419012
  7.2 308.6 %all-gather.5.cloned.1.call-start = ((), (), s32[]{:S(2)}) async-start(), calls=%async_computation | async-start | bytes 30081024 | tf_op jit(solution)/shard_map/all_gather | solution.py:344
  11.6 437.8 %all-reduce.22.cloned.1.call-start = ((), (), s32[]{:S(2)}) async-start(), calls=%async_computation.1 | async-start | bytes 9633792 | tf_op jit(solution)/shard_map/psum | solution.py:157
  350.8 333.9 %all-gather.11.cloned.1.call-start = ((), (), s32[]{:S(2)}) async-start(), calls=%async_computation.5 | async-start | bytes 30081024 | tf_op jit(solution)/shard_map/all_gather | solution.py:346
  355.1 378.2 %all-reduce.24.cloned.1.call-start = ((), (), s32[]{:S(2)}) async-start(), calls=%async_computation.2 | async-start | bytes 9633792 | tf_op jit(solution)/shard_map/psum | solution.py:161
  356.6 97.9 %copy-start.117 = (f32[1024]{0:T(1024)}, f32[1024]{0:T(1024)S(1)}, u32[]{:S(2)}) copy-start(f32[1024]{0:T(1024)S(1)} %get-tuple-element.650) | copy-start | bytes 12292
  356.6 97.9 %copy-start.148 = (f32[1024]{0:T(1024)}, f32[1024]{0:T(1024)S(1)}, u32[]{:S(2)}) copy-start(f32[1024]{0:T(1024)S(1)} %get-tuple-element.649) | copy-start | bytes 12292
  356.7 381.7 %copy-start.112 = (f32[1024]{0:T(1024)}, f32[1024]{0:T(1024)S(1)}, u32[]{:S(2)}) copy-start(f32[1024]{0:T(1024)S(1)} %get-tuple-element.647) | copy-start | bytes 12292
  356.7 381.7 %copy-start.150 = (f32[1024]{0:T(1024)}, f32[1024]{0:T(1024)S(1)}, u32[]{:S(2)}) copy-start(f32[1024]{0:T(1024)S(1)} %get-tuple-element.646) | copy-start | bytes 12292
  454.6 8.9 copy-start.96
  454.6 8.9 copy-start.106
  552.7 250.4 %all-gather.7.cloned.1.call-start = ((), (), s32[]{:S(2)}) async-start(), calls=%async_computation.3 | async-start | bytes 5431296 | tf_op jit(solution)/shard_map/all_gather | solution.py:345
  554.6 355.4 %all-reduce.48.cloned.1.call-start = ((), (), s32[]{:S(2)}) async-start(), calls=%async_computation.17 | async-start | bytes 19267584 | tf_op jit(solution)/shard_map/psum | solution.py:161
  737.7 9.7 copy-start.1
  737.7 9.7 copy-start.83
  738.4 9.1 copy-start.98
  738.4 9.1 copy-start.108
  741.6 9.5 copy-start.45
  758.8 229.0 %all-gather.9.cloned.1.call-start = ((), (), s32[]{:S(2)}) async-start(), calls=%async_computation.4 | async-start | bytes 2949120 | tf_op jit(solution)/shard_map/all_gather | solution.py:384
  760.5 233.5 %copy-start.121 = (f32[384]{0:T(512)}, f32[384]{0:T(512)S(1)}, u32[]{:S(2)}) copy-start(f32[384]{0:T(512)S(1)} %get-tuple-element.640) | copy-start | bytes 4612
  760.5 233.5 %copy-start.155 = (f32[384]{0:T(512)}, f32[384]{0:T(512)S(1)}, u32[]{:S(2)}) copy-start(f32[384]{0:T(512)S(1)} %get-tuple-element.639) | copy-start | bytes 4612
  825.9 113.7 %copy-start.40 = (bf16[1024,192]{1,0:T(8,128)(2,1)}, bf16[1024,192]{1,0:T(8,128)(2,1)S(1)}, u32[]{:S(2)}) copy-start(bf16[1024,192]{1,0:T(8,128)(2,1)S(1)} %reshape.574) | copy-start | bytes 1179652
  914.7 24.1 copy-start.85
  919.8 19.0 copy-start.89
  928.4 10.4 slice-start
  942.9 220.1 %all-reduce.46.cloned.1.call-start = ((), (), s32[]{:S(2)}) async-start(), calls=%async_computation.16 | async-start | bytes 13246464 | tf_op jit(solution)/shard_map/psum | solution.py:161
  1004.7 32.1 %copy-start.62 = (bf16[192,384]{1,0:T(8,128)(2,1)S(1)}, bf16[192,384]{1,0:T(8,128)(2,1)}, u32[]{:S(2)}) copy-start(bf16[192,384]{1,0:T(8,128)(2,1)} %reshape.579) | copy-start | bytes 442372
  1038.5 189.0 %all-reduce.44.cloned.1.call-start = ((), (), s32[]{:S(2)}) async-start(), calls=%async_computation.15 | async-start | bytes 13246464 | tf_op jit(solution)/shard_map/psum | solution.py:161
  1055.2 115.2 %copy-start.69 = (bf16[384,768]{1,0:T(8,128)(2,1)}, bf16[384,768]{1,0:T(8,128)(2,1)S(1)}, u32[]{:S(2)}) copy-start(bf16[384,768]{1,0:T(8,128)(2,1)S(1)} %reshape.580) | copy-start | bytes 1769476
  1196.0 31.5 %copy-start.130 = (f32[1024]{0:T(1024)S(1)}, f32[1024]{0:T(1024)}, u32[]{:S(2)}) copy-start(f32[1024]{0:T(1024)} %get-tuple-element.654) | copy-start | bytes 12292
  1196.0 111.9 %all-reduce.26.cloned.1.call-start = ((), (), s32[]{:S(2)}) async-start(), calls=%async_computation.6 | async-start | bytes 1806336 | tf_op jit(solution)/shard_map/psum | solution.py:165
  1292.5 48.8 %all-reduce.28.cloned.1.call-start = ((), (), s32[]{:S(2)}) async-start(), calls=%async_computation.7 | async-start | bytes 1806336 | tf_op jit(solution)/shard_map/psum | solution.py:272
  1320.5 133.1 %all-reduce.30.cloned.1.call-start = ((), (), s32[]{:S(2)}) async-start(), calls=%async_computation.8 | async-start | bytes 1806336 | tf_op jit(solution)/shard_map/psum | solution.py:165
  1432.8 59.0 %all-reduce.32.cloned.1.call-start = ((), (), s32[]{:S(2)}) async-start(), calls=%async_computation.9 | async-start | bytes 4816896 | tf_op jit(solution)/shard_map/psum | solution.py:165
  1447.7 9.1 copy-start.103
  1447.7 11.8 copy-start.116
  1468.8 23.1 copy-start.86
  1468.8 23.1 copy-start.90
  1468.8 23.1 copy-start.111
  1468.8 81.6 %all-reduce.34.cloned.1.call-start = ((), (), s32[]{:S(2)}) async-start(), calls=%async_computation.10 | async-start | bytes 4816896 | tf_op jit(solution)/shard_map/psum | solution.py:272
  1475.5 21.9 copy-start.101
  1501.6 16.8 copy-start.21
  1501.6 16.8 copy-start.44
  1527.3 23.1 copy-start.84
  1527.3 23.1 copy-start.113
  1527.4 219.4 %all-reduce.36.cloned.1.call-start = ((), (), s32[]{:S(2)}) async-start(), calls=%async_computation.11 | async-start | bytes 4816896 | tf_op jit(solution)/shard_map/psum | solution.py:165
  1528.7 27.0 copy-start.99
  1528.7 27.0 copy-start.109
  1689.5 217.7 %all-reduce.42.cloned.1.call-start = ((), (), s32[]{:S(2)}) async-start(), calls=%async_computation.14 | async-start | bytes 10223616
  1690.6 10.7 copy-start.151
  1690.6 951.1 %all-reduce.40.cloned.1.call-start = ((), (), s32[]{:S(2)}) async-start(), calls=%async_computation.13 | async-start | bytes 56623104
  1712.8 14.9 slice-start.8
  1712.8 16.5 slice-start.2
  1718.1 9.6 slice-start.9
  1718.1 9.6 copy-start.37
  1718.1 11.2 slice-start.3
  1746.7 11.4 slice-start.10
  1768.7 9.5 slice-start.6
  1787.9 979.5 %all-reduce.38.cloned.1.call-start = ((), (), s32[]{:S(2)}) async-start(), calls=%async_computation.12 | async-start | bytes 196608 | tf_op jit(solution)/shard_map/psum | solution.py:471
  1909.6 901.8 %copy-start.75 = (f32[23936]{0:T(1024)S(1)}, f32[23936]{0:T(1024)}, u32[]{:S(2)}) copy-start(f32[23936]{0:T(1024)} %param.32) | copy-start | bytes 287236
  1909.6 901.8 %copy-start.92 = (f32[23936]{0:T(1024)S(1)}, f32[23936]{0:T(1024)}, u32[]{:S(2)}) copy-start(f32[23936]{0:T(1024)} %param.34) | copy-start | bytes 287236
  1909.6 901.8 %copy-start.93 = (f32[23936]{0:T(1024)S(1)}, f32[23936]{0:T(1024)}, u32[]{:S(2)}) copy-start(f32[23936]{0:T(1024)} %param.33) | copy-start | bytes 287236
  1909.6 903.4 %copy-start.80 = (f32[16384]{0:T(1024)S(1)}, f32[16384]{0:T(1024)}, u32[]{:S(2)}) copy-start(f32[16384]{0:T(1024)} %param.35) | copy-start | bytes 196612
  2813.0 16.8 copy-start.78
  (135 other events, 536.3 us)
Sparse Core Ops, SparseCore 0:
  11.7 303.9 all-gather.4
  350.9 27.4 all-reduce.21
  382.2 302.4 all-gather.10
  687.2 27.4 all-reduce.23
  718.0 85.0 all-gather.6
  805.5 39.7 all-reduce.47
  943.0 9.0 all-gather.8
  1038.6 31.3 all-reduce.45
  1196.1 31.3 all-reduce.43
  1292.7 15.2 all-reduce.25
  1320.7 20.5 all-reduce.27
  1433.0 20.5 all-reduce.29
  1468.9 22.9 all-reduce.31
  1527.5 22.8 all-reduce.33
  1689.7 22.8 all-reduce.35
  1718.3 188.8 all-reduce.41
  1913.5 728.1 all-reduce.39
  2647.7 119.6 all-reduce.37
where the time goes:
time: 2860 us; the launch traced here: 2840 us
  waiting for transfers between devices  1430 us (50%)
  local copies, waits for them, and re-layouts  653 us (23%)
  matrix products  431 us (15%)
  other arithmetic  218 us (8%)
  blocking collectives  84.2 us (3%)
    unnamed x20, waiting for transfers between devices  835 us
    slice x12, local copies, waits for them, and re-layouts, unflat(): flat_row[offset:offset + height * breadth].reshape(height, breadth)  424 us
    all_gather x1, waiting for transfers between devices, shards(): lax.all_gather(enc_low, 'dp', axis=1, tiled=True)  304 us
    dot_general x60, matrix products, matmul_nt(): lax.dot_general(left, right, (((1,), (1,)), ((), ())), preferred_element_...  180 us
    dot_general x51, matrix products, matmul(): return jnp.dot(left, right, preferred_element_type=jnp.float32)  148 us
    psum x1, waiting for transfers between devices, shards(): lax.psum((square_sum, vector_part, local_loss), ('dp', 'tensor'))  119 us
    dot_general x39, matrix products, matmul_tn(): lax.dot_general(left, right, (((0,), (0,)), ((), ())), preferred_element_...  102 us
    unnamed x377, local copies, waits for them, and re-layouts  86.7 us
  transfers between devices with their start and end apart: 18, of which 12 were waited for; matrix products, arithmetic and copies ran while one was open for 28% of the time, Pallas kernels for 0%

commit v1 on v0

v1 whole, which is shorter than its diff:
```python
import functools
import math

import jax
import jax.numpy as jnp
from jax import lax
from jax.experimental import pallas as pl
from jax.experimental.pallas import tpu as pltpu
from jax.sharding import PartitionSpec as P

D = 1024
HEADS = 16
HEAD_DIM = 64
MLP = 4096
PATCH = 1536
PD = 384
PHEADS = 12
PHEAD_DIM = 32
PMLP = 1536


BETA_ONE = 0.9
BETA_TWO = 0.999
ADAM_EPS = 1e-08
RATE_MAT = 0.01
RATE_VEC = 0.05
DECAY = 0.05
CLIP = 0.0002
TAU = 0.75
NORM_EPS = 1e-06
VAR_EPS = 0.0001
LOCAL_BIAS = {
    "b_qkv": True,
    "b_pqkv": True,
    "b_up": False,
    "b_pup": False,
    "b_pin": False,
    "b_pproj": False,
}
ROW_GAINS = ("ln2_g", "ln2_b", "pln2_g", "pln2_b")


def enc_shapes(ways):
    return [
        ("w_patch", PATCH // ways, D),
        ("w_qkv", D, 3 * D // ways),
        ("w_out", D // ways, D),
        ("w_up", D, MLP // ways),
        ("w_down", MLP // ways, D),
    ]


def pred_shapes(ways):
    return [
        ("w_pin", D, PD // ways),
        ("w_pqkv", PD, 3 * PD // ways),
        ("w_pout", PD // ways, PD),
        ("w_pup", PD, PMLP // ways),
        ("w_pdown", PMLP // ways, PD),
        ("w_pproj", PD, D // ways),
    ]


def enc_vectors():
    return [
        ("b_patch", D),
        ("ln1_g", D),
        ("ln1_b", D),
        ("b_qkv", 3 * D),
        ("b_out", D),
        ("ln2_g", D),
        ("ln2_b", D),
        ("b_up", MLP),
        ("b_down", D),
        ("lnf_g", D),
        ("lnf_b", D),
    ]


def pred_vectors():
    return [
        ("b_pin", PD),
        ("mask_tok", PD),
        ("pln1_g", PD),
        ("pln1_b", PD),
        ("b_pqkv", 3 * PD),
        ("b_pout", PD),
        ("pln2_g", PD),
        ("pln2_b", PD),
        ("b_pup", PMLP),
        ("b_pdown", PD),
        ("plnf_g", PD),
        ("plnf_b", PD),
        ("b_pproj", D),
    ]


def unflat(flat_row, shapes):
    result = {}
    offset = 0
    for label, height, breadth in shapes:
        result[label] = flat_row[offset : offset + height * breadth].reshape(height, breadth)
        offset += height * breadth
    return result


def split_vector(vector, sections):
    result = {}
    offset = 0
    for label, length in sections:
        result[label] = vector[offset : offset + length]
        offset += length
    return result


def positions(segment_row):
    earlier = jnp.sum((segment_row[None, :] < segment_row[:, None]).astype(jnp.int32), axis=1)
    return (jnp.arange(segment_row.shape[0], dtype=jnp.int32) - earlier).astype(jnp.float32)


def sincos(places, width):
    half_width = width // 2
    freqs = jnp.exp(-math.log(10000.0) * jnp.arange(half_width).astype(jnp.float32) / half_width)
    angles = places[:, None] * freqs[None, :]
    return jnp.concatenate([jnp.sin(angles), jnp.cos(angles)], axis=1)


def layer_norm(values, gain, shift):
    centered = values - jnp.mean(values, axis=-1, keepdims=True)
    spread = jnp.mean(centered * centered, axis=-1, keepdims=True)
    return centered * lax.rsqrt(spread + NORM_EPS) * gain + shift


def plain_norm(values):
    centered = values - jnp.mean(values, axis=-1, keepdims=True)
    return centered * lax.rsqrt(jnp.mean(centered * centered, axis=-1, keepdims=True) + NORM_EPS)


def norm_backward(values, gain, shift, cotangent):
    return jax.vjp(layer_norm, values, gain, shift)[1](cotangent)


def matmul(left, right):
    return jnp.dot(left, right, preferred_element_type=jnp.float32)


def matmul_tn(left, right):
    return lax.dot_general(
        left, right, (((0,), (0,)), ((), ())), preferred_element_type=jnp.float32
    )


def matmul_nt(left, right):
    return lax.dot_general(
        left, right, (((1,), (1,)), ((), ())), preferred_element_type=jnp.float32
    )


def local_columns(vector, thirds, ways, member):
    if thirds:
        width = vector.shape[0] // 3
        slab = vector.reshape(3, width)
        return lax.dynamic_slice_in_dim(slab, member * (width // ways), width // ways, 1).reshape(
            -1
        )
    return lax.dynamic_slice_in_dim(
        vector, member * (vector.shape[0] // ways), vector.shape[0] // ways, 0
    )


def place_columns(local, length, thirds, ways, member):
    if thirds:
        slab = jnp.zeros((3, length // 3), jnp.float32)
        placed = lax.dynamic_update_slice_in_dim(
            slab, local.reshape(3, -1), member * (length // 3 // ways), 1
        )
        return placed.reshape(-1)
    return lax.dynamic_update_slice_in_dim(
        jnp.zeros((length,), jnp.float32), local, member * (length // ways), 0
    )


QB = 256
LOG2E = math.log2(math.e)

def roundup(n, m):
    return -(-n // m) * m

def dot_nn(a, b):
    return lax.dot_general(a, b, (((1,), (0,)), ((), ())), preferred_element_type=jnp.float32)

def dot_nt(a, b):
    return lax.dot_general(a, b, (((1,), (1,)), ((), ())), preferred_element_type=jnp.float32)

def pad_rows(x, n):
    return jnp.concatenate([x.astype(jnp.float32), jnp.zeros((n - x.shape[0], x.shape[1]), jnp.float32)], 0).astype(x.dtype)

def lane_keep(x, lo, hi):
    lane = lax.broadcasted_iota(jnp.int32, (1, x.shape[1]), 1)
    keep = jnp.where((lane >= lo) & (lane < hi), 1.0, 0.0).astype(x.dtype)
    return x * keep

def attn_fwd_kernel(heads, e, T, TP, W, packed_ref, qa_ref, ka_ref, o_ref, lse_ref, q_s, k_s, v_s, o_s):
    g = pl.program_id(0)
    base = pl.multiple_of(g * 128, 128)
    q_s[...] = pad_rows(packed_ref[:, pl.ds(base, 128)], TP)
    k_s[:, :128] = pad_rows(packed_ref[:, pl.ds(base + W, 128)], TP)
    k_s[:, 128:] = ka_ref[...]
    v_s[...] = pad_rows(packed_ref[:, pl.ds(base + 2 * W, 128)], TP)
    scale = e ** -0.5 * LOG2E
    lane = lax.broadcasted_iota(jnp.int32, (QB, 128), 1)

    def block(i, _):
        rows = pl.ds(pl.multiple_of(i * QB, QB), QB)
        q = q_s[rows, :]
        qa = qa_ref[rows, :]
        out = jnp.zeros((QB, 128), jnp.float32)
        stats = jnp.zeros((QB, 128), jnp.float32)
        for h in range(heads):
            qq = jnp.concatenate([lane_keep(q, h * e, (h + 1) * e), qa], 1)
            s = dot_nt(qq, k_s[...]) * scale
            peak = jnp.max(s, axis=1, keepdims=True)
            p = jnp.exp2(s - peak)
            total = jnp.sum(p, axis=1, keepdims=True)
            p = (p * (1.0 / total)).astype(jnp.bfloat16)
            o = dot_nn(p, v_s[...])
            mine = (lane >= h * e) & (lane < (h + 1) * e)
            out = jnp.where(mine, o, out)
            stats = jnp.where(lane == h, peak + jnp.log2(total), stats)
        o_s[rows, :] = out.astype(jnp.bfloat16)
        lse_ref[0, :, rows] = stats.T[:8, :]
        return 0

    lax.fori_loop(0, TP // QB, block, 0)
    o_ref[...] = o_s[:T, :]

def attn_fwd(packed, qa, ka, heads, e):
    T, W3 = packed.shape
    W = W3 // 3
    TP = roundup(T, QB)
    groups = W // 128
    return pl.pallas_call(
        functools.partial(attn_fwd_kernel, heads, e, T, TP, W),
        grid=(groups,),
        in_specs=[pl.BlockSpec((T, W3), lambda g: (0, 0)), pl.BlockSpec((TP, 128), lambda g: (0, 0)), pl.BlockSpec((TP, 128), lambda g: (0, 0))],
        out_specs=[pl.BlockSpec((T, 128), lambda g: (0, g)), pl.BlockSpec((1, 8, TP), lambda g: (g, 0, 0))],
        out_shape=[jax.ShapeDtypeStruct((T, W), jnp.bfloat16), jax.ShapeDtypeStruct((groups, 8, TP), jnp.float32)],
        scratch_shapes=[pltpu.VMEM((TP, 128), jnp.bfloat16), pltpu.VMEM((TP, 256), jnp.bfloat16), pltpu.VMEM((TP, 128), jnp.bfloat16), pltpu.VMEM((TP, 128), jnp.bfloat16)],
        compiler_params=pltpu.CompilerParams(vmem_limit_bytes=48 << 20),
        cost_estimate=pl.CostEstimate(flops=groups * heads * 4 * T * T * 256, bytes_accessed=T * W3 * 3, transcendentals=groups * heads * T * T),
        name="attn_fwd",
    )(packed, qa, ka)

def attn_bwd_kernel(heads, e, T, TP, W, packed_ref, do_ref, qa_ref, ka_ref, lse_ref, d_ref, q_s, k_s, v_s, do_s, dk_s, dv_s, dq_s):
    g = pl.program_id(0)
    base = pl.multiple_of(g * 128, 128)
    q_s[:, :128] = pad_rows(packed_ref[:, pl.ds(base, 128)], TP)
    q_s[:, 128:] = qa_ref[...]
    k = pad_rows(packed_ref[:, pl.ds(base + W, 128)], TP)
    k_s[...] = k
    v_s[...] = pad_rows(packed_ref[:, pl.ds(base + 2 * W, 128)], TP)
    do_s[...] = pad_rows(do_ref[...], TP)
    dk_s[...] = jnp.zeros_like(dk_s)
    dv_s[...] = jnp.zeros_like(dv_s)
    kt = k.astype(jnp.float32).T.astype(jnp.bfloat16)
    sub = lax.broadcasted_iota(jnp.int32, (128, 1), 0)
    lane = lax.broadcasted_iota(jnp.int32, (TP, 128), 1)
    scale2 = e ** -0.5 * LOG2E
    scale = e ** -0.5
    for h in range(heads):
        lo, hi = h * e, (h + 1) * e
        kk = jnp.concatenate([lane_keep(k_s[...], lo, hi), ka_ref[...]], 1)
        vh = lane_keep(v_s[...], lo, hi)
        kth = kt * jnp.where((sub >= lo) & (sub < hi), 1.0, 0.0).astype(jnp.bfloat16)

        def block(i, carry):
            rows = pl.ds(pl.multiple_of(i * QB, QB), QB)
            qb = q_s[rows, :]
            dob = do_s[rows, :]
            st = dot_nt(kk, qb) * scale2
            pt = jnp.exp2(st - lse_ref[0, h : h + 1, rows])
            dpt = dot_nt(vh, dob)
            d = jnp.sum(pt * dpt, axis=0, keepdims=True)
            dst = (pt * (dpt - d)).astype(jnp.bfloat16)
            dv = dot_nn(pt.astype(jnp.bfloat16), dob)
            dk = dot_nn(dst, qb[:, :128])
            dqt = dot_nn(kth, dst)
            mine = (lane >= lo) & (lane < hi)
            dv_s[...] += jnp.where(mine, dv, 0.0)
            dk_s[...] += jnp.where(mine, dk, 0.0)
            if h == 0:
                dq_s[:, rows] = dqt
            else:
                dq_s[:, rows] += dqt
            return 0

        lax.fori_loop(0, TP // QB, block, 0)
    dq = dq_s[...].T * scale
    d_ref[:, pl.ds(base, 128)] = dq.astype(jnp.bfloat16)[:T]
    d_ref[:, pl.ds(base + W, 128)] = (dk_s[...] * scale).astype(jnp.bfloat16)[:T]
    d_ref[:, pl.ds(base + 2 * W, 128)] = dv_s[...].astype(jnp.bfloat16)[:T]

def attn_bwd(packed, do, qa, ka, lse, heads, e):
    T, W3 = packed.shape
    W = W3 // 3
    TP = roundup(T, QB)
    groups = W // 128
    full = lambda g: (0, 0)
    return pl.pallas_call(
        functools.partial(attn_bwd_kernel, heads, e, T, TP, W),
        grid=(groups,),
        in_specs=[pl.BlockSpec((T, W3), full), pl.BlockSpec((T, 128), lambda g: (0, g)), pl.BlockSpec((TP, 128), full), pl.BlockSpec((TP, 128), full), pl.BlockSpec((1, 8, TP), lambda g: (g, 0, 0))],
        out_specs=pl.BlockSpec((T, W3), full),
        out_shape=jax.ShapeDtypeStruct((T, W3), jnp.bfloat16),
        scratch_shapes=[pltpu.VMEM((TP, 256), jnp.bfloat16), pltpu.VMEM((TP, 128), jnp.bfloat16), pltpu.VMEM((TP, 128), jnp.bfloat16), pltpu.VMEM((TP, 128), jnp.bfloat16), pltpu.VMEM((TP, 128), jnp.float32), pltpu.VMEM((TP, 128), jnp.float32), pltpu.VMEM((128, TP), jnp.float32)],
        compiler_params=pltpu.CompilerParams(vmem_limit_bytes=48 << 20),
        cost_estimate=pl.CostEstimate(flops=groups * heads * 10 * T * T * 256, bytes_accessed=T * W3 * 5, transcendentals=groups * heads * T * T),
        name="attn_bwd",
    )(packed, do, qa, ka, lse)

def mask_sides(segment, context_row, TP):
    T = segment.shape[0]
    s = jnp.arange(128)[None, :]
    one = (segment[:, None] == s)
    qa = jnp.where(one, -1e30, 0.0).astype(jnp.bfloat16)
    ka = jnp.where((s < 8) & ~(one & (context_row[:, None] > 0)), 1.0, 0.0).astype(jnp.bfloat16)
    qa = jnp.concatenate([qa, jnp.zeros((TP - T, 128), jnp.bfloat16)], 0)
    ka = jnp.concatenate([ka, jnp.broadcast_to(jnp.where(s < 8, 1.0, 0.0).astype(jnp.bfloat16), (TP - T, 128))], 0)
    return qa, ka


CHUNK = 16384
UNIT = 3 * CHUNK
SWAP = ((0, 1), (1, 0))


def swap(x):
    return lax.ppermute(x, "tensor", SWAP)


def tensor_total(part):
    return part + swap(part)


def tensor_back(part):
    low = part.astype(jnp.bfloat16)
    return low.astype(jnp.float32) + swap(low).astype(jnp.float32)


def doubling(x, axis):
    size = lax.axis_size(axis)
    if size & (size - 1):
        return lax.psum(x, axis)
    bit = 1
    while bit < size:
        x = x + lax.ppermute(x, axis, [(i, i ^ bit) for i in range(size)])
        bit *= 2
    return x


def tile_width(label):
    return {"w_qkv": 12, "w_up": 16}.get(label, 8)


def enc_chunks(ways):
    spans = []
    start = 0
    for label, height, breadth in enc_shapes(ways):
        count = height * breadth // CHUNK
        spans.append((start, start + count, breadth // 128))
        start += count
    return spans


def regions(unit, spans, emit):
    first = unit * 3
    wide = [s for s in spans if s[2] == 12]
    flat = [s for s in spans if s[2] != 12]
    in_wide = functools.reduce(jnp.logical_or, [(first >= a) & (first < b) for a, b, _ in wide])

    @pl.when(in_wide)
    def _():
        emit(0, 0, 12, 4)

    @pl.when(jnp.logical_not(in_wide))
    def _():
        for c in range(3):
            for width in (8, 16):
                hit = functools.reduce(
                    jnp.logical_or,
                    [(first + c >= a) & (first + c < b) for a, b, w in flat if w == width],
                )

                @pl.when(hit)
                def _():
                    emit(c * 128, c * 16, width, 16 // width)


def pack_kernel(spans, units, place_ref, x_ref, o_ref):
    def emit(row, tile, width, groups):
        for t in range(groups):
            for j in range(width):
                o_ref[tile + t * width + j] = x_ref[
                    pl.ds(row + t * 8 * width + j, 8, stride=width), :
                ].astype(jnp.bfloat16)

    regions(place_ref[0] * units + pl.program_id(0), spans, emit)


def pack_tiles(flat, place, spans):
    units = flat.shape[0] // 384
    return pl.pallas_call(
        functools.partial(pack_kernel, spans, units),
        grid_spec=pltpu.PrefetchScalarGridSpec(
            num_scalar_prefetch=1,
            grid=(units,),
            in_specs=[pl.BlockSpec((384, 128), lambda i, s: (i, 0))],
            out_specs=pl.BlockSpec((48, 8, 128), lambda i, s: (i, 0, 0)),
        ),
        out_shape=jax.ShapeDtypeStruct((units * 48, 8, 128), jnp.bfloat16),
        name="pack_tiles",
    )(place, flat)


def unpack_kernel(spans, units, place_ref, x_ref, o_ref, sq_ref):
    def emit(row, tile, width, groups):
        for t in range(groups):
            for j in range(width):
                o_ref[pl.ds(row + t * 8 * width + j, 8, stride=width), :] = x_ref[
                    tile + t * width + j
                ].astype(jnp.float32)

    regions(place_ref[0] * units + pl.program_id(0), spans, emit)

    @pl.when(pl.program_id(0) == 0)
    def _():
        sq_ref[...] = jnp.zeros_like(sq_ref)

    values = o_ref[...]
    sq_ref[...] += jnp.sum((values * values).reshape(48, 8, 128), axis=0)


def unpack_tiles(tiles, place, spans):
    units = tiles.shape[0] // 48
    return pl.pallas_call(
        functools.partial(unpack_kernel, spans, units),
        grid_spec=pltpu.PrefetchScalarGridSpec(
            num_scalar_prefetch=1,
            grid=(units,),
            in_specs=[pl.BlockSpec((48, 8, 128), lambda i, s: (i, 0, 0))],
            out_specs=[
                pl.BlockSpec((384, 128), lambda i, s: (i, 0)),
                pl.BlockSpec((8, 128), lambda i, s: (0, 0)),
            ],
        ),
        out_shape=[
            jax.ShapeDtypeStruct((units * 384, 128), jnp.float32),
            jax.ShapeDtypeStruct((8, 128), jnp.float32),
        ],
        name="unpack_tiles",
    )(place, tiles)


def adam_kernel(with_target, scalars, p_ref, m_ref, v_ref, g_ref, *rest):
    if with_target:
        t_ref, po_ref, mo_ref, vo_ref, to_ref = rest
    else:
        po_ref, mo_ref, vo_ref = rest
    grad = g_ref[...] * scalars[0]
    first = BETA_ONE * m_ref[...] + (1 - BETA_ONE) * grad
    second = BETA_TWO * v_ref[...] + (1 - BETA_TWO) * grad * grad
    weight = p_ref[...]
    ratio = (first * scalars[1]) / (jnp.sqrt(second * scalars[2]) + ADAM_EPS)
    weight = weight - RATE_MAT * (ratio + DECAY * weight)
    po_ref[...] = weight
    mo_ref[...] = first
    vo_ref[...] = second
    if with_target:
        to_ref[...] = TAU * t_ref[...] + (1 - TAU) * weight


def adam_flat(scalars, arrays):
    rows = arrays[0].shape[0]
    parts = next((n for n in (9, 6, 3) if rows % (8 * n) == 0), 1)
    with_target = len(arrays) == 5
    spec = pl.BlockSpec((rows // parts, 128), lambda i: (i, 0))
    n_out = 4 if with_target else 3
    return pl.pallas_call(
        functools.partial(adam_kernel, with_target),
        grid=(parts,),
        in_specs=[pl.BlockSpec(memory_space=pltpu.SMEM)] + [spec] * len(arrays),
        out_specs=[spec] * n_out,
        out_shape=[jax.ShapeDtypeStruct((rows, 128), jnp.float32)] * n_out,
        compiler_params=pltpu.CompilerParams(vmem_limit_bytes=32 << 20),
        name="adam",
    )(scalars, *arrays)


def from_tiles(full, ways):
    result = {}
    start = 0
    for label, height, breadth in enc_shapes(ways):
        count = height * breadth // 1024
        piece = full[start : start + count].reshape(height // 8, breadth // 128, 8, 128)
        result[label] = piece.transpose(0, 2, 1, 3).reshape(height, breadth)
        start += count
    return result


def to_tiles(matrix):
    height, breadth = matrix.shape
    return (
        matrix.reshape(height // 8, 8, breadth // 128, 128)
        .transpose(0, 2, 1, 3)
        .reshape(height * breadth // 1024, 8, 128)
    )


def gather_dp(x):
    return lax.all_gather(x, "dp", axis=0, tiled=True)


def gather_flat(flat, shapes):
    return unflat(gather_dp(flat.astype(jnp.bfloat16)).reshape(-1), shapes)


def scatter_flat(grads, shapes, kind):
    whole = jnp.concatenate(
        [grads[label].astype(kind).reshape(-1, 128) for label, _, _ in shapes], 0
    )
    return lax.psum_scatter(whole, "dp", scatter_dimension=0, tiled=True).astype(jnp.float32)


def permute(x, pairs):
    return lax.ppermute(x, "dp", pairs)


XOR_X = [(i, i ^ 1) for i in range(16)]
XOR_Y = [(i, i ^ 2) for i in range(16)]
RING_UP = [(i, (i + 4) % 16) for i in range(16)]
RING_DOWN = [((i + 4) % 16, i) for i in range(16)]


def pick(x, index, axis):
    return lax.dynamic_index_in_dim(x, index, axis, keepdims=False)


def plus(a, b):
    return a.astype(jnp.float32) + b.astype(jnp.float32)


def tree_scatter(tiles, planes):
    low = jnp.bfloat16
    place = lax.axis_index("dp")
    z, y, x = place // 4, place // 2 % 2, place % 2
    count = len(planes)
    copies = 4 // count
    tail = tiles.shape[1:]
    part = tiles.shape[0] // (4 * count * 2 * copies)
    grid = tiles.reshape((count, 2, 2, 2, copies * part) + tail)
    halves = []
    for side in range(2):
        axis_one = 1 if side == 0 else 2
        first_at, second_at = (y, x) if side == 0 else (x, y)
        first_ring, second_ring = (XOR_Y, XOR_X) if side == 0 else (XOR_X, XOR_Y)
        mine = grid[:, :, :, side]
        sent = permute(pick(mine, 1 - first_at, axis_one), first_ring)
        one = plus(pick(mine, first_at, axis_one), sent)
        sent = permute(pick(one, 1 - second_at, 1).astype(low), second_ring)
        two = plus(pick(one, second_at, 1), sent)
        blocks = two.reshape((count, copies, part) + tail).swapaxes(0, 1)
        blocks = blocks.reshape((4, part) + tail)
        step = 1 if side == 0 else -1
        ring = RING_UP if side == 0 else RING_DOWN
        held = pick(blocks, (z - step) % 4, 0)
        for s in range(1, 4):
            held = permute(held, ring) + pick(blocks, (z - step * (s + 1)) % 4, 0)
        pieces = []
        for c in range(copies):
            pairs = [
                ((c * count + j) * 4 + i, planes[j] * 4 + i)
                for j in range(count)
                for i in range(4)
                if c * count + j != planes[j]
            ]
            piece = permute(held.astype(low), pairs).astype(jnp.float32)
            if len(pairs) < 4 * count:
                stay = [planes[j] for j in range(count) if c * count + j == planes[j]]
                here = functools.reduce(jnp.logical_or, [z == p for p in stay])
                piece = jnp.where(here, held, piece)
            pieces.append(piece)
        halves.append(jnp.concatenate(pieces, 0))
    return jnp.concatenate(halves, 0)


def stack_tiles(pieces):
    total = sum(p.shape[0] for p in pieces)
    stacked = jnp.zeros((total,) + pieces[0].shape[1:], pieces[0].dtype)
    start = 0
    for piece in pieces:
        stacked = lax.dynamic_update_slice_in_dim(stacked, piece, start, 0)
        start += piece.shape[0]
    return stacked


def group_pad(x, axis, e, per_group):
    used = e * per_group
    shape = x.shape
    parts = x.reshape(shape[:axis] + (shape[axis] // used, used) + shape[axis + 1 :])
    widths = [(0, 0)] * parts.ndim
    widths[axis + 1] = (0, 128 - used)
    padded = jnp.pad(parts, widths)
    return padded.reshape(shape[:axis] + (shape[axis] // used * 128,) + shape[axis + 1 :])


def group_cut(x, axis, e, per_group):
    used = e * per_group
    shape = x.shape
    parts = x.reshape(shape[:axis] + (shape[axis] // 128, 128) + shape[axis + 1 :])
    parts = lax.slice_in_dim(parts, 0, used, axis=axis + 1)
    return parts.reshape(shape[:axis] + (shape[axis] // 128 * used,) + shape[axis + 1 :])


def layer_forward(stream, mats, vectors, tag, per_group, head_dim, sides, ways, member):
    normed_low = layer_norm(stream, vectors[tag + "ln1_g"], vectors[tag + "ln1_b"]).astype(
        jnp.bfloat16
    )
    bias = group_pad(
        local_columns(vectors["b_" + tag + "qkv"], True, ways, member), 0, head_dim, per_group
    )
    packed = (matmul(normed_low, mats["w_" + tag + "qkv"]) + bias).astype(jnp.bfloat16)
    mixed_rows, log_totals = attn_fwd(packed, sides[0], sides[1], per_group, head_dim)
    attn_part = matmul(mixed_rows, mats["w_" + tag + "out"])
    middle = stream + tensor_total(attn_part) + vectors["b_" + tag + "out"]
    normed_two = layer_norm(middle, vectors[tag + "ln2_g"], vectors[tag + "ln2_b"]).astype(
        jnp.bfloat16
    )
    hidden = matmul(normed_two, mats["w_" + tag + "up"]) + local_columns(
        vectors["b_" + tag + "up"], False, ways, member
    )
    activated = jax.nn.gelu(hidden).astype(jnp.bfloat16)
    down_part = matmul(activated, mats["w_" + tag + "down"])
    result = middle + tensor_total(down_part) + vectors["b_" + tag + "down"]
    kept = (
        stream,
        normed_low,
        packed,
        mixed_rows,
        log_totals,
        middle,
        normed_two,
        hidden,
        activated,
    )
    return (result, kept)


def layer_backward(grad_out, kept, mats, vectors, tag, per_group, head_dim, sides):
    (
        stream,
        normed_low,
        packed,
        mixed_rows,
        log_totals,
        middle,
        normed_two,
        hidden,
        activated,
    ) = kept
    grads = {}
    grad_low = grad_out.astype(jnp.bfloat16)
    grads["w_" + tag + "down"] = matmul_tn(activated, grad_low)
    grads["b_" + tag + "down"] = jnp.sum(grad_out, axis=0)
    grad_act = matmul_nt(grad_low, mats["w_" + tag + "down"])
    grad_hidden = jax.vjp(jax.nn.gelu, hidden)[1](grad_act)[0].astype(jnp.bfloat16)
    grads["w_" + tag + "up"] = matmul_tn(normed_two, grad_hidden)
    grads["b_" + tag + "up"] = jnp.sum(grad_hidden.astype(jnp.float32), axis=0)
    grad_normed = tensor_back(matmul_nt(grad_hidden, mats["w_" + tag + "up"]))
    grad_middle, grads[tag + "ln2_g"], grads[tag + "ln2_b"] = norm_backward(
        middle, vectors[tag + "ln2_g"], vectors[tag + "ln2_b"], grad_normed
    )
    grad_middle = grad_middle + grad_out
    grad_mid_low = grad_middle.astype(jnp.bfloat16)
    grads["w_" + tag + "out"] = group_cut(
        matmul_tn(mixed_rows, grad_mid_low), 0, head_dim, per_group
    )
    grads["b_" + tag + "out"] = jnp.sum(grad_middle, axis=0)
    grad_mixed = matmul_nt(grad_mid_low, mats["w_" + tag + "out"]).astype(jnp.bfloat16)
    grad_packed = attn_bwd(
        packed, grad_mixed, sides[0], sides[1], log_totals, per_group, head_dim
    )
    grads["w_" + tag + "qkv"] = group_cut(
        matmul_tn(normed_low, grad_packed), 1, head_dim, per_group
    )
    grads["b_" + tag + "qkv"] = group_cut(
        jnp.sum(grad_packed.astype(jnp.float32), axis=0), 0, head_dim, per_group
    )
    grad_first = tensor_back(matmul_nt(grad_packed, mats["w_" + tag + "qkv"]))
    grad_stream, grads[tag + "ln1_g"], grads[tag + "ln1_b"] = norm_backward(
        stream, vectors[tag + "ln1_g"], vectors[tag + "ln1_b"], grad_first
    )
    return (grad_stream + grad_middle, grads)


def adam(weight, first, second, grad, rate, decay, count):
    first_new = BETA_ONE * first + (1 - BETA_ONE) * grad
    second_new = BETA_TWO * second + (1 - BETA_TWO) * grad * grad
    first_hat = first_new / (1 - BETA_ONE**count)
    second_hat = second_new / (1 - BETA_TWO**count)
    weight_new = weight - rate * (first_hat / (jnp.sqrt(second_hat) + ADAM_EPS) + decay * weight)
    return (weight_new, first_new, second_new)


ENC_GROUP = 2
PRED_GROUP = 3


def shards(
    enc_params,
    enc_m1,
    enc_m2,
    pred_params,
    pred_m1,
    pred_m2,
    target_params,
    vecs,
    vec_m1,
    vec_m2,
    target_vecs,
    patches,
    segment,
    context,
    step_count,
):
    ways = lax.axis_size("tensor")
    member = lax.axis_index("tensor")
    dp_count = lax.axis_size("dp")
    place = lax.axis_index("dp").astype(jnp.int32).reshape(1)
    spans = enc_chunks(ways)
    rows = lambda x: x.reshape(-1, 128)
    tiled = dp_count == 16 and enc_params.shape[1] % UNIT == 0 and all(
        a % 3 == 0 and b % 3 == 0 for a, b, w in spans if w == 12
    )
    if tiled:
        enc_tiles = gather_dp(pack_tiles(rows(enc_params), place, spans))
        mats = from_tiles(enc_tiles, ways)
        target_tiles = pack_tiles(rows(target_params), place, spans)
    else:
        mats = gather_flat(rows(enc_params), enc_shapes(ways))
    mats.update(gather_flat(rows(pred_params), pred_shapes(ways)))
    mats["w_pqkv"] = group_pad(mats["w_pqkv"], 1, PHEAD_DIM, PRED_GROUP)
    mats["w_pout"] = group_pad(mats["w_pout"], 0, PHEAD_DIM, PRED_GROUP)
    vectors = split_vector(vecs, enc_vectors() + pred_vectors())
    target_vectors = split_vector(target_vecs, enc_vectors())
    places = positions(segment)
    context_mask = context > 0
    padded = roundup(segment.shape[0], QB)
    online_sides = mask_sides(segment, context, padded)
    all_sides = mask_sides(segment, jnp.ones_like(context), padded)
    embed_pos = sincos(places, D)

    def embed(patch_rows, weight_set, vector_set):
        return (
            tensor_total(matmul(patch_rows, weight_set["w_patch"])) + vector_set["b_patch"] + embed_pos
        )

    online_mid, online_kept = layer_forward(
        embed(patches, mats, vectors), mats, vectors, "", ENC_GROUP, HEAD_DIM, online_sides, ways, member
    )
    encoded_low = layer_norm(online_mid, vectors["lnf_g"], vectors["lnf_b"]).astype(jnp.bfloat16)
    pin_local = matmul(encoded_low, mats["w_pin"]) + local_columns(
        vectors["b_pin"], False, ways, member
    )
    pin_other = swap(pin_local)
    pin_full = jnp.where(
        member == 0,
        jnp.concatenate([pin_local, pin_other], 1),
        jnp.concatenate([pin_other, pin_local], 1),
    )
    pred_in = jnp.where(context_mask[:, None], pin_full, vectors["mask_tok"][None, :]) + sincos(
        places, PD
    )
    pred_mid, pred_kept = layer_forward(
        pred_in, mats, vectors, "p", PRED_GROUP, PHEAD_DIM, all_sides, ways, member
    )
    pred_rows = layer_norm(pred_mid, vectors["plnf_g"], vectors["plnf_b"]).astype(jnp.bfloat16)
    predicted = matmul(pred_rows, mats["w_pproj"]) + local_columns(
        vectors["b_pproj"], False, ways, member
    )
    if tiled:
        target_mats = from_tiles(gather_dp(target_tiles), ways)
    else:
        target_mats = gather_flat(rows(target_params), enc_shapes(ways))
    target_patches, predicted = lax.optimization_barrier((patches, predicted))
    target_mid, _ = layer_forward(
        embed(target_patches, target_mats, target_vectors),
        target_mats,
        target_vectors,
        "",
        ENC_GROUP,
        HEAD_DIM,
        all_sides,
        ways,
        member,
    )
    targets = plain_norm(layer_norm(target_mid, target_vectors["lnf_g"], target_vectors["lnf_b"]))
    target_cols = lax.dynamic_slice_in_dim(targets, member * (D // ways), D // ways, 1)
    target_mask = (1 - context).astype(jnp.float32)
    width = D // ways
    sums = doubling(
        jnp.concatenate(
            [
                jnp.sum(target_mask[:, None] * predicted, axis=0),
                jnp.sum(target_mask[:, None] * predicted * predicted, axis=0),
                jnp.broadcast_to(jnp.sum(target_mask), (128,)),
            ]
        ),
        "dp",
    )
    sum_all, square_all, count_all = sums[:width], sums[width : 2 * width], sums[2 * width]
    difference = predicted - target_cols
    error = jnp.sum(target_mask[:, None] * jnp.abs(difference)) / (count_all * D)
    column_mean = sum_all / count_all
    column_var = square_all / count_all - column_mean * column_mean
    spread = jnp.sqrt(column_var + VAR_EPS)
    local_loss = error + jnp.sum((spread - 1.0) ** 2) / D / dp_count
    grad_var = (spread - 1.0) / (D * spread)
    grad_pred = target_mask[:, None] * (
        jnp.sign(difference) / (count_all * D)
        + 2.0 * grad_var * (predicted - column_mean) / count_all
    )
    grads = {}
    grad_low = grad_pred.astype(jnp.bfloat16)
    grads["w_pproj"] = matmul_tn(pred_rows, grad_low)
    grads["b_pproj"] = jnp.sum(grad_pred, axis=0)
    grad_normed = tensor_back(matmul_nt(grad_low, mats["w_pproj"]))
    grad_mid, grads["plnf_g"], grads["plnf_b"] = norm_backward(
        pred_mid, vectors["plnf_g"], vectors["plnf_b"], grad_normed
    )
    grad_in, layer_grads = layer_backward(
        grad_mid, pred_kept, mats, vectors, "p", PRED_GROUP, PHEAD_DIM, all_sides
    )
    grads.update(layer_grads)
    grads["mask_tok"] = jnp.sum(jnp.where(context_mask[:, None], 0.0, grad_in), axis=0)
    grad_pin = lax.dynamic_slice_in_dim(
        jnp.where(context_mask[:, None], grad_in, 0.0), member * (PD // ways), PD // ways, 1
    )
    grad_pin_low = grad_pin.astype(jnp.bfloat16)
    grads["w_pin"] = matmul_tn(encoded_low, grad_pin_low)
    grads["b_pin"] = jnp.sum(grad_pin, axis=0)
    grad_encoded = tensor_back(matmul_nt(grad_pin_low, mats["w_pin"]))
    grad_mid, grads["lnf_g"], grads["lnf_b"] = norm_backward(
        online_mid, vectors["lnf_g"], vectors["lnf_b"], grad_encoded
    )
    pred_share = scatter_flat(grads, pred_shapes(ways), jnp.float32)
    grad_in, layer_grads = layer_backward(
        grad_mid, online_kept, mats, vectors, "", ENC_GROUP, HEAD_DIM, online_sides
    )
    grads.update(layer_grads)
    grads["w_patch"] = matmul_tn(patches, grad_in.astype(jnp.bfloat16))
    grads["b_patch"] = jnp.sum(grad_in, axis=0)
    if tiled:
        pieces = {
            label: to_tiles(grads[label].astype(jnp.bfloat16)) for label, _, _ in enc_shapes(ways)
        }
        groups = []
        quarter = sum(p.shape[0] for p in pieces.values()) // 4
        for planes in ((2, 3), (1,), (0,)):
            low, high = planes[0] * quarter, (planes[-1] + 1) * quarter
            chosen = []
            start = 0
            for label, _, _ in enc_shapes(ways):
                end = start + pieces[label].shape[0]
                if start < high and end > low:
                    chosen.append(pieces[label][max(low - start, 0) : min(high, end) - start])
                start = end
            groups.append(tree_scatter(stack_tiles(chosen), planes))
        share = jnp.where(
            place[0] >= 8, groups[0], jnp.where(place[0] >= 4, groups[1], groups[2])
        )
        enc_share, enc_square = unpack_tiles(share, place, spans)
    else:
        enc_share = scatter_flat(grads, enc_shapes(ways), jnp.float32)
        enc_square = enc_share * enc_share
    halves = []
    for label, length in enc_vectors() + pred_vectors():
        if label in LOCAL_BIAS:
            halves.append(place_columns(grads[label], length, LOCAL_BIAS[label], ways, member))
        else:
            halves.append(0.5 * grads[label])
    halves.append(jnp.broadcast_to(local_loss, (128,)))
    vector_sum = doubling(doubling(jnp.concatenate(halves), "tensor"), "dp")
    vector_grad, loss_value = vector_sum[: vecs.shape[0]], vector_sum[vecs.shape[0]]
    square_sum = jnp.sum(enc_square) + jnp.sum(pred_share * pred_share)
    square_total = doubling(doubling(jnp.broadcast_to(square_sum, (128,)), "tensor"), "dp")[0]
    grad_norm = jnp.sqrt(square_total + jnp.sum(vector_grad * vector_grad))
    factor = jnp.minimum(1.0, CLIP / (grad_norm + 1e-06))
    count = step_count[0].astype(jnp.float32)
    scalars = jnp.stack(
        [factor, 1.0 / (1 - BETA_ONE**count), 1.0 / (1 - BETA_TWO**count)]
    ).astype(jnp.float32)
    back = lambda x: x.reshape(1, -1)
    new_enc, enc_first, enc_second, new_target = map(
        back,
        adam_flat(
            scalars,
            [rows(enc_params), rows(enc_m1), rows(enc_m2), enc_share, rows(target_params)],
        ),
    )
    new_pred, pred_first, pred_second = map(
        back, adam_flat(scalars, [rows(pred_params), rows(pred_m1), rows(pred_m2), pred_share])
    )
    new_vec, vec_first, vec_second = adam(
        vecs, vec_m1, vec_m2, vector_grad * factor, RATE_VEC, 0.0, count
    )
    new_target_vec = TAU * target_vecs + (1 - TAU) * new_vec[: target_vecs.shape[0]]
    return (
        new_enc,
        enc_first,
        enc_second,
        new_enc.astype(jnp.bfloat16),
        new_pred,
        pred_first,
        pred_second,
        new_pred.astype(jnp.bfloat16),
        new_target,
        new_vec,
        vec_first,
        vec_second,
        new_target_vec,
        loss_value,
        grad_norm,
    )


def solution(mesh):
    placed = (
        P("tensor", "dp"),
        P("tensor", "dp"),
        P("tensor", "dp"),
        P("tensor", "dp"),
        P("tensor", "dp"),
        P("tensor", "dp"),
        P("tensor", "dp"),
        P(),
        P(),
        P(),
        P(),
        P("dp", "tensor"),
        P("dp"),
        P("dp"),
        P(),
    )
    return jax.shard_map(
        shards,
        mesh=mesh,
        in_specs=placed,
        out_specs=(
            P("tensor", "dp"),
            P("tensor", "dp"),
            P("tensor", "dp"),
            P("tensor", "dp"),
            P("tensor", "dp"),
            P("tensor", "dp"),
            P("tensor", "dp"),
            P("tensor", "dp"),
            P("tensor", "dp"),
            P(),
            P(),
            P(),
            P(),
            P(),
            P(),
        ),
        check_vma=False,
    )
```

time: 2860 us -> 1240 us (0.43)
  waiting for transfers between devices: 1430 us -> 406 us
  local copies, waits for them, and re-layouts: 653 us -> 140 us
  matrix products: 431 us -> 157 us
  Pallas kernels: 0 us -> 226 us
  starting transfers between devices: 2.12 us -> 94.1 us
  blocking collectives: 84.2 us -> 0 us
    unnamed x20 -> x4, waiting for transfers between devices: 835 us -> 0.07 us
    slice x12 -> x5, local copies, waits for them, and re-layouts: 424 us -> 5.85 us  [unflat(): flat_row[offset:offset + height * breadth].reshape(height, breadth)]
    pallas_call x0 -> x10, Pallas kernels: none -> 226 us  [the longest x2 100 us: attn_bwd(): pl.pallas_call(functools.partial(attn_bwd_kernel, heads, e, T, TP, W), gr...]
    psum x12 -> x0, waiting for transfers between devices: 218 us -> none  [the longest x1 119 us: shards(): lax.psum((square_sum, vector_part, local_loss), ('dp', 'tensor'))]
    ppermute x0 -> x79, waiting for transfers between devices: none -> 200 us  [the longest x50 146 us: permute(): return lax.ppermute(x, 'dp', pairs)]
    all_gather x4 -> x3, waiting for transfers between devices: 377 us -> 206 us  [gather_dp(): return lax.all_gather(x, 'dp', axis=0, tiled=True)]
    dot_general x60 -> x10, matrix products: 180 us -> 43.7 us  [matmul_nt(): lax.dot_general(left, right, (((1,), (1,)), ((), ())), preferred_element_...]
    ppermute x0 -> x79, starting transfers between devices: none -> 93.8 us  [the longest x50 80.7 us: permute(): return lax.ppermute(x, 'dp', pairs)]
  transfers between devices with their start and end apart: 18 -> 83, of which waited for: 12 -> 44; matrix products, arithmetic and copies ran while one was open for 28% -> 21% of each run, Pallas kernels for 0% -> 11%
where the time goes in v1:
time: 1240 us
  waiting for transfers between devices  406 us (33%)
  Pallas kernels  226 us (18%)
  other arithmetic  190 us (15%)
  matrix products  157 us (13%)
  local copies, waits for them, and re-layouts  140 us (11%)
  starting transfers between devices  94.1 us (8%)
  between operations  24.1 us (2%)
    all_gather x3, waiting for transfers between devices, gather_dp(): return lax.all_gather(x, 'dp', axis=0, tiled=True)  206 us
    ppermute x50, waiting for transfers between devices, permute(): return lax.ppermute(x, 'dp', pairs)  146 us
    pallas_call x2, Pallas kernels, attn_bwd(): pl.pallas_call(functools.partial(attn_bwd_kernel, heads, e, T, TP, W), gr...  100 us
    pallas_call x3, Pallas kernels, attn_fwd(): pl.pallas_call(functools.partial(attn_fwd_kernel, heads, e, T, TP, W), gr...  99.5 us
    ppermute x50, starting transfers between devices, permute(): return lax.ppermute(x, 'dp', pairs)  80.7 us
    dot_general x15, matrix products, matmul(): return jnp.dot(left, right, preferred_element_type=jnp.float32)  66.9 us
    reduce_sum x13, other arithmetic, layer_norm(): centered = values - jnp.mean(values, axis=-1, keepdims=True)  53.6 us
    dot_general x11, matrix products, matmul_tn(): lax.dot_general(left, right, (((0,), (0,)), ((), ())), preferred_element_...  46.4 us
  transfers between devices with their start and end apart: 83, of which 44 were waited for; matrix products, arithmetic and copies ran while one was open for 21% of the time, Pallas kernels for 11%

profile of v1, /device:TPU:0, one launch (start us, length us, event | category | flops | bytes accessed | tf_op | source)
XLA Modules:
  0.0 1237.0 jit_solution(16002636040857137410)
XLA Ops:
  7.3 6.2 pack_tiles.2
  14.3 168.9 %all-gather.4.cloned.1.call-done = bf16[6912,8,128]{2,1,0:T(8,128)(2,1)} async-done(((bf16[432,8,128]{2,1,0:T(8,128)(2,1)}), bf16[6912,8,128]{2,1,0:T(8,128)(2,1)}) %all-gather.4.cloned.1.call-update) | async-done | bytes 14155792 | tf_op jit(solution)/shard_map/all_gather | solution.py:520
  188.9 6.1 pack_tiles.3
  197.8 9.7 multiply_sine_fusion
  213.8 5.4 fusion.131
  222.8 4.6 fusion.15.packed_ref
  227.5 36.5 %attn_fwd.3 = (bf16[1176,512]{1,0:T(8,128)(2,1)S(1)}, f32[4,8,1280]{2,1,0:T(8,128)S(1)}) custom-call(bf16[1176,1536]{1,0:T(8,128)(2,1)S(1)} %fusion.15.packed_ref, bf16[1280,128]{1,0:T(8,128)(2,1)S(1)} %concatenate.43.qa_ref, bf16[1280,128]{1,0:T(8,128)(2,1)S(1)} %get-tuple-element.156.ka_ref), custom_call_target="tpu_custom_call" | custom-call | flops 11329339392 | bytes 5419008 | tf_op jit(solution)/shard_map/attn_fwd/pallas_call | solution.py:242
  268.1 5.5 fusion.133
  276.1 5.1 fusion.130
  281.9 5.7 convolution_add_fusion.2
  287.7 7.6 fusion.112
  299.2 4.5 collective-permute-done.2
  303.7 6.0 fusion.129
  314.3 5.3 multiply_sine_fusion.1
  331.4 25.9 %attn_fwd.4 = (bf16[1176,256]{1,0:T(8,128)(2,1)S(1)}, f32[2,8,1280]{2,1,0:T(8,128)S(1)}) custom-call(bf16[1176,768]{1,0:T(8,128)(2,1)S(1)} %fusion.29.packed_ref, bf16[1280,128]{1,0:T(8,128)(2,1)S(1)} %concatenate.43.qa_ref, bf16[1280,128]{1,0:T(8,128)(2,1)S(1)} %get-tuple-element.155.ka_ref), custom_call_target="tpu_custom_call" | custom-call | flops 8497004544 | bytes 2709504 | tf_op jit(solution)/shard_map/attn_fwd/pallas_call | solution.py:242
  380.7 36.7 %all-gather.8.cloned.1.call-done = bf16[6912,8,128]{2,1,0:T(8,128)(2,1)} async-done(((bf16[432,8,128]{2,1,0:T(8,128)(2,1)}), bf16[6912,8,128]{2,1,0:T(8,128)(2,1)}) %all-gather.8.cloned.1.call-update) | async-done | bytes 14155792 | tf_op jit(solution)/shard_map/all_gather | solution.py:520
  433.6 8.3 collective-permute-done.6
  441.9 5.3 fusion.124
  449.1 4.6 fusion.16.packed_ref
  453.7 37.1 %attn_fwd.5 = (bf16[1176,512]{1,0:T(8,128)(2,1)S(1)}, f32[4,8,1280]{2,1,0:T(8,128)}) custom-call(bf16[1176,1536]{1,0:T(8,128)(2,1)S(1)} %fusion.16.packed_ref, bf16[1280,128]{1,0:T(8,128)(2,1)S(1)} %concatenate.43.qa_ref, bf16[1280,128]{1,0:T(8,128)(2,1)S(1)} %get-tuple-element.155.ka_ref), custom_call_target="tpu_custom_call" | custom-call | flops 11329339392 | bytes 5419008 | tf_op jit(solution)/shard_map/attn_fwd/pallas_call | solution.py:242
  492.5 7.6 fusion.132
  502.6 5.1 fusion.123
  510.5 19.4 %fusion.56 = f32[1176,1024]{1,0:T(8,128)} fusion(bf16[2048,1024]{1,0:T(8,128)(2,1)} %bitcast.382, bf16[1024,2048]{1,0:T(8,128)(2,1)} %bitcast.381, f32[2048]{0:T(1024)S(1)} %dynamic_slice.189, f32[1176,1024]{1,0:T(8,128)} %copy-done.30, f32[1024]{0:T(1024)S(1)} %get-tuple-element.148, f32[1024]{0:T(1024)S(1)} %get-tuple-element.149, ...), kind=kOutput, calls=%fused_computation.171 | convolution fusion | flops 9895108608 | bytes 18048192 | tf_op jit(solution)/shard_map/dot_general | solution.py:144
  530.7 7.5 collective-permute-done.8
  538.2 5.0 fusion.122
  570.1 4.7 fusion.115
  591.4 4.2 convert_reduce_fusion.3
  614.3 41.4 %attn_bwd.2 = bf16[1176,768]{1,0:T(8,128)(2,1)S(1)} custom-call(bf16[1176,768]{1,0:T(8,128)(2,1)S(1)} %copy-done.21, bf16[1176,256]{1,0:T(8,128)(2,1)S(1)} %convolution_convert_fusion.9.do_ref, bf16[1280,128]{1,0:T(8,128)(2,1)S(1)} %concatenate.43.qa_ref, bf16[1280,128]{1,0:T(8,128)(2,1)S(1)} %get-tuple-element.155.ka_ref, ...), custom_call_target="tpu_custom_call" | custom-call | flops 21242511360 | bytes 4515840 | tf_op jit(solution)/shard_map/attn_bwd/pallas_call | solution.py:309
  684.0 4.2 fusion.110
  710.6 6.9 multiply_reduce_fusion
  717.5 4.5 fusion.119
  722.1 16.1 %convert_reduce_fusion = (f32[2048]{0:T(1024)S(1)}, bf16[1176,2048]{1,0:T(8,128)(2,1)}) fusion(f32[1176,2048]{1,0:T(8,128)} %copy-done.187, bf16[2048,1024]{1,0:T(8,128)(2,1)S(1)} %bitcast.380, f32[1176,1024]{1,0:T(8,128)S(1)} %get-tuple-element.86, f32[1176]{0:T(1024)S(1)} %negate_multiply_fusion.2), kind=kOutput, calls=%fused_computation.18 | convolution fusion | flops 4987893760 | bytes 23474784 | tf_op jit(solution)/shard_map/dot_general | solution.py:154
  738.2 9.5 convolution_convert_fusion.3
  747.8 7.0 convert_bitcast_fusion
  755.0 24.7 %pad_maximum_fusion = bf16[3456,8,128]{2,1,0:T(8,128)(2,1)S(1)} fusion(bf16[2048,8,128]{2,1,0:T(8,128)(2,1)S(1)} %bitcast.376, bf16[1408,8,128]{2,1,0:T(8,128)(2,1)S(1)} %bitcast.337), kind=kLoop, calls=%fused_computation.29 | loop fusion | flops 3538944 | bytes 14155776 | tf_op jit(solution)/shard_map/dynamic_update_slice | solution.py:601
  783.7 9.3 convolution_convert_fusion.2
  802.8 24.3 %collective-permute-done.24 = bf16[2,2,216,8,128]{4,3,2,1,0:T(8,128)(2,1)} collective-permute-done((bf16[2,2,216,8,128]{4,3,2,1,0:T(8,128)(2,1)}, bf16[2,2,216,8,128]{4,3,2,1,0:T(8,128)(2,1)}, u32[]{:S(2)}, u32[]{:S(2)}) %collective-permute-start.24) | collective-permute-done | bytes 1769504 | tf_op jit(solution)/shard_map/ppermute | solution.py:535
  832.1 11.1 collective-permute-done.17
  848.1 4.6 multiply_reduce_fusion.1
  852.8 4.5 fusion.118
  862.7 58.6 %attn_bwd.3 = bf16[1176,1536]{1,0:T(8,128)(2,1)S(1)} custom-call(bf16[1176,1536]{1,0:T(8,128)(2,1)} %copy-done.22, bf16[1176,512]{1,0:T(8,128)(2,1)S(1)} %convolution_convert_fusion.5.do_ref, bf16[1280,128]{1,0:T(8,128)(2,1)S(1)} %concatenate.43.qa_ref, bf16[1280,128]{1,0:T(8,128)(2,1)S(1)} %copy-done.15, f32[4,8,1280]{2,1,0:T(8,128)S(1)} %get-tuple-element.37.lse_ref), custom_call_target="tpu_custom_call" | custom-call | flops 28323348480 | bytes 9031680 | tf_op jit(solution)/shard_map/attn_bwd/pallas_call | solution.py:309
  922.1 5.0 fusion.44
  928.7 4.3 dynamic_update_slice.36
  937.7 5.3 convolution_convert_fusion.1
  952.4 4.3 collective-permute-done.26
  957.9 4.3 collective-permute-start.27
  962.2 5.9 collective-permute-done.19
  979.7 7.3 collective-permute-done.20
  991.6 19.1 %collective-permute-done.34 = f32[54,8,128]{2,1,0:T(8,128)S(1)} collective-permute-done((f32[54,8,128]{2,1,0:T(8,128)S(1)}, f32[54,8,128]{2,1,0:T(8,128)S(1)}, u32[]{:S(2)}, u32[]{:S(2)}) %collective-permute-start.34) | collective-permute-done | bytes 221216 | tf_op jit(solution)/shard_map/ppermute | solution.py:535
  1023.2 9.1 collective-permute-start.22
  1032.5 5.6 collective-permute-done.22
  1038.1 6.7 collective-permute-start.45
  1048.8 7.4 collective-permute-start.37
  1060.7 5.6 collective-permute-start.46
  1085.3 11.2 pad_maximum_fusion.2
  1101.8 14.3 %collective-permute-done.51 = bf16[1,2,216,8,128]{4,3,2,1,0:T(8,128)(2,1)S(1)} collective-permute-done((bf16[1,2,216,8,128]{4,3,2,1,0:T(8,128)(2,1)S(1)}, bf16[1,2,216,8,128]{4,3,2,1,0:T(8,128)(2,1)S(1)}, u32[]{:S(2)}, u32[]{:S(2)}) %collective-permute-start.51) | collective-permute-done | bytes 884768 | tf_op jit(solution)/shard_map/ppermute | solution.py:535
  1120.3 4.4 collective-permute-done.52
  1128.8 6.1 collective-permute-done.53
  1144.3 9.2 collective-permute-done.63
  1157.6 5.8 collective-permute-done.64
  1168.9 6.0 collective-permute-done.66
  1176.6 6.3 unpack_tiles.1
  1188.9 4.5 collective-permute-done.77
  1219.2 5.5 adam.2
  (894 shorter events, 374.8 us)
Async XLA Ops:
  7.2 176.0 %all-gather.4.cloned.1.call-start = ((), (), s32[]{:S(2)}) async-start(), calls=%async_computation.1 | async-start | bytes 15040512 | tf_op jit(solution)/shard_map/all_gather | solution.py:520
  13.5 283.5 %all-gather.6.cloned.1.call-start = ((), (), s32[]{:S(2)}) async-start(), calls=%async_computation.2 | async-start | bytes 2715648 | tf_op jit(solution)/shard_map/all_gather | solution.py:520
  14.2 403.2 %all-gather.8.cloned.1.call-start = ((), (), s32[]{:S(2)}) async-start(), calls=%async_computation.3 | async-start | bytes 15040512 | tf_op jit(solution)/shard_map/all_gather | solution.py:520
  188.8 25.0 %collective-permute-start = (f32[1176,1024]{1,0:T(8,128)}, f32[1176,1024]{1,0:T(8,128)}, u32[]{:S(2)}, u32[]{:S(2)}) collective-permute-start(f32[1176,1024]{1,0:T(8,128)} %convolution_bitcast_fusion), channel_id=1, source_target_pairs={{0,1},{1,0},{2,3},{3,2},{4,5},{5,4},{6,7},{7,6},{8,9},{9,8},{10,11... | collective-permute-start | bytes 14450696 | tf_op jit(solution)/shard_map/ppermute | solution.py:338
  195.0 989.2 %reduce-scatter.2.cloned.1.call-start = ((), (), s32[]{:S(2)}) async-start(), calls=%async_computation.4 | async-start | bytes 5431296 | tf_op jit(solution)/shard_map/reduce_scatter | solution.py:531
  267.6 8.5 collective-permute-start.1
  295.3 8.4 collective-permute-start.2
  313.7 12.6 %collective-permute-start.3 = (f32[1176,192]{0,1:T(8,128)}, f32[1176,192]{0,1:T(8,128)}, u32[]{:S(2)}, u32[]{:S(2)}) collective-permute-start(f32[1176,192]{0,1:T(8,128)} %convolution_add_fusion.6), channel_id=1, source_target_pairs={{0,1},{1,0},{2,3},{3,2},{4,5},{5,4},{6,7},{7,6},{8,9},{9,8},{10,11... | collective-permute-start | bytes 2709512 | tf_op jit(solution)/shard_map/ppermute | solution.py:338
  359.9 8.8 collective-permute-start.4
  379.3 41.1 %collective-permute-start.5 = (f32[1176,384]{1,0:T(8,128)}, f32[1176,384]{1,0:T(8,128)}, u32[]{:S(2)}, u32[]{:S(2)}) collective-permute-start(f32[1176,384]{1,0:T(8,128)} %fusion.111), channel_id=1, source_target_pairs={{0,1},{1,0},{2,3},{3,2},{4,5},{5,4},{6,7},{7,6},{8,9},{9,8},{10,11... | collective-permute-start | bytes 5419016 | tf_op jit(solution)/shard_map/ppermute | solution.py:338
  433.5 8.4 collective-permute-start.6
  529.9 8.3 collective-permute-start.8
  674.3 36.3 %collective-permute-start.16 = (bf16[1176,1024]{1,0:T(8,128)(2,1)}, bf16[1176,1024]{1,0:T(8,128)(2,1)}, u32[]{:S(2)}, u32[]{:S(2)}) collective-permute-start(bf16[1176,1024]{1,0:T(8,128)(2,1)} %convolution_convert_fusion.4), channel_id=1, source_target_pairs={{0,1},{1,0},{2,3},{3,2},{4,5},{5,4},{6,7},{7,6},{8,9},{9,8},{10,11... | collective-permute-start | bytes 7225352 | tf_op jit(solution)/shard_map/ppermute | solution.py:338
  781.5 45.6 %collective-permute-start.24 = (bf16[2,2,216,8,128]{4,3,2,1,0:T(8,128)(2,1)}, bf16[2,2,216,8,128]{4,3,2,1,0:T(8,128)(2,1)}, u32[]{:S(2)}, u32[]{:S(2)}) collective-permute-start(bf16[2,2,216,8,128]{4,3,2,1,0:T(8,128)(2,1)} %dynamic-slice_bitcast_fusion), channel_id=1, source_target_pairs={{0,2},{2,0},{4,6},{6,4},{8,10},{10,8},{12,14},{14,12},{16,18},{18,... | collective-permute-start | bytes 5308424 | tf_op jit(solution)/shard_map/ppermute | solution.py:535
  793.0 55.1 %collective-permute-start.31 = (bf16[1176,1024]{1,0:T(8,128)(2,1)}, bf16[1176,1024]{1,0:T(8,128)(2,1)}, u32[]{:S(2)}, u32[]{:S(2)}) collective-permute-start(bf16[1176,1024]{1,0:T(8,128)(2,1)} %convolution_convert_fusion.2), channel_id=1, source_target_pairs={{0,1},{1,0},{2,3},{3,2},{4,5},{5,4},{6,7},{7,6},{8,9},{9,8},{10,11... | collective-permute-start | bytes 7225352 | tf_op jit(solution)/shard_map/ppermute | solution.py:338
  794.6 48.6 %collective-permute-start.17 = (bf16[2,2,216,8,128]{4,3,2,1,0:T(8,128)(2,1)}, bf16[2,2,216,8,128]{4,3,2,1,0:T(8,128)(2,1)}, u32[]{:S(2)}, u32[]{:S(2)}) collective-permute-start(bf16[2,2,216,8,128]{4,3,2,1,0:T(8,128)(2,1)} %dynamic-slice_bitcast_fusion.1), channel_id=1, source_target_pairs={{0,4},{2,6},{4,0},{6,2},{8,12},{10,14},{12,8},{14,10},{16,20},{18,... | collective-permute-start | bytes 5308424 | tf_op jit(solution)/shard_map/ppermute | solution.py:535
  830.6 112.4 %collective-permute-start.25 = (bf16[2,216,8,128]{3,2,1,0:T(8,128)(2,1)}, bf16[2,216,8,128]{3,2,1,0:T(8,128)(2,1)}, u32[]{:S(2)}, u32[]{:S(2)}) collective-permute-start(bf16[2,216,8,128]{3,2,1,0:T(8,128)(2,1)} %fusion.58), channel_id=1, source_target_pairs={{0,4},{2,6},{4,0},{6,2},{8,12},{10,14},{12,8},{14,10},{16,20},{18,... | collective-permute-start | bytes 2654216 | tf_op jit(solution)/shard_map/ppermute | solution.py:535
  846.4 99.3 %collective-permute-start.18 = (bf16[2,216,8,128]{3,2,1,0:T(8,128)(2,1)}, bf16[2,216,8,128]{3,2,1,0:T(8,128)(2,1)}, u32[]{:S(2)}, u32[]{:S(2)}) collective-permute-start(bf16[2,216,8,128]{3,2,1,0:T(8,128)(2,1)} %fusion.57), channel_id=1, source_target_pairs={{0,2},{2,0},{4,6},{6,4},{8,10},{10,8},{12,14},{14,12},{16,18},{18,... | collective-permute-start | bytes 2654216 | tf_op jit(solution)/shard_map/ppermute | solution.py:535
  936.1 33.5 %collective-permute-start.32 = (bf16[1,2,216,8,128]{4,3,2,1,0:T(8,128)(2,1)S(1)}, bf16[1,2,216,8,128]{4,3,2,1,0:T(8,128)(2,1)}, u32[]{:S(2)}, u32[]{:S(2)}) collective-permute-start(bf16[1,2,216,8,128]{4,3,2,1,0:T(8,128)(2,1)S(1)} %dynamic-slice_bitcast_fusion.5), channel_id=1, source_target_pairs={{0,4},{2,6},{4,0},{6,2},{8,12},{10,14},{12,8},{14,10},{16,20},{18,... | collective-permute-start | bytes 2654216 | tf_op jit(solution)/shard_map/ppermute | solution.py:535
  944.5 12.2 collective-permute-start.26
  950.4 17.7 %collective-permute-start.19 = (f32[108,8,128]{2,1,0:T(8,128)}, f32[108,8,128]{2,1,0:T(8,128)}, u32[]{:S(2)}, u32[]{:S(2)}) collective-permute-start(f32[108,8,128]{2,1,0:T(8,128)} %dynamic-slice_bitcast_fusion.7), channel_id=1, source_target_pairs={{0,8},{2,10},{4,12},{6,14},{8,16},{10,18},{12,20},{14,22},{16,24},... | collective-permute-start | bytes 1327112 | tf_op jit(solution)/shard_map/ppermute | solution.py:535
  951.9 21.0 %collective-permute-start.41 = (bf16[1,2,216,8,128]{4,3,2,1,0:T(8,128)(2,1)S(1)}, bf16[1,2,216,8,128]{4,3,2,1,0:T(8,128)(2,1)S(1)}, u32[]{:S(2)}, u32[]{:S(2)}) collective-permute-start(bf16[1,2,216,8,128]{4,3,2,1,0:T(8,128)(2,1)S(1)} %dynamic-slice_bitcast_fusion.4), channel_id=1, source_target_pairs={{0,2},{2,0},{4,6},{6,4},{8,10},{10,8},{12,14},{14,12},{16,18},{18,... | collective-permute-start | bytes 2654216 | tf_op jit(solution)/shard_map/ppermute | solution.py:535
  952.4 117.4 %collective-permute-start.50 = (bf16[1176,1024]{1,0:T(8,128)(2,1)}, bf16[1176,1024]{1,0:T(8,128)(2,1)S(1)}, u32[]{:S(2)}, u32[]{:S(2)}) collective-permute-start(bf16[1176,1024]{1,0:T(8,128)(2,1)} %convolution_convert_fusion.1), channel_id=1, source_target_pairs={{0,1},{1,0},{2,3},{3,2},{4,5},{5,4},{6,7},{7,6},{8,9},{9,8},{10,11... | collective-permute-start | bytes 7225352 | tf_op jit(solution)/shard_map/ppermute | solution.py:338
  957.9 18.4 %collective-permute-start.27 = (f32[108,8,128]{2,1,0:T(8,128)S(1)}, f32[108,8,128]{2,1,0:T(8,128)S(1)}, u32[]{:S(2)}, u32[]{:S(2)}) collective-permute-start(f32[108,8,128]{2,1,0:T(8,128)S(1)} %bitcast_add_fusion.8), channel_id=1, source_target_pairs={{8,0},{10,2},{12,4},{14,6},{16,8},{18,10},{20,12},{22,14},{24,16},... | collective-permute-start | bytes 1327112 | tf_op jit(solution)/shard_map/ppermute | solution.py:535
  969.2 17.8 %collective-permute-start.20 = (f32[108,8,128]{2,1,0:T(8,128)S(1)}, f32[108,8,128]{2,1,0:T(8,128)S(1)}, u32[]{:S(2)}, u32[]{:S(2)}) collective-permute-start(f32[108,8,128]{2,1,0:T(8,128)S(1)} %bitcast_add_fusion.11), channel_id=1, source_target_pairs={{0,8},{2,10},{4,12},{6,14},{8,16},{10,18},{12,20},{14,22},{16,24},... | collective-permute-start | bytes 1327112 | tf_op jit(solution)/shard_map/ppermute | solution.py:535
  971.0 16.4 %collective-permute-start.33 = (bf16[1,216,8,128]{3,2,1,0:T(8,128)(2,1)S(1)}, bf16[1,216,8,128]{3,2,1,0:T(8,128)(2,1)S(1)}, u32[]{:S(2)}, u32[]{:S(2)}) collective-permute-start(bf16[1,216,8,128]{3,2,1,0:T(8,128)(2,1)S(1)} %fusion.73), channel_id=1, source_target_pairs={{0,2},{2,0},{4,6},{6,4},{8,10},{10,8},{12,14},{14,12},{16,18},{18,... | collective-permute-start | bytes 1327112 | tf_op jit(solution)/shard_map/ppermute | solution.py:535
  973.1 15.9 %collective-permute-start.42 = (bf16[1,216,8,128]{3,2,1,0:T(8,128)(2,1)S(1)}, bf16[1,216,8,128]{3,2,1,0:T(8,128)(2,1)S(1)}, u32[]{:S(2)}, u32[]{:S(2)}) collective-permute-start(bf16[1,216,8,128]{3,2,1,0:T(8,128)(2,1)S(1)} %fusion.74), channel_id=1, source_target_pairs={{0,4},{2,6},{4,0},{6,2},{8,12},{10,14},{12,8},{14,10},{16,20},{18,... | collective-permute-start | bytes 1327112 | tf_op jit(solution)/shard_map/ppermute | solution.py:535
  976.4 40.0 %collective-permute-start.28 = (f32[108,8,128]{2,1,0:T(8,128)S(1)}, f32[108,8,128]{2,1,0:T(8,128)S(1)}, u32[]{:S(2)}, u32[]{:S(2)}) collective-permute-start(f32[108,8,128]{2,1,0:T(8,128)S(1)} %bitcast_add_fusion.7), channel_id=1, source_target_pairs={{8,0},{10,2},{12,4},{14,6},{16,8},{18,10},{20,12},{22,14},{24,16},... | collective-permute-start | bytes 1327112 | tf_op jit(solution)/shard_map/ppermute | solution.py:535
  987.1 30.1 %collective-permute-start.21 = (f32[108,8,128]{2,1,0:T(8,128)S(1)}, f32[108,8,128]{2,1,0:T(8,128)S(1)}, u32[]{:S(2)}, u32[]{:S(2)}) collective-permute-start(f32[108,8,128]{2,1,0:T(8,128)S(1)} %bitcast_add_fusion.10), channel_id=1, source_target_pairs={{0,8},{2,10},{4,12},{6,14},{8,16},{10,18},{12,20},{14,22},{16,24},... | collective-permute-start | bytes 1327112 | tf_op jit(solution)/shard_map/ppermute | solution.py:535
  987.5 23.1 %collective-permute-start.34 = (f32[54,8,128]{2,1,0:T(8,128)S(1)}, f32[54,8,128]{2,1,0:T(8,128)S(1)}, u32[]{:S(2)}, u32[]{:S(2)}) collective-permute-start(f32[54,8,128]{2,1,0:T(8,128)S(1)} %dynamic-slice_bitcast_fusion.11), channel_id=1, source_target_pairs={{0,8},{2,10},{4,12},{6,14},{8,16},{10,18},{12,20},{14,22},{16,24},... | collective-permute-start | bytes 663560 | tf_op jit(solution)/shard_map/ppermute | solution.py:535
  989.1 23.8 %collective-permute-start.43 = (f32[54,8,128]{2,1,0:T(8,128)S(1)}, f32[54,8,128]{2,1,0:T(8,128)S(1)}, u32[]{:S(2)}, u32[]{:S(2)}) collective-permute-start(f32[54,8,128]{2,1,0:T(8,128)S(1)} %dynamic-slice_bitcast_fusion.10), channel_id=1, source_target_pairs={{8,0},{10,2},{12,4},{14,6},{16,8},{18,10},{20,12},{22,14},{24,16},... | collective-permute-start | bytes 663560 | tf_op jit(solution)/shard_map/ppermute | solution.py:535
  1010.7 10.1 collective-permute-start.35
  1013.0 10.2 collective-permute-start.44
  1016.5 28.4 %collective-permute-start.30 = (bf16[108,8,128]{2,1,0:T(8,128)(2,1)S(1)}, bf16[108,8,128]{2,1,0:T(8,128)(2,1)S(1)}, u32[]{:S(2)}, u32[]{:S(2)}) collective-permute-start(bf16[108,8,128]{2,1,0:T(8,128)(2,1)S(1)} %fusion.79), channel_id=1, source_target_pairs={} | collective-permute-start | bytes 663560 | tf_op jit(solution)/shard_map/ppermute | solution.py:535
  1017.2 15.2 %collective-permute-start.29 = (bf16[108,8,128]{2,1,0:T(8,128)(2,1)S(1)}, bf16[108,8,128]{2,1,0:T(8,128)(2,1)S(1)}, u32[]{:S(2)}, u32[]{:S(2)}) collective-permute-start(bf16[108,8,128]{2,1,0:T(8,128)(2,1)S(1)} %fusion.79), channel_id=1, source_target_pairs={{0,16},{2,18},{4,20},{6,22},{8,24},{10,26},{12,28},{14,30},{1,17},... | collective-permute-start | bytes 663560 | tf_op jit(solution)/shard_map/ppermute | solution.py:535
  1020.8 24.9 %collective-permute-start.23 = (bf16[108,8,128]{2,1,0:T(8,128)(2,1)S(1)}, bf16[108,8,128]{2,1,0:T(8,128)(2,1)S(1)}, u32[]{:S(2)}, u32[]{:S(2)}) collective-permute-start(bf16[108,8,128]{2,1,0:T(8,128)(2,1)S(1)} %fusion.78), channel_id=1, source_target_pairs={} | collective-permute-start | bytes 663560 | tf_op jit(solution)/shard_map/ppermute | solution.py:535
  1023.2 15.0 %collective-permute-start.22 = (bf16[108,8,128]{2,1,0:T(8,128)(2,1)S(1)}, bf16[108,8,128]{2,1,0:T(8,128)(2,1)S(1)}, u32[]{:S(2)}, u32[]{:S(2)}) collective-permute-start(bf16[108,8,128]{2,1,0:T(8,128)(2,1)S(1)} %fusion.78), channel_id=1, source_target_pairs={{0,16},{2,18},{4,20},{6,22},{8,24},{10,26},{12,28},{14,30},{1,17},... | collective-permute-start | bytes 663560 | tf_op jit(solution)/shard_map/ppermute | solution.py:535
  1032.3 14.2 %collective-permute-start.36 = (f32[54,8,128]{2,1,0:T(8,128)S(1)}, f32[54,8,128]{2,1,0:T(8,128)S(1)}, u32[]{:S(2)}, u32[]{:S(2)}) collective-permute-start(f32[54,8,128]{2,1,0:T(8,128)S(1)} %bitcast_add_fusion.22), channel_id=1, source_target_pairs={{0,8},{2,10},{4,12},{6,14},{8,16},{10,18},{12,20},{14,22},{16,24},... | collective-permute-start | bytes 663560 | tf_op jit(solution)/shard_map/ppermute | solution.py:535
  1038.1 10.7 collective-permute-start.45
  1046.6 14.1 %collective-permute-start.40 = (bf16[54,8,128]{2,1,0:T(8,128)(2,1)S(1)}, bf16[54,8,128]{2,1,0:T(8,128)(2,1)S(1)}, u32[]{:S(2)}, u32[]{:S(2)}) collective-permute-start(bf16[54,8,128]{2,1,0:T(8,128)(2,1)S(1)} %fusion.84), channel_id=1, source_target_pairs={{24,8},{26,10},{28,12},{30,14},{25,9},{27,11},{29,13},{31,15}} | collective-permute-start | bytes 331784 | tf_op jit(solution)/shard_map/ppermute | solution.py:535
  1047.3 12.7 %collective-permute-start.39 = (bf16[54,8,128]{2,1,0:T(8,128)(2,1)S(1)}, bf16[54,8,128]{2,1,0:T(8,128)(2,1)S(1)}, u32[]{:S(2)}, u32[]{:S(2)}) collective-permute-start(bf16[54,8,128]{2,1,0:T(8,128)(2,1)S(1)} %fusion.84), channel_id=1, source_target_pairs={{16,8},{18,10},{20,12},{22,14},{17,9},{19,11},{21,13},{23,15}} | collective-permute-start | bytes 331784 | tf_op jit(solution)/shard_map/ppermute | solution.py:535
  1047.9 11.3 collective-permute-start.38
  1048.8 9.7 collective-permute-start.37
  1058.5 60.9 %collective-permute-start.49 = (bf16[54,8,128]{2,1,0:T(8,128)(2,1)S(1)}, bf16[54,8,128]{2,1,0:T(8,128)(2,1)S(1)}, u32[]{:S(2)}, u32[]{:S(2)}) collective-permute-start(bf16[54,8,128]{2,1,0:T(8,128)(2,1)S(1)} %fusion.85), channel_id=1, source_target_pairs={{24,8},{26,10},{28,12},{30,14},{25,9},{27,11},{29,13},{31,15}} | collective-permute-start | bytes 331784 | tf_op jit(solution)/shard_map/ppermute | solution.py:535
  1059.2 40.5 %collective-permute-start.48 = (bf16[54,8,128]{2,1,0:T(8,128)(2,1)S(1)}, bf16[54,8,128]{2,1,0:T(8,128)(2,1)S(1)}, u32[]{:S(2)}, u32[]{:S(2)}) collective-permute-start(bf16[54,8,128]{2,1,0:T(8,128)(2,1)S(1)} %fusion.85), channel_id=1, source_target_pairs={{16,8},{18,10},{20,12},{22,14},{17,9},{19,11},{21,13},{23,15}} | collective-permute-start | bytes 331784 | tf_op jit(solution)/shard_map/ppermute | solution.py:535
  1059.9 8.6 collective-permute-start.47
  1097.1 18.9 %collective-permute-start.51 = (bf16[1,2,216,8,128]{4,3,2,1,0:T(8,128)(2,1)S(1)}, bf16[1,2,216,8,128]{4,3,2,1,0:T(8,128)(2,1)S(1)}, u32[]{:S(2)}, u32[]{:S(2)}) collective-permute-start(bf16[1,2,216,8,128]{4,3,2,1,0:T(8,128)(2,1)S(1)} %dynamic-slice_bitcast_fusion.3), channel_id=1, source_target_pairs={{0,4},{2,6},{4,0},{6,2},{8,12},{10,14},{12,8},{14,10},{16,20},{18,... | collective-permute-start | bytes 2654216 | tf_op jit(solution)/shard_map/ppermute | solution.py:535
  1097.9 19.9 %collective-permute-start.60 = (bf16[1,2,216,8,128]{4,3,2,1,0:T(8,128)(2,1)S(1)}, bf16[1,2,216,8,128]{4,3,2,1,0:T(8,128)(2,1)S(1)}, u32[]{:S(2)}, u32[]{:S(2)}) collective-permute-start(bf16[1,2,216,8,128]{4,3,2,1,0:T(8,128)(2,1)S(1)} %dynamic-slice_bitcast_fusion.2), channel_id=1, source_target_pairs={{0,2},{2,0},{4,6},{6,4},{8,10},{10,8},{12,14},{14,12},{16,18},{18,... | collective-permute-start | bytes 2654216 | tf_op jit(solution)/shard_map/ppermute | solution.py:535
  1101.1 18.4 %collective-permute-start.75 = (f32[24064]{0:T(1024)S(1)}, f32[24064]{0:T(1024)S(1)}, u32[]{:S(2)}, u32[]{:S(2)}) collective-permute-start(f32[24064]{0:T(1024)S(1)} %add.926), channel_id=1, source_target_pairs={{0,2},{2,0},{4,6},{6,4},{8,10},{10,8},{12,14},{14,12},{16,18},{18,... | collective-permute-start | bytes 288776 | tf_op jit(solution)/shard_map/ppermute | solution.py:356
  1116.3 8.4 collective-permute-start.52
  1118.0 9.2 collective-permute-start.61
  1119.5 67.7 %collective-permute-start.76 = (f32[24064]{0:T(1024)S(1)}, f32[24064]{0:T(1024)}, u32[]{:S(2)}, u32[]{:S(2)}) collective-permute-start(f32[24064]{0:T(1024)S(1)} %add.927), channel_id=1, source_target_pairs={{0,4},{2,6},{4,0},{6,2},{8,12},{10,14},{12,8},{14,10},{16,20},{18,... | collective-permute-start | bytes 288776 | tf_op jit(solution)/shard_map/ppermute | solution.py:356
  1124.7 10.1 collective-permute-start.53
  1127.3 12.0 collective-permute-start.62
  1134.9 9.3 collective-permute-start.54
  1139.4 14.2 %collective-permute-start.63 = (f32[54,8,128]{2,1,0:T(8,128)S(1)}, f32[54,8,128]{2,1,0:T(8,128)S(1)}, u32[]{:S(2)}, u32[]{:S(2)}) collective-permute-start(f32[54,8,128]{2,1,0:T(8,128)S(1)} %bitcast_add_fusion.14), channel_id=1, source_target_pairs={{8,0},{10,2},{12,4},{14,6},{16,8},{18,10},{20,12},{22,14},{24,16},... | collective-permute-start | bytes 663560 | tf_op jit(solution)/shard_map/ppermute | solution.py:535
  1144.3 9.4 collective-permute-start.55
  1153.6 9.9 collective-permute-start.64
  1153.7 14.5 %collective-permute-start.59 = (bf16[54,8,128]{2,1,0:T(8,128)(2,1)S(1)}, bf16[54,8,128]{2,1,0:T(8,128)(2,1)S(1)}, u32[]{:S(2)}, u32[]{:S(2)}) collective-permute-start(bf16[54,8,128]{2,1,0:T(8,128)(2,1)S(1)} %fusion.86), channel_id=1, source_target_pairs={{24,0},{26,2},{28,4},{30,6},{25,1},{27,3},{29,5},{31,7}} | collective-permute-start | bytes 331784 | tf_op jit(solution)/shard_map/ppermute | solution.py:535
  1155.0 11.8 collective-permute-start.58
  1156.3 9.2 collective-permute-start.57
  1164.1 10.9 collective-permute-start.68
  1165.5 9.5 collective-permute-start.67
  1166.8 8.1 collective-permute-start.66
  (233 other events, 2420.9 us)
Sparse Core Ops, SparseCore 0:
  13.6 169.5 all-gather.3
  186.6 61.5 all-gather.5
  251.6 165.8 all-gather.7
  801.1 140.7 reduce-scatter.1

commit v2 on v1

--- a/solution.py
+++ b/solution.py
@@ -200,7 +200,7 @@
     keep = jnp.where((lane >= lo) & (lane < hi), 1.0, 0.0).astype(x.dtype)
     return x * keep
 
-def attn_fwd_kernel(heads, e, T, TP, W, packed_ref, qa_ref, ka_ref, o_ref, lse_ref, q_s, k_s, v_s, o_s):
+def attn_fwd_kernel(heads, e, T, TP, W, packed_ref, qa_ref, ka_ref, o_ref, lse_ref, q_s, k_s, v_s, o_s, s_s, p_s):
     g = pl.program_id(0)
     base = pl.multiple_of(g * 128, 128)
     q_s[...] = pad_rows(packed_ref[:, pl.ds(base, 128)], TP)
@@ -209,29 +209,42 @@
     v_s[...] = pad_rows(packed_ref[:, pl.ds(base + 2 * W, 128)], TP)
     scale = e ** -0.5 * LOG2E
     lane = lax.broadcasted_iota(jnp.int32, (QB, 128), 1)
-
-    def block(i, _):
-        rows = pl.ds(pl.multiple_of(i * QB, QB), QB)
-        q = q_s[rows, :]
-        qa = qa_ref[rows, :]
-        out = jnp.zeros((QB, 128), jnp.float32)
-        stats = jnp.zeros((QB, 128), jnp.float32)
-        for h in range(heads):
-            qq = jnp.concatenate([lane_keep(q, h * e, (h + 1) * e), qa], 1)
-            s = dot_nt(qq, k_s[...]) * scale
+    step = 16
+    units = [(i, h) for i in range(TP // QB) for h in range(heads)]
+
+    def scores(n):
+        i, h = units[n]
+        rows = slice(i * QB, (i + 1) * QB)
+        qq = jnp.concatenate([lane_keep(q_s[rows, :], h * e, (h + 1) * e), qa_ref[rows, :]], 1)
+        s_s[n % 2] = dot_nt(qq, k_s[...])
+
+    scores(0)
+    for n, (i, h) in enumerate(units):
+        if n + 1 < len(units):
+            scores(n + 1)
+        rows = slice(i * QB, (i + 1) * QB)
+        peaks, totals = [], []
+        for r in range(0, QB, step):
+            s = s_s[n % 2, r : r + step, :] * scale
             peak = jnp.max(s, axis=1, keepdims=True)
             p = jnp.exp2(s - peak)
             total = jnp.sum(p, axis=1, keepdims=True)
-            p = (p * (1.0 / total)).astype(jnp.bfloat16)
-            o = dot_nn(p, v_s[...])
-            mine = (lane >= h * e) & (lane < (h + 1) * e)
-            out = jnp.where(mine, o, out)
-            stats = jnp.where(lane == h, peak + jnp.log2(total), stats)
-        o_s[rows, :] = out.astype(jnp.bfloat16)
-        lse_ref[0, :, rows] = stats.T[:8, :]
-        return 0
-
-    lax.fori_loop(0, TP // QB, block, 0)
+            p_s[n % 2, r : r + step, :] = (p * (1.0 / total)).astype(jnp.bfloat16)
+            peaks.append(peak)
+            totals.append(total)
+        o = dot_nn(p_s[n % 2], v_s[...])
+        stat = jnp.concatenate(peaks, 0) + jnp.log2(jnp.concatenate(totals, 0))
+        if h == 0:
+            out = o
+            stats = jnp.broadcast_to(stat, (QB, 128))
+        else:
+            out = jnp.where(lane < h * e, out, o)
+            stats = jnp.where(lane < h, stats, stat)
+        if h == heads - 1:
+            if heads * e < 128:
+                out = jnp.where(lane < heads * e, out, 0.0)
+            o_s[rows, :] = out.astype(jnp.bfloat16)
+            lse_ref[0, :, rows] = stats.T[:8, :]
     o_ref[...] = o_s[:T, :]
 
 def attn_fwd(packed, qa, ka, heads, e):
@@ -245,14 +258,15 @@
         in_specs=[pl.BlockSpec((T, W3), lambda g: (0, 0)), pl.BlockSpec((TP, 128), lambda g: (0, 0)), pl.BlockSpec((TP, 128), lambda g: (0, 0))],
         out_specs=[pl.BlockSpec((T, 128), lambda g: (0, g)), pl.BlockSpec((1, 8, TP), lambda g: (g, 0, 0))],
         out_shape=[jax.ShapeDtypeStruct((T, W), jnp.bfloat16), jax.ShapeDtypeStruct((groups, 8, TP), jnp.float32)],
-        scratch_shapes=[pltpu.VMEM((TP, 128), jnp.bfloat16), pltpu.VMEM((TP, 256), jnp.bfloat16), pltpu.VMEM((TP, 128), jnp.bfloat16), pltpu.VMEM((TP, 128), jnp.bfloat16)],
+        scratch_shapes=[pltpu.VMEM((TP, 128), jnp.bfloat16), pltpu.VMEM((TP, 256), jnp.bfloat16), pltpu.VMEM((TP, 128), jnp.bfloat16), pltpu.VMEM((TP, 128), jnp.bfloat16), pltpu.VMEM((2, QB, TP), jnp.float32), pltpu.VMEM((2, QB, TP), jnp.bfloat16)],
         compiler_params=pltpu.CompilerParams(vmem_limit_bytes=48 << 20),
         cost_estimate=pl.CostEstimate(flops=groups * heads * 4 * T * T * 256, bytes_accessed=T * W3 * 3, transcendentals=groups * heads * T * T),
         name="attn_fwd",
     )(packed, qa, ka)
 
-def attn_bwd_kernel(heads, e, T, TP, W, packed_ref, do_ref, qa_ref, ka_ref, lse_ref, d_ref, q_s, k_s, v_s, do_s, dk_s, dv_s, dq_s):
-    g = pl.program_id(0)
+def attn_bwd_kernel(heads, e, T, TP, W, first, chained, packed_ref, do_ref, qa_ref, ka_ref, lse_ref, *rest):
+    d_ref, q_s, k_s, v_s, do_s, dk_s, dv_s, dq_s, out_s, s_s, d_s, p_s, ds_s, sems = rest[1:] if chained else rest
+    g = pl.program_id(0) + first
     base = pl.multiple_of(g * 128, 128)
     q_s[:, :128] = pad_rows(packed_ref[:, pl.ds(base, 128)], TP)
     q_s[:, 128:] = qa_ref[...]
@@ -260,63 +274,91 @@
     k_s[...] = k
     v_s[...] = pad_rows(packed_ref[:, pl.ds(base + 2 * W, 128)], TP)
     do_s[...] = pad_rows(do_ref[...], TP)
-    dk_s[...] = jnp.zeros_like(dk_s)
-    dv_s[...] = jnp.zeros_like(dv_s)
     kt = k.astype(jnp.float32).T.astype(jnp.bfloat16)
     sub = lax.broadcasted_iota(jnp.int32, (128, 1), 0)
     lane = lax.broadcasted_iota(jnp.int32, (TP, 128), 1)
     scale2 = e ** -0.5 * LOG2E
     scale = e ** -0.5
-    for h in range(heads):
+    step = 64
+    blocks = TP // QB
+    units = [(h, i) for h in range(heads) for i in range(blocks)]
+
+    def products(n):
+        h, i = units[n]
+        rows = slice(i * QB, (i + 1) * QB)
         lo, hi = h * e, (h + 1) * e
         kk = jnp.concatenate([lane_keep(k_s[...], lo, hi), ka_ref[...]], 1)
-        vh = lane_keep(v_s[...], lo, hi)
-        kth = kt * jnp.where((sub >= lo) & (sub < hi), 1.0, 0.0).astype(jnp.bfloat16)
-
-        def block(i, carry):
-            rows = pl.ds(pl.multiple_of(i * QB, QB), QB)
-            qb = q_s[rows, :]
-            dob = do_s[rows, :]
-            st = dot_nt(kk, qb) * scale2
-            pt = jnp.exp2(st - lse_ref[0, h : h + 1, rows])
-            dpt = dot_nt(vh, dob)
-            d = jnp.sum(pt * dpt, axis=0, keepdims=True)
-            dst = (pt * (dpt - d)).astype(jnp.bfloat16)
-            dv = dot_nn(pt.astype(jnp.bfloat16), dob)
-            dk = dot_nn(dst, qb[:, :128])
-            dqt = dot_nn(kth, dst)
-            mine = (lane >= lo) & (lane < hi)
-            dv_s[...] += jnp.where(mine, dv, 0.0)
-            dk_s[...] += jnp.where(mine, dk, 0.0)
-            if h == 0:
-                dq_s[:, rows] = dqt
-            else:
-                dq_s[:, rows] += dqt
-            return 0
-
-        lax.fori_loop(0, TP // QB, block, 0)
+        s_s[n % 2] = dot_nt(kk, q_s[rows, :])
+        d_s[n % 2] = dot_nt(lane_keep(v_s[...], lo, hi), do_s[rows, :])
+
+    def gather(h):
+        lo, hi = h * e, (h + 1) * e
+        dv = dot_nn(p_s[h % 2], do_s[...])
+        dk = dot_nn(ds_s[h % 2], q_s[:, :128])
+        dq = dot_nn(kt * jnp.where((sub >= lo) & (sub < hi), 1.0, 0.0).astype(jnp.bfloat16), ds_s[h % 2])
+        if h == 0:
+            dv_s[...], dk_s[...], dq_s[...] = dv, dk, dq
+        else:
+            dv_s[...] = jnp.where(lane < lo, dv_s[...], dv)
+            dk_s[...] = jnp.where(lane < lo, dk_s[...], dk)
+            dq_s[...] += dq
+
+    products(0)
+    for n, (h, i) in enumerate(units):
+        if n + 1 < len(units):
+            products(n + 1)
+        rows = slice(i * QB, (i + 1) * QB)
+        lse = lse_ref[0, h : h + 1, rows]
+        d = jnp.zeros((8, QB), jnp.float32)
+        for r in range(0, TP, step):
+            part = slice(r, r + step)
+            pt = jnp.exp2(s_s[n % 2, part, :] * scale2 - lse)
+            s_s[n % 2, part, :] = pt
+            p_s[h % 2, part, rows] = pt.astype(jnp.bfloat16)
+            d += jnp.sum((pt * d_s[n % 2, part, :]).reshape(step // 8, 8, QB), axis=0)
+        d = jnp.sum(d, axis=0, keepdims=True)
+        for r in range(0, TP, step):
+            part = slice(r, r + step)
+            ds_s[h % 2, part, rows] = (s_s[n % 2, part, :] * (d_s[n % 2, part, :] - d)).astype(jnp.bfloat16)
+        if h and i == 0:
+            gather(h - 1)
+    gather(heads - 1)
+    if heads * e < 128:
+        dv_s[...] = jnp.where(lane < heads * e, dv_s[...], 0.0)
+        dk_s[...] = jnp.where(lane < heads * e, dk_s[...], 0.0)
     dq = dq_s[...].T * scale
-    d_ref[:, pl.ds(base, 128)] = dq.astype(jnp.bfloat16)[:T]
-    d_ref[:, pl.ds(base + W, 128)] = (dk_s[...] * scale).astype(jnp.bfloat16)[:T]
-    d_ref[:, pl.ds(base + 2 * W, 128)] = dv_s[...].astype(jnp.bfloat16)[:T]
-
-def attn_bwd(packed, do, qa, ka, lse, heads, e):
+    out_s[0] = dq.astype(jnp.bfloat16)[:T]
+    out_s[1] = (dk_s[...] * scale).astype(jnp.bfloat16)[:T]
+    out_s[2] = dv_s[...].astype(jnp.bfloat16)[:T]
+    copies = [
+        pltpu.make_async_copy(out_s.at[i], d_ref.at[:, pl.ds(base + i * W, 128)], sems.at[i])
+        for i in range(3)
+    ]
+    for copy in copies:
+        copy.start()
+    for copy in copies:
+        copy.wait()
+
+def attn_bwd(packed, do, qa, ka, lse, heads, e, first=0, groups=None, so_far=None):
     T, W3 = packed.shape
     W = W3 // 3
     TP = roundup(T, QB)
-    groups = W // 128
+    groups = W // 128 if groups is None else groups
+    chained = so_far is not None
     full = lambda g: (0, 0)
     return pl.pallas_call(
-        functools.partial(attn_bwd_kernel, heads, e, T, TP, W),
+        functools.partial(attn_bwd_kernel, heads, e, T, TP, W, first, chained),
         grid=(groups,),
-        in_specs=[pl.BlockSpec((T, W3), full), pl.BlockSpec((T, 128), lambda g: (0, g)), pl.BlockSpec((TP, 128), full), pl.BlockSpec((TP, 128), full), pl.BlockSpec((1, 8, TP), lambda g: (g, 0, 0))],
-        out_specs=pl.BlockSpec((T, W3), full),
+        in_specs=[pl.BlockSpec((T, W3), full), pl.BlockSpec((T, 128), lambda g: (0, g + first)), pl.BlockSpec((TP, 128), full), pl.BlockSpec((TP, 128), full), pl.BlockSpec((1, 8, TP), lambda g: (g + first, 0, 0))]
+        + ([pl.BlockSpec(memory_space=pl.ANY)] if chained else []),
+        out_specs=pl.BlockSpec(memory_space=pl.ANY),
+        input_output_aliases={5: 0} if chained else {},
         out_shape=jax.ShapeDtypeStruct((T, W3), jnp.bfloat16),
-        scratch_shapes=[pltpu.VMEM((TP, 256), jnp.bfloat16), pltpu.VMEM((TP, 128), jnp.bfloat16), pltpu.VMEM((TP, 128), jnp.bfloat16), pltpu.VMEM((TP, 128), jnp.bfloat16), pltpu.VMEM((TP, 128), jnp.float32), pltpu.VMEM((TP, 128), jnp.float32), pltpu.VMEM((128, TP), jnp.float32)],
+        scratch_shapes=[pltpu.VMEM((TP, 256), jnp.bfloat16), pltpu.VMEM((TP, 128), jnp.bfloat16), pltpu.VMEM((TP, 128), jnp.bfloat16), pltpu.VMEM((TP, 128), jnp.bfloat16), pltpu.VMEM((TP, 128), jnp.float32), pltpu.VMEM((TP, 128), jnp.float32), pltpu.VMEM((128, TP), jnp.float32), pltpu.VMEM((3, T, 128), jnp.bfloat16), pltpu.VMEM((2, TP, QB), jnp.float32), pltpu.VMEM((2, TP, QB), jnp.float32), pltpu.VMEM((2, TP, TP), jnp.bfloat16), pltpu.VMEM((2, TP, TP), jnp.bfloat16), pltpu.SemaphoreType.DMA((3,))],
         compiler_params=pltpu.CompilerParams(vmem_limit_bytes=48 << 20),
         cost_estimate=pl.CostEstimate(flops=groups * heads * 10 * T * T * 256, bytes_accessed=T * W3 * 5, transcendentals=groups * heads * T * T),
         name="attn_bwd",
-    )(packed, do, qa, ka, lse)
+    )(packed, do, qa, ka, lse, *([so_far] if chained else []))
 
 def mask_sides(segment, context_row, TP):
     T = segment.shape[0]
@@ -347,15 +389,28 @@
     return low.astype(jnp.float32) + swap(low).astype(jnp.float32)
 
 
-def doubling(x, axis):
+def doubling(x, axis, after=None):
     size = lax.axis_size(axis)
     if size & (size - 1):
         return lax.psum(x, axis)
-    bit = 1
-    while bit < size:
-        x = x + lax.ppermute(x, axis, [(i, i ^ bit) for i in range(size)])
-        bit *= 2
+    stride = 1
+    while stride < size:
+        reach = 4 if size // stride % 4 == 0 else 2
+        others = [
+            lax.ppermute(x, axis, [(i, i ^ (m * stride)) for i in range(size)])
+            for m in range(1, reach)
+        ]
+        if stride * reach >= size:
+            others = pin(others, after)
+        x = x + others[0]
+        if reach == 4:
+            x = x + (others[1] + others[2])
+        stride *= reach
     return x
+
+
+def pin(x, after):
+    return x if after is None else lax.optimization_barrier((x, after))[0]
 
 
 def tile_width(label):
@@ -418,11 +473,11 @@
             out_specs=pl.BlockSpec((48, 8, 128), lambda i, s: (i, 0, 0)),
         ),
         out_shape=jax.ShapeDtypeStruct((units * 48, 8, 128), jnp.bfloat16),
-        name="pack_tiles",
+        name="pack",
     )(place, flat)
 
 
-def unpack_kernel(spans, units, place_ref, x_ref, o_ref, sq_ref):
+def unpack_kernel(spans, units, place_ref, x_ref, o_ref):
     def emit(row, tile, width, groups):
         for t in range(groups):
             for j in range(width):
@@ -431,13 +486,6 @@
                 ].astype(jnp.float32)
 
     regions(place_ref[0] * units + pl.program_id(0), spans, emit)
-
-    @pl.when(pl.program_id(0) == 0)
-    def _():
-        sq_ref[...] = jnp.zeros_like(sq_ref)
-
-    values = o_ref[...]
-    sq_ref[...] += jnp.sum((values * values).reshape(48, 8, 128), axis=0)
 
 
 def unpack_tiles(tiles, place, spans):
@@ -448,16 +496,10 @@
             num_scalar_prefetch=1,
             grid=(units,),
             in_specs=[pl.BlockSpec((48, 8, 128), lambda i, s: (i, 0, 0))],
-            out_specs=[
-                pl.BlockSpec((384, 128), lambda i, s: (i, 0)),
-                pl.BlockSpec((8, 128), lambda i, s: (0, 0)),
-            ],
+            out_specs=pl.BlockSpec((384, 128), lambda i, s: (i, 0)),
         ),
-        out_shape=[
-            jax.ShapeDtypeStruct((units * 384, 128), jnp.float32),
-            jax.ShapeDtypeStruct((8, 128), jnp.float32),
-        ],
-        name="unpack_tiles",
+        out_shape=jax.ShapeDtypeStruct((units * 384, 128), jnp.float32),
+        name="unpack",
     )(place, tiles)
 
 
@@ -496,14 +538,11 @@
     )(scalars, *arrays)
 
 
-def from_tiles(full, ways):
+def from_tiles(parts, ways):
     result = {}
-    start = 0
-    for label, height, breadth in enc_shapes(ways):
-        count = height * breadth // 1024
-        piece = full[start : start + count].reshape(height // 8, breadth // 128, 8, 128)
+    for tiles, (label, height, breadth) in zip(parts, enc_shapes(ways)):
+        piece = tiles.reshape(height // 8, breadth // 128, 8, 128)
         result[label] = piece.transpose(0, 2, 1, 3).reshape(height, breadth)
-        start += count
     return result
 
 
@@ -520,8 +559,65 @@
     return lax.all_gather(x, "dp", axis=0, tiled=True)
 
 
+def split_gathered(gathered, sizes, part, first, total):
+    results = []
+    start = 0
+    for size in sizes:
+        moves = []
+        for device in range(gathered.shape[0] // total):
+            low, high = max(start, device * part), min(start + size, (device + 1) * part)
+            if low < high:
+                source = device * total + first + low - device * part
+                moves.append((0, source, low - start, high - low))
+        results.append(copy_tiles([gathered], moves, size, pltpu.HBM, 52))
+        start += size
+    return results
+
+
 def gather_flat(flat, shapes):
     return unflat(gather_dp(flat.astype(jnp.bfloat16)).reshape(-1), shapes)
+
+
+def flat_kernel(shapes, *refs):
+    ins, out, column = refs[:-2], refs[-2], refs[-1]
+
+    def by_turns(ref, first, width, height):
+        column[:height, :width] = ref[:, first : first + width]
+        pairs = height // 2
+        return column[pl.ds(0, pairs, stride=2), :], column[pl.ds(1, pairs, stride=2), :]
+
+    base = 0
+    for ref, (height, breadth) in zip(ins, shapes):
+        full = breadth // 128
+        if breadth % 128 == 0:
+            for j in range(full):
+                out[pl.ds(base + j, height, stride=full), :] = ref[:, j * 128 : (j + 1) * 128]
+        else:
+            pairs = height // 2
+            step = 2 * full + 1
+            even, odd = zip(*[by_turns(ref, j * 128, 128, height) for j in range(full)])
+            even_end, odd_end = [e[:, :64] for e in by_turns(ref, full * 128, 64, height)]
+            rows = list(even) + [jnp.concatenate([even_end, odd[0][:, :64]], 1)]
+            for j in range(full):
+                after = odd[j + 1][:, :64] if j + 1 < full else odd_end
+                rows.append(jnp.concatenate([odd[j][:, 64:], after], 1))
+            for j, row in enumerate(rows):
+                out[pl.ds(base + j, pairs, stride=step), :] = row
+        base += height * breadth // 128
+
+
+def flatten_matrices(matrices):
+    shapes = [m.shape for m in matrices]
+    total = sum(h * b for h, b in shapes) // 128
+    return pl.pallas_call(
+        functools.partial(flat_kernel, shapes),
+        in_specs=[pl.BlockSpec(memory_space=pltpu.VMEM)] * len(matrices),
+        out_specs=pl.BlockSpec(memory_space=pltpu.VMEM),
+        out_shape=jax.ShapeDtypeStruct((total, 128), jnp.float32),
+        scratch_shapes=[pltpu.VMEM((max(h for h, _ in shapes), 128), jnp.float32)],
+        compiler_params=pltpu.CompilerParams(vmem_limit_bytes=40 << 20),
+        name="flatten",
+    )(*matrices)
 
 
 def scatter_flat(grads, shapes, kind):
@@ -535,72 +631,104 @@
     return lax.ppermute(x, "dp", pairs)
 
 
-XOR_X = [(i, i ^ 1) for i in range(16)]
-XOR_Y = [(i, i ^ 2) for i in range(16)]
-RING_UP = [(i, (i + 4) % 16) for i in range(16)]
-RING_DOWN = [((i + 4) % 16, i) for i in range(16)]
+ENC_TILES = [(label, height * breadth // 1024) for label, height, breadth in enc_shapes(2)]
+
+
+def plus(a, b):
+    return a.astype(jnp.float32) + b.astype(jnp.float32)
 
 
 def pick(x, index, axis):
     return lax.dynamic_index_in_dim(x, index, axis, keepdims=False)
 
 
-def plus(a, b):
-    return a.astype(jnp.float32) + b.astype(jnp.float32)
+def stack_kernel(moves, count, *refs):
+    ins, out, sems = refs[:count], refs[count], refs[count + 1]
+    copies = [
+        pltpu.make_async_copy(
+            ins[source].at[pl.ds(first, length)], out.at[pl.ds(target, length)], sems.at[number]
+        )
+        for number, (source, first, target, length) in enumerate(moves)
+    ]
+    for copy in copies:
+        copy.start()
+    for copy in copies:
+        copy.wait()
+
+
+def copy_tiles(sources, moves, length, space=pl.ANY, room=24):
+    return pl.pallas_call(
+        functools.partial(stack_kernel, moves, len(sources)),
+        in_specs=[pl.BlockSpec(memory_space=space)] * len(sources),
+        out_specs=pl.BlockSpec(memory_space=pltpu.VMEM),
+        out_shape=jax.ShapeDtypeStruct((length, 8, 128), jnp.bfloat16),
+        scratch_shapes=[pltpu.SemaphoreType.DMA((len(moves),))],
+        compiler_params=pltpu.CompilerParams(vmem_limit_bytes=room << 20),
+        name="stack",
+    )(*sources)
+
+
+def stack_tiles(pieces, planes):
+    shard = sum(size for _, size in ENC_TILES) // 16
+    low, high = planes[0] * 4 * shard, (planes[-1] + 1) * 4 * shard
+    moves, used = [], []
+    start = 0
+    for label, size in ENC_TILES:
+        first, last = max(low, start), min(high, start + size)
+        if first < last:
+            moves.append((len(used), first - start, first - low, last - first))
+            used.append(pieces[label])
+        start += size
+    return copy_tiles(used, moves, high - low)
 
 
 def tree_scatter(tiles, planes):
     low = jnp.bfloat16
     place = lax.axis_index("dp")
-    z, y, x = place // 4, place // 2 % 2, place % 2
+    z, near = place // 4, place % 4
     count = len(planes)
     copies = 4 // count
-    tail = tiles.shape[1:]
-    part = tiles.shape[0] // (4 * count * 2 * copies)
-    grid = tiles.reshape((count, 2, 2, 2, copies * part) + tail)
-    halves = []
-    for side in range(2):
-        axis_one = 1 if side == 0 else 2
-        first_at, second_at = (y, x) if side == 0 else (x, y)
-        first_ring, second_ring = (XOR_Y, XOR_X) if side == 0 else (XOR_X, XOR_Y)
-        mine = grid[:, :, :, side]
-        sent = permute(pick(mine, 1 - first_at, axis_one), first_ring)
-        one = plus(pick(mine, first_at, axis_one), sent)
-        sent = permute(pick(one, 1 - second_at, 1).astype(low), second_ring)
-        two = plus(pick(one, second_at, 1), sent)
-        blocks = two.reshape((count, copies, part) + tail).swapaxes(0, 1)
-        blocks = blocks.reshape((4, part) + tail)
-        step = 1 if side == 0 else -1
-        ring = RING_UP if side == 0 else RING_DOWN
-        held = pick(blocks, (z - step) % 4, 0)
-        for s in range(1, 4):
-            held = permute(held, ring) + pick(blocks, (z - step * (s + 1)) % 4, 0)
-        pieces = []
-        for c in range(copies):
-            pairs = [
-                ((c * count + j) * 4 + i, planes[j] * 4 + i)
-                for j in range(count)
-                for i in range(4)
-                if c * count + j != planes[j]
-            ]
-            piece = permute(held.astype(low), pairs).astype(jnp.float32)
-            if len(pairs) < 4 * count:
-                stay = [planes[j] for j in range(count) if c * count + j == planes[j]]
-                here = functools.reduce(jnp.logical_or, [z == p for p in stay])
-                piece = jnp.where(here, held, piece)
-            pieces.append(piece)
-        halves.append(jnp.concatenate(pieces, 0))
-    return jnp.concatenate(halves, 0)
-
-
-def stack_tiles(pieces):
-    total = sum(p.shape[0] for p in pieces)
-    stacked = jnp.zeros((total,) + pieces[0].shape[1:], pieces[0].dtype)
-    start = 0
-    for piece in pieces:
-        stacked = lax.dynamic_update_slice_in_dim(stacked, piece, start, 0)
-        start += piece.shape[0]
-    return stacked
+    size = tiles.shape[0] // (4 * count * copies)
+    grid = tiles.reshape((count, 4, copies, size) + tiles.shape[1:])
+
+    def exchange(take, at, stride):
+        ready = [take(at ^ m) for m in range(1, 4)]
+        sent = [
+            permute(ready[m - 1], [(i, i ^ (m * stride)) for i in range(16)]) for m in range(1, 4)
+        ]
+        return ready, sent
+
+    ready, sent = exchange(lambda n: pick(grid, n, 1).astype(low), near, 1)
+    after = yield ready
+    sent = pin(sent, after)
+    plane_sum = sum(part.astype(jnp.float32) for part in [pick(grid, near, 1)] + sent)
+    blocks = plane_sum.swapaxes(0, 1).reshape((4, size) + tiles.shape[1:])
+    ready, sent = exchange(lambda n: pick(blocks, n, 0).astype(low), z, 4)
+    after = yield ready
+    sent = pin(sent, after)
+    held = sum(part.astype(jnp.float32) for part in [pick(blocks, z, 0)] + sent)
+    if copies == 1:
+        yield held
+    held = held.astype(low)
+    got = []
+    for c in range(copies):
+        pairs = [
+            ((c * count + j) * 4 + i, planes[j] * 4 + i)
+            for j in range(count)
+            for i in range(4)
+            if c * count + j != planes[j]
+        ]
+        stay = [planes[j] for j in range(count) if c * count + j == planes[j]]
+        piece = permute(held, pairs) if pairs else held
+        if pairs and stay:
+            piece = jnp.where(functools.reduce(jnp.logical_or, [z == p for p in stay]), held, piece)
+        got.append(piece)
+    after = yield [held]
+    yield jnp.concatenate(pin(got, after), 0)
+
+
+def advance(tree, after):
+    return tree.send(after)
 
 
 def group_pad(x, axis, e, per_group):
@@ -621,7 +749,9 @@
     return parts.reshape(shape[:axis] + (shape[axis] // 128 * used,) + shape[axis + 1 :])
 
 
-def layer_forward(stream, mats, vectors, tag, per_group, head_dim, sides, ways, member):
+def layer_forward(
+    stream, mats, vectors, tag, per_group, head_dim, sides, ways, member, watch=lambda value: None
+):
     normed_low = layer_norm(stream, vectors[tag + "ln1_g"], vectors[tag + "ln1_b"]).astype(
         jnp.bfloat16
     )
@@ -635,10 +765,11 @@
     normed_two = layer_norm(middle, vectors[tag + "ln2_g"], vectors[tag + "ln2_b"]).astype(
         jnp.bfloat16
     )
+    normed_two = pin(normed_two, watch(normed_two))
     hidden = matmul(normed_two, mats["w_" + tag + "up"]) + local_columns(
         vectors["b_" + tag + "up"], False, ways, member
     )
-    activated = jax.nn.gelu(hidden).astype(jnp.bfloat16)
+    activated = lax.optimization_barrier(jax.nn.gelu(hidden).astype(jnp.bfloat16))
     down_part = matmul(activated, mats["w_" + tag + "down"])
     result = middle + tensor_total(down_part) + vectors["b_" + tag + "down"]
     kept = (
@@ -655,7 +786,7 @@
     return (result, kept)
 
 
-def layer_backward(grad_out, kept, mats, vectors, tag, per_group, head_dim, sides):
+def layer_backward(grad_out, kept, mats, vectors, tag, per_group, head_dim, sides, watch):
     (
         stream,
         normed_low,
@@ -675,6 +806,7 @@
     grad_hidden = jax.vjp(jax.nn.gelu, hidden)[1](grad_act)[0].astype(jnp.bfloat16)
     grads["w_" + tag + "up"] = matmul_tn(normed_two, grad_hidden)
     grads["b_" + tag + "up"] = jnp.sum(grad_hidden.astype(jnp.float32), axis=0)
+    grad_hidden = pin(grad_hidden, watch(AT_HIDDEN, grads, grad_hidden))
     grad_normed = tensor_back(matmul_nt(grad_hidden, mats["w_" + tag + "up"]))
     grad_middle, grads[tag + "ln2_g"], grads[tag + "ln2_b"] = norm_backward(
         middle, vectors[tag + "ln2_g"], vectors[tag + "ln2_b"], grad_normed
@@ -686,16 +818,46 @@
     )
     grads["b_" + tag + "out"] = jnp.sum(grad_middle, axis=0)
     grad_mixed = matmul_nt(grad_mid_low, mats["w_" + tag + "out"]).astype(jnp.bfloat16)
-    grad_packed = attn_bwd(
-        packed, grad_mixed, sides[0], sides[1], log_totals, per_group, head_dim
-    )
+    groups = packed.shape[1] // 384
+    if tag:
+        grad_packed = attn_bwd(
+            packed, grad_mixed, sides[0], sides[1], log_totals, per_group, head_dim
+        )
+    else:
+        grad_packed = attn_bwd(
+            packed,
+            grad_mixed,
+            sides[0],
+            sides[1],
+            log_totals,
+            per_group,
+            head_dim,
+            groups=groups // 2,
+        )
+        grad_mixed = pin(grad_mixed, watch(AT_HALF, grads, grad_packed))
+        grad_packed = attn_bwd(
+            packed,
+            grad_mixed,
+            sides[0],
+            sides[1],
+            log_totals,
+            per_group,
+            head_dim,
+            first=groups // 2,
+            groups=groups // 2,
+            so_far=grad_packed,
+        )
     grads["w_" + tag + "qkv"] = group_cut(
         matmul_tn(normed_low, grad_packed), 1, head_dim, per_group
     )
     grads["b_" + tag + "qkv"] = group_cut(
         jnp.sum(grad_packed.astype(jnp.float32), axis=0), 0, head_dim, per_group
     )
-    grad_first = tensor_back(matmul_nt(grad_packed, mats["w_" + tag + "qkv"]))
+    grad_packed = pin(grad_packed, watch(AT_PACKED, grads, grad_packed))
+    first_part = matmul_nt(grad_packed, mats["w_" + tag + "qkv"]).astype(jnp.bfloat16)
+    first_part = pin(first_part, watch(AT_PART, grads, first_part))
+    grad_first = tensor_back(first_part)
+    grad_first = pin(grad_first, watch(AT_FIRST, grads, grad_first))
     grad_stream, grads[tag + "ln1_g"], grads[tag + "ln1_b"] = norm_backward(
         stream, vectors[tag + "ln1_g"], vectors[tag + "ln1_b"], grad_first
     )
@@ -711,6 +873,9 @@
     return (weight_new, first_new, second_new)
 
 
+UPPER, MIDDLE, LOWER = range(3)
+AT_HIDDEN, AT_HALF, AT_PACKED, AT_PART, AT_FIRST = range(5)
+SQUARE, LOSS = range(2)
 ENC_GROUP = 2
 PRED_GROUP = 3
 
@@ -741,15 +906,6 @@
     tiled = dp_count == 16 and enc_params.shape[1] % UNIT == 0 and all(
         a % 3 == 0 and b % 3 == 0 for a, b, w in spans if w == 12
     )
-    if tiled:
-        enc_tiles = gather_dp(pack_tiles(rows(enc_params), place, spans))
-        mats = from_tiles(enc_tiles, ways)
-        target_tiles = pack_tiles(rows(target_params), place, spans)
-    else:
-        mats = gather_flat(rows(enc_params), enc_shapes(ways))
-    mats.update(gather_flat(rows(pred_params), pred_shapes(ways)))
-    mats["w_pqkv"] = group_pad(mats["w_pqkv"], 1, PHEAD_DIM, PRED_GROUP)
-    mats["w_pout"] = group_pad(mats["w_pout"], 0, PHEAD_DIM, PRED_GROUP)
     vectors = split_vector(vecs, enc_vectors() + pred_vectors())
     target_vectors = split_vector(target_vecs, enc_vectors())
     places = positions(segment)
@@ -758,15 +914,46 @@
     online_sides = mask_sides(segment, context, padded)
     all_sides = mask_sides(segment, jnp.ones_like(context), padded)
     embed_pos = sincos(places, D)
-
+    pred_pos = sincos(places, PD)
+    if tiled:
+        pred_tiles = rows(pred_params).astype(jnp.bfloat16).reshape(-1, 8, 128)
+        own_tiles = jnp.concatenate([pack_tiles(rows(enc_params), place, spans), pred_tiles], 0)
+        enc_tiles = gather_dp(own_tiles)
+        target_tiles = pack_tiles(rows(target_params), place, spans)
+        enc_tiles, target_tiles, embed_pos, pred_pos, online_sides, all_sides = (
+            lax.optimization_barrier(
+                (enc_tiles, target_tiles, embed_pos, pred_pos, online_sides, all_sides)
+            )
+        )
+        sizes = [size for _, size in ENC_TILES]
+        shard, both = sum(sizes) // 16, own_tiles.shape[0]
+        mats = from_tiles(split_gathered(enc_tiles, sizes, shard, 0, both), ways)
+        pred_count = [16 * (both - shard)]
+        pred_whole = split_gathered(enc_tiles, pred_count, both - shard, shard, both)[0]
+    else:
+        mats = gather_flat(rows(enc_params), enc_shapes(ways))
     def embed(patch_rows, weight_set, vector_set):
         return (
             tensor_total(matmul(patch_rows, weight_set["w_patch"])) + vector_set["b_patch"] + embed_pos
         )
 
     online_mid, online_kept = layer_forward(
-        embed(patches, mats, vectors), mats, vectors, "", ENC_GROUP, HEAD_DIM, online_sides, ways, member
-    )
+        embed(patches, mats, vectors),
+        mats,
+        vectors,
+        "",
+        ENC_GROUP,
+        HEAD_DIM,
+        online_sides,
+        ways,
+        member,
+    )
+    if tiled:
+        mats.update(unflat(pred_whole.reshape(-1), pred_shapes(ways)))
+    else:
+        mats.update(gather_flat(rows(pred_params), pred_shapes(ways)))
+    mats["w_pqkv"] = group_pad(mats["w_pqkv"], 1, PHEAD_DIM, PRED_GROUP)
+    mats["w_pout"] = group_pad(mats["w_pout"], 0, PHEAD_DIM, PRED_GROUP)
     encoded_low = layer_norm(online_mid, vectors["lnf_g"], vectors["lnf_b"]).astype(jnp.bfloat16)
     pin_local = matmul(encoded_low, mats["w_pin"]) + local_columns(
         vectors["b_pin"], False, ways, member
@@ -777,18 +964,28 @@
         jnp.concatenate([pin_local, pin_other], 1),
         jnp.concatenate([pin_other, pin_local], 1),
     )
-    pred_in = jnp.where(context_mask[:, None], pin_full, vectors["mask_tok"][None, :]) + sincos(
-        places, PD
-    )
+    pred_in = jnp.where(context_mask[:, None], pin_full, vectors["mask_tok"][None, :])
+    pred_in = pred_in + pred_pos
+    if tiled:
+        target_whole = gather_dp(target_tiles)
     pred_mid, pred_kept = layer_forward(
-        pred_in, mats, vectors, "p", PRED_GROUP, PHEAD_DIM, all_sides, ways, member
+        pred_in,
+        mats,
+        vectors,
+        "p",
+        PRED_GROUP,
+        PHEAD_DIM,
+        all_sides,
+        ways,
+        member,
+        (lambda value: target_whole) if tiled else (lambda value: None),
     )
     pred_rows = layer_norm(pred_mid, vectors["plnf_g"], vectors["plnf_b"]).astype(jnp.bfloat16)
     predicted = matmul(pred_rows, mats["w_pproj"]) + local_columns(
         vectors["b_pproj"], False, ways, member
     )
     if tiled:
-        target_mats = from_tiles(gather_dp(target_tiles), ways)
+        target_mats = from_tiles(split_gathered(target_whole, sizes, shard, 0, shard), ways)
     else:
         target_mats = gather_flat(rows(target_params), enc_shapes(ways))
     target_patches, predicted = lax.optimization_barrier((patches, predicted))
@@ -838,7 +1035,7 @@
         pred_mid, vectors["plnf_g"], vectors["plnf_b"], grad_normed
     )
     grad_in, layer_grads = layer_backward(
-        grad_mid, pred_kept, mats, vectors, "p", PRED_GROUP, PHEAD_DIM, all_sides
+        grad_mid, pred_kept, mats, vectors, "p", PRED_GROUP, PHEAD_DIM, all_sides, lambda *_: None
     )
     grads.update(layer_grads)
     grads["mask_tok"] = jnp.sum(jnp.where(context_mask[:, None], 0.0, grad_in), axis=0)
@@ -852,47 +1049,104 @@
     grad_mid, grads["lnf_g"], grads["lnf_b"] = norm_backward(
         online_mid, vectors["lnf_g"], vectors["lnf_b"], grad_encoded
     )
-    pred_share = scatter_flat(grads, pred_shapes(ways), jnp.float32)
+    pred_flat = flatten_matrices([grads[label] for label, _, _ in pred_shapes(ways)])
+    pred_flat, grad_mid = lax.optimization_barrier((pred_flat, grad_mid))
+    pred_share = None
+    if tiled:
+        pred_tree = tree_scatter(pred_flat.reshape(-1, 8, 128), (0, 1, 2, 3))
+        next(pred_tree)
+    else:
+        pred_share = lax.psum_scatter(pred_flat, "dp", scatter_dimension=0, tiled=True)
+    sections = enc_vectors() + pred_vectors()
+    early = []
+    pred_shares = []
+
+    def shared_part(found, label, length):
+        if label in LOCAL_BIAS:
+            return place_columns(found[label], length, LOCAL_BIAS[label], ways, member)
+        return 0.5 * found[label]
+
+    def all_devices(parts, after=None):
+        total = doubling(doubling(jnp.concatenate(list(parts.values())), "tensor"), "dp", after)
+        result = {}
+        start = 0
+        for label, part in parts.items():
+            result[label] = total[start : start + part.shape[0]]
+            start += part.shape[0]
+        return result
+
+    def early_sum(found):
+        found = {**grads, **found}
+        parts = {
+            label: shared_part(found, label, length)
+            for label, length in sections
+            if label in found
+        }
+        parts[LOSS] = jnp.broadcast_to(local_loss, (128,))
+        return all_devices(parts)
+
+    pieces = {}
+    trees = {}
+
+    def watch(name, so_far, value):
+        if not tiled:
+            return None
+        for label, grad in so_far.items():
+            if label.startswith("w_") and label not in pieces:
+                pieces[label] = to_tiles(grad.astype(jnp.bfloat16))
+        if name == AT_HIDDEN:
+            pred_ready = advance(pred_tree, value)
+            trees[UPPER] = tree_scatter(stack_tiles(pieces, (2, 3)), (2, 3))
+            return (next(trees[UPPER]), pred_ready)
+        if name == AT_PACKED:
+            trees[MIDDLE] = tree_scatter(stack_tiles(pieces, (1,)), (1,))
+            return (advance(trees[UPPER], value), next(trees[MIDDLE]))
+        if name == AT_HALF:
+            pred_shares.append(advance(pred_tree, value).reshape(-1, 128))
+            early.append(early_sum(so_far))
+        return None
+
     grad_in, layer_grads = layer_backward(
-        grad_mid, online_kept, mats, vectors, "", ENC_GROUP, HEAD_DIM, online_sides
+        grad_mid, online_kept, mats, vectors, "", ENC_GROUP, HEAD_DIM, online_sides, watch
     )
     grads.update(layer_grads)
-    grads["w_patch"] = matmul_tn(patches, grad_in.astype(jnp.bfloat16))
+    grad_in_low = grad_in.astype(jnp.bfloat16)
+    grads["w_patch"] = matmul_tn(patches, grad_in_low)
     grads["b_patch"] = jnp.sum(grad_in, axis=0)
     if tiled:
-        pieces = {
-            label: to_tiles(grads[label].astype(jnp.bfloat16)) for label, _, _ in enc_shapes(ways)
-        }
-        groups = []
-        quarter = sum(p.shape[0] for p in pieces.values()) // 4
-        for planes in ((2, 3), (1,), (0,)):
-            low, high = planes[0] * quarter, (planes[-1] + 1) * quarter
-            chosen = []
-            start = 0
-            for label, _, _ in enc_shapes(ways):
-                end = start + pieces[label].shape[0]
-                if start < high and end > low:
-                    chosen.append(pieces[label][max(low - start, 0) : min(high, end) - start])
-                start = end
-            groups.append(tree_scatter(stack_tiles(chosen), planes))
+        pieces["w_patch"] = to_tiles(grads["w_patch"].astype(jnp.bfloat16))
+        trees[LOWER] = tree_scatter(stack_tiles(pieces, (0,)), (0,))
+        token = next(trees[LOWER])
+        token = [advance(trees[UPPER], token), advance(trees[MIDDLE], token)]
+        token = advance(trees[LOWER], token)
+        token = advance(trees[MIDDLE], token)
+        shares = {UPPER: advance(trees[UPPER], token)}
+        token = advance(trees[LOWER], token)
+        shares[MIDDLE] = advance(trees[MIDDLE], token)
+        shares[LOWER] = advance(trees[LOWER], token)
         share = jnp.where(
-            place[0] >= 8, groups[0], jnp.where(place[0] >= 4, groups[1], groups[2])
+            place[0] >= 8,
+            shares[UPPER],
+            jnp.where(place[0] >= 4, shares[MIDDLE], shares[LOWER]),
         )
-        enc_share, enc_square = unpack_tiles(share, place, spans)
+        enc_square = jnp.square(share.astype(jnp.float32))
+        enc_share = unpack_tiles(share, place, spans)
     else:
         enc_share = scatter_flat(grads, enc_shapes(ways), jnp.float32)
         enc_square = enc_share * enc_share
-    halves = []
-    for label, length in enc_vectors() + pred_vectors():
-        if label in LOCAL_BIAS:
-            halves.append(place_columns(grads[label], length, LOCAL_BIAS[label], ways, member))
-        else:
-            halves.append(0.5 * grads[label])
-    halves.append(jnp.broadcast_to(local_loss, (128,)))
-    vector_sum = doubling(doubling(jnp.concatenate(halves), "tensor"), "dp")
-    vector_grad, loss_value = vector_sum[: vecs.shape[0]], vector_sum[vecs.shape[0]]
+    if not early:
+        early.append(early_sum(grads))
+    sums = dict(early[0])
+    loss_value = sums.pop(LOSS)[0]
+    if tiled:
+        pred_share = pred_shares[0]
     square_sum = jnp.sum(enc_square) + jnp.sum(pred_share * pred_share)
-    square_total = doubling(doubling(jnp.broadcast_to(square_sum, (128,)), "tensor"), "dp")[0]
+    late = {label: shared_part(grads, label, length) for label, length in sections}
+    late = {label: part for label, part in late.items() if label not in sums}
+    late[SQUARE] = jnp.broadcast_to(square_sum, (128,))
+    sums.update(all_devices(late, enc_share))
+    square_total = sums.pop(SQUARE)[0]
+    vector_grad = jnp.concatenate([sums[label] for label, _ in sections])
     grad_norm = jnp.sqrt(square_total + jnp.sum(vector_grad * vector_grad))
     factor = jnp.minimum(1.0, CLIP / (grad_norm + 1e-06))
     count = step_count[0].astype(jnp.float32)

time: 1240 us -> 1030 us (0.83)
  waiting for transfers between devices: 406 us -> 293 us
  local copies, waits for them, and re-layouts: 140 us -> 106 us
  other arithmetic: 190 us -> 163 us
  starting transfers between devices: 94.1 us -> 67.9 us
  Pallas kernels: 226 us -> 204 us
    ppermute x50 -> x31, waiting for transfers between devices: 146 us -> 73.5 us  [permute(): return lax.ppermute(x, 'dp', pairs)]
    ppermute x50 -> x31, starting transfers between devices: 80.7 us -> 42.8 us  [permute(): return lax.ppermute(x, 'dp', pairs)]
    dynamic_update_slice x2 -> x0, other arithmetic: 35.9 us -> none  [stack_tiles(): stacked = lax.dynamic_update_slice_in_dim(stacked, piece, start, 0)]
    pallas_call x3, Pallas kernels: 99.5 us -> 66.7 us  [attn_fwd(): pl.pallas_call(functools.partial(attn_fwd_kernel, heads, e, T, TP, W), gr...]
    slice x21 -> x3, local copies, waits for them, and re-layouts: 26.5 us -> 1.03 us  [the longest x1 0.52 us: shards(): loss_value = sums.pop(LOSS)[0]]
    ppermute x14 -> x20, waiting for transfers between devices: 23.4 us -> 6.58 us  [doubling(): lax.ppermute(x, axis, [(i, i ^ m * stride) for i in range(size)])]
    all_gather x3 -> x2, waiting for transfers between devices: 206 us -> 192 us  [gather_dp(): return lax.all_gather(x, 'dp', axis=0, tiled=True)]
    pallas_call x2 -> x18, Pallas kernels: 100 us -> 111 us  [the longest x3 74.7 us: attn_bwd(): pl.pallas_call(functools.partial(attn_bwd_kernel, heads, e, T, TP, W, fir...]
  transfers between devices with their start and end apart: 83 -> 68, of which waited for: 44 -> 30; matrix products, arithmetic and copies ran while one was open for 21% -> 21% of each run, Pallas kernels for 11% -> 13%
where the time goes in v2:
time: 1030 us; the launch traced here: 1020 us
  waiting for transfers between devices  293 us (28%)
  Pallas kernels  204 us (20%)
  other arithmetic  163 us (16%)
  matrix products  162 us (16%)
  local copies, waits for them, and re-layouts  106 us (10%)
  starting transfers between devices  67.9 us (7%)
  between operations  24.2 us (2%)
    all_gather x2, waiting for transfers between devices, gather_dp(): return lax.all_gather(x, 'dp', axis=0, tiled=True)  192 us
    pallas_call x3, Pallas kernels, attn_bwd(): pl.pallas_call(functools.partial(attn_bwd_kernel, heads, e, T, TP, W, fir...  74.7 us
    ppermute x31, waiting for transfers between devices, permute(): return lax.ppermute(x, 'dp', pairs)  73.5 us
    dot_general x16, matrix products, matmul(): return jnp.dot(left, right, preferred_element_type=jnp.float32)  70.8 us
    pallas_call x3, Pallas kernels, attn_fwd(): pl.pallas_call(functools.partial(attn_fwd_kernel, heads, e, T, TP, W), gr...  66.7 us
    reduce_sum x13, other arithmetic, layer_norm(): centered = values - jnp.mean(values, axis=-1, keepdims=True)  55.2 us
    unnamed x416, local copies, waits for them, and re-layouts  49.5 us
    dot_general x11, matrix products, matmul_tn(): lax.dot_general(left, right, (((0,), (0,)), ((), ())), preferred_element_...  48.6 us
  transfers between devices with their start and end apart: 68, of which 30 were waited for; matrix products, arithmetic and copies ran while one was open for 21% of the time, Pallas kernels for 13%

profile of v2, /device:TPU:0, one launch (start us, length us, event | category | flops | bytes accessed | tf_op | source)
XLA Modules:
  0.0 1019.3 jit_solution(282469784194381531)
XLA Ops:
  9.2 6.0 pack.2
  17.5 6.0 pack.3
  31.0 8.6 multiply_sine_fusion
  42.3 169.1 %all-gather.3.cloned.1.call-done.refs_0_ = bf16[8160,8,128]{2,1,0:T(8,128)(2,1)} async-done(((bf16[510,8,128]{2,1,0:T(8,128)(2,1)}), bf16[8160,8,128]{2,1,0:T(8,128)(2,1)}) %all-gather.3.cloned.1.call-update) | async-done | bytes 16711696 | tf_op jit(solution)/shard_map/all_gather | solution.py:559
  212.8 4.3 convolution_bitcast_fusion
  219.6 4.0 stack.31
  225.5 6.3 fusion.148
  235.4 4.6 fusion.15.packed_ref
  240.1 24.5 %attn_fwd.3 = (bf16[1176,512]{1,0:T(8,128)(2,1)S(1)}, f32[4,8,1280]{2,1,0:T(8,128)S(1)}) custom-call(bf16[1176,1536]{1,0:T(8,128)(2,1)S(1)} %fusion.15.packed_ref, bf16[1280,128]{1,0:T(8,128)(2,1)S(1)} %copy-done.24, bf16[1280,128]{1,0:T(8,128)(2,1)S(1)} %get-tuple-element.82.ka_ref), custom_call_target="tpu_custom_call" | custom-call | flops 11329339392 | bytes 5419008 | tf_op jit(solution)/shard_map/attn_fwd/pallas_call | solution.py:255
  264.6 3.6 fusion.155
  268.3 4.4 stack.34
  272.7 4.2 stack.33
  276.9 5.1 fusion.147
  285.9 10.2 %multiply_convert_fusion = (bf16[1176,2048]{1,0:T(8,128)(2,1)S(1)}, f32[1176,2048]{1,0:T(8,128)}) fusion(f32[2048]{0:T(1024)S(1)} %dynamic_slice.133, bf16[1024,2048]{1,0:T(8,128)(2,1)S(1)} %bitcast.347, f32[1176,1024]{1,0:T(8,128)S(1)} %get-tuple-element.204, f32[1024]{0:T(1024)S(1)} %get-tuple-element.245, f32[1024]{0:T(1024)S(1)} %get-tuple-element.246, ...), kind=kOutput, calls=%fused_computation.19 | convolution fusion | flops 4962607104 | bytes 23487680 | tf_op jit(solution)/shard_map/dot_general | solution.py:144
  296.3 7.1 fusion.156
  304.5 3.6 stack.35
  311.8 6.0 fusion.146
  331.3 17.3 %attn_fwd.4 = (bf16[1176,256]{1,0:T(8,128)(2,1)S(1)}, f32[2,8,1280]{2,1,0:T(8,128)S(1)}) custom-call(bf16[1176,768]{1,0:T(8,128)(2,1)S(1)} %fusion.31.packed_ref, bf16[1280,128]{1,0:T(8,128)(2,1)S(1)} %copy-done.25, bf16[1280,128]{1,0:T(8,128)(2,1)S(1)} %get-tuple-element.86.ka_ref), custom_call_target="tpu_custom_call" | custom-call | flops 8497004544 | bytes 2709504 | tf_op jit(solution)/shard_map/attn_fwd/pallas_call | solution.py:255
  366.3 22.6 %all-gather.5.cloned.1.call-done.refs_0_ = bf16[6912,8,128]{2,1,0:T(8,128)(2,1)} async-done(((bf16[432,8,128]{2,1,0:T(8,128)(2,1)}), bf16[6912,8,128]{2,1,0:T(8,128)(2,1)}) %all-gather.5.cloned.1.call-update) | async-done | bytes 14155792 | tf_op jit(solution)/shard_map/all_gather | solution.py:559
  389.0 4.7 multiply_convert_fusion.1
  410.2 4.2 fusion.159
  416.4 3.7 stack.37
  422.9 4.6 fusion.141
  431.2 4.7 fusion.16.packed_ref
  435.9 24.9 %attn_fwd.5 = (bf16[1176,512]{1,0:T(8,128)(2,1)S(1)}, f32[4,8,1280]{2,1,0:T(8,128)}) custom-call(bf16[1176,1536]{1,0:T(8,128)(2,1)S(1)} %fusion.16.packed_ref, bf16[1280,128]{1,0:T(8,128)(2,1)S(1)} %copy-done.26, bf16[1280,128]{1,0:T(8,128)(2,1)S(1)} %copy-done.23), custom_call_target="tpu_custom_call" | custom-call | flops 11329339392 | bytes 5419008 | tf_op jit(solution)/shard_map/attn_fwd/pallas_call | solution.py:255
  460.8 3.7 fusion.160
  464.9 4.3 stack.40
  469.2 4.2 stack.39
  473.5 5.1 fusion.140
  482.5 8.8 fusion.14
  491.4 5.3 fusion.161
  497.7 7.1 collective-permute-done.8
  507.0 5.1 fusion.139
  535.9 4.7 fusion.132
  550.1 3.5 multiply_reduce_fusion.15
  556.5 4.2 convert_reduce_fusion.3
  576.7 29.5 %attn_bwd.3 = bf16[1176,768]{1,0:T(8,128)(2,1)S(1)} custom-call(bf16[1176,768]{1,0:T(8,128)(2,1)S(1)} %copy-done.32, bf16[1176,256]{1,0:T(8,128)(2,1)S(1)} %convolution_convert_fusion.10.do_ref, bf16[1280,128]{1,0:T(8,128)(2,1)S(1)} %copy-done.26, bf16[1280,128]{1,0:T(8,128)(2,1)S(1)} %copy-done.23, f32[2,8,1280]{2,1,0:T(8,128)S(1)} %copy-done.37), custom_call_target="tpu_custom_call" | custom-call | flops 21242511360 | bytes 4515840 | tf_op jit(solution)/shard_map/attn_bwd/pallas_call | solution.py:349
  625.7 3.6 fusion.77.refs_5_
  643.9 5.4 multiply_reduce_fusion
  649.4 4.3 fusion.136
  661.2 16.8 %convert_reduce_fusion = (f32[2048]{0:T(1024)S(1)}, bf16[1176,2048]{1,0:T(8,128)(2,1)}) fusion(f32[1176,2048]{1,0:T(8,128)} %get-tuple-element.281, bf16[2048,1024]{1,0:T(8,128)(2,1)} %bitcast.349, f32[1176,1024]{1,0:T(8,128)} %broadcast_add_fusion), kind=kOutput, calls=%fused_computation.18 | convolution fusion | flops 4986689536 | bytes 23470080 | tf_op jit(solution)/shard_map/dot_general | solution.py:154
  678.0 9.6 convolution_convert_fusion.4
  687.7 8.5 convolution_convert_fusion.3
  708.5 7.9 convolution_convert_fusion.2
  726.2 4.0 fusion.135
  735.7 22.7 %attn_bwd.4.rest_0_ = bf16[1176,1536]{1,0:T(8,128)(2,1)S(1)} custom-call(bf16[1176,1536]{1,0:T(8,128)(2,1)} %copy-done.33, bf16[1176,512]{1,0:T(8,128)(2,1)S(1)} %convolution_convert_fusion.6.do_ref, bf16[1280,128]{1,0:T(8,128)(2,1)S(1)} %copy-done.26, bf16[1280,128]{1,0:T(8,128)(2,1)S(1)} %copy-done.21, f32[4,8,1280]{2,1,0:T(8,128)S(1)} %copy-done.35), custom_call_target="tpu_custom_call" | custom-call | flops 14161674240 | bytes 9031680 | tf_op jit(solution)/shard_map/attn_bwd/pallas_call | solution.py:349
  760.1 22.5 %attn_bwd.5 = bf16[1176,1536]{1,0:T(8,128)(2,1)S(1)} custom-call(bf16[1176,1536]{1,0:T(8,128)(2,1)} %copy-done.33, bf16[1176,512]{1,0:T(8,128)(2,1)S(1)} %convolution_convert_fusion.6.do_ref, bf16[1280,128]{1,0:T(8,128)(2,1)S(1)} %copy-done.26, bf16[1280,128]{1,0:T(8,128)(2,1)S(1)} %copy-done.21, ...), custom_call_target="tpu_custom_call", output_to_operand_aliasing={{}: (5, {})} | custom-call | flops 14161674240 | bytes 9031680 | tf_op jit(solution)/shard_map/attn_bwd/pallas_call | solution.py:349
  782.6 5.3 convolution_convert_fusion.11
  788.0 8.6 convolution_convert_fusion
  809.6 5.4 convolution_convert_fusion.1
  830.6 5.4 multiply_reduce_fusion.2
  836.1 4.6 fusion.134
  842.9 3.9 fusion.56
  858.7 5.5 collective-permute-done.32
  877.3 10.4 %collective-permute-done.39 = bf16[1,4,108,8,128]{4,3,2,1,0:T(8,128)(2,1)S(1)} collective-permute-done((bf16[1,4,108,8,128]{4,3,2,1,0:T(8,128)(2,1)S(1)}, bf16[1,4,108,8,128]{4,3,2,1,0:T(8,128)(2,1)S(1)}, u32[]{:S(2)}, u32[]{:S(2)}) %collective-permute-start.39) | collective-permute-done | bytes 884768 | tf_op jit(solution)/shard_map/ppermute | solution.py:631
  890.0 15.6 %collective-permute-done.38 = bf16[1,4,108,8,128]{4,3,2,1,0:T(8,128)(2,1)S(1)} collective-permute-done((bf16[1,4,108,8,128]{4,3,2,1,0:T(8,128)(2,1)S(1)}, bf16[1,4,108,8,128]{4,3,2,1,0:T(8,128)(2,1)S(1)}, u32[]{:S(2)}, u32[]{:S(2)}) %collective-permute-start.38) | collective-permute-done | bytes 884768 | tf_op jit(solution)/shard_map/ppermute | solution.py:631
  911.2 8.3 collective-permute-done.35
  919.6 3.6 collective-permute-start.43
  927.2 12.8 %collective-permute-done.44 = bf16[108,8,128]{2,1,0:T(8,128)(2,1)S(1)} collective-permute-done((bf16[108,8,128]{2,1,0:T(8,128)(2,1)S(1)}, bf16[108,8,128]{2,1,0:T(8,128)(2,1)S(1)}, u32[]{:S(2)}, u32[]{:S(2)}) %collective-permute-start.44) | collective-permute-done | bytes 221216 | tf_op jit(solution)/shard_map/ppermute | solution.py:631
  948.3 3.6 collective-permute-done.48
  952.5 4.3 collective-permute-done.47
  979.8 6.0 unpack.1.g_ref
  1001.2 5.5 adam.2
  1006.7 4.2 convert_element_type.607
  (792 shorter events, 326.9 us)
Async XLA Ops:
  7.2 204.2 %all-gather.3.cloned.1.call-start = ((), (), s32[]{:S(2)}) async-start(), calls=%async_computation | async-start | bytes 17756160 | tf_op jit(solution)/shard_map/all_gather | solution.py:559
  17.5 371.5 %all-gather.5.cloned.1.call-start = ((), (), s32[]{:S(2)}) async-start(), calls=%async_computation.1 | async-start | bytes 15040512 | tf_op jit(solution)/shard_map/all_gather | solution.py:559
  217.1 8.4 collective-permute-start
  268.2 8.7 collective-permute-start.1
  303.4 8.5 collective-permute-start.2
  322.8 2.9 collective-permute-start.3
  351.2 7.1 collective-permute-start.4
  396.0 5.4 collective-permute-start.5
  414.4 8.5 collective-permute-start.6
  464.5 8.9 collective-permute-start.7
  496.6 8.1 collective-permute-start.8
  520.7 3.7 collective-permute-start.10
  522.3 4.5 collective-permute-start.11
  523.7 3.7 collective-permute-start.9
  527.3 5.5 collective-permute-start.14
  528.8 4.5 collective-permute-start.13
  529.0 4.4 collective-permute-start.12
  625.5 17.8 %collective-permute-start.18 = (bf16[1176,1024]{1,0:T(8,128)(2,1)}, bf16[1176,1024]{1,0:T(8,128)(2,1)}, u32[]{:S(2)}, u32[]{:S(2)}) collective-permute-start(bf16[1176,1024]{1,0:T(8,128)(2,1)} %convolution_convert_fusion.5), channel_id=1, source_target_pairs={{0,1},{1,0},{2,3},{3,2},{4,5},{5,4},{6,7},{7,6},{8,9},{9,8},{10,11... | collective-permute-start | bytes 7225352 | tf_op jit(solution)/shard_map/ppermute | solution.py:380
  657.7 46.8 %collective-permute-start.21 = (bf16[4,1,78,8,128]{4,3,2,1,0:T(8,128)(2,1)}, bf16[4,1,78,8,128]{4,3,2,1,0:T(8,128)(2,1)S(1)}, u32[]{:S(2)}, u32[]{:S(2)}) collective-permute-start(bf16[4,1,78,8,128]{4,3,2,1,0:T(8,128)(2,1)} %get-tuple-element.211), channel_id=1, source_target_pairs={{0,6},{2,4},{4,2},{6,0},{8,14},{10,12},{12,10},{14,8},{16,22},{18,... | collective-permute-start | bytes 1916936 | tf_op jit(solution)/shard_map/ppermute | solution.py:631
  659.2 45.3 %collective-permute-start.20 = (bf16[4,1,78,8,128]{4,3,2,1,0:T(8,128)(2,1)}, bf16[4,1,78,8,128]{4,3,2,1,0:T(8,128)(2,1)}, u32[]{:S(2)}, u32[]{:S(2)}) collective-permute-start(bf16[4,1,78,8,128]{4,3,2,1,0:T(8,128)(2,1)} %get-tuple-element.212), channel_id=1, source_target_pairs={{0,4},{2,6},{4,0},{6,2},{8,12},{10,14},{12,8},{14,10},{16,20},{18,... | collective-permute-start | bytes 1916936 | tf_op jit(solution)/shard_map/ppermute | solution.py:631
  659.7 45.6 %collective-permute-start.19 = (bf16[4,1,78,8,128]{4,3,2,1,0:T(8,128)(2,1)S(1)}, bf16[4,1,78,8,128]{4,3,2,1,0:T(8,128)(2,1)}, u32[]{:S(2)}, u32[]{:S(2)}) collective-permute-start(bf16[4,1,78,8,128]{4,3,2,1,0:T(8,128)(2,1)S(1)} %get-tuple-element.213), channel_id=1, source_target_pairs={{0,2},{2,0},{4,6},{6,4},{8,10},{10,8},{12,14},{14,12},{16,18},{18,... | collective-permute-start | bytes 1916936 | tf_op jit(solution)/shard_map/ppermute | solution.py:631
  716.5 5.7 collective-permute-start.22
  716.6 80.0 %collective-permute-start.23 = (bf16[2,2,216,8,128]{4,3,2,0,1:T(8,128)(2,1)}, bf16[2,2,216,8,128]{4,3,2,0,1:T(8,128)(2,1)}, u32[]{:S(2)}, u32[]{:S(2)}) collective-permute-start(bf16[2,2,216,8,128]{4,3,2,0,1:T(8,128)(2,1)} %bitcast.289), channel_id=1, source_target_pairs={{0,2},{2,0},{4,6},{6,4},{8,10},{10,8},{12,14},{14,12},{16,18},{18,... | collective-permute-start | bytes 5308424 | tf_op jit(solution)/shard_map/ppermute | solution.py:631
  717.2 79.3 %collective-permute-start.24 = (bf16[2,2,216,8,128]{4,3,2,0,1:T(8,128)(2,1)}, bf16[2,2,216,8,128]{4,3,2,0,1:T(8,128)(2,1)}, u32[]{:S(2)}, u32[]{:S(2)}) collective-permute-start(bf16[2,2,216,8,128]{4,3,2,0,1:T(8,128)(2,1)} %bitcast.288), channel_id=1, source_target_pairs={{0,4},{2,6},{4,0},{6,2},{8,12},{10,14},{12,8},{14,10},{16,20},{18,... | collective-permute-start | bytes 5308424 | tf_op jit(solution)/shard_map/ppermute | solution.py:631
  718.7 39.7 %collective-permute-start.51 = (bf16[78,8,128]{2,1,0:T(8,128)(2,1)}, bf16[78,8,128]{2,1,0:T(8,128)(2,1)S(1)}, u32[]{:S(2)}, u32[]{:S(2)}) collective-permute-start(bf16[78,8,128]{2,1,0:T(8,128)(2,1)} %get-tuple-element.238), channel_id=1, source_target_pairs={{0,24},{2,26},{4,28},{6,30},{8,16},{10,18},{12,20},{14,22},{16,8},... | collective-permute-start | bytes 479240 | tf_op jit(solution)/shard_map/ppermute | solution.py:631
  721.0 39.0 %collective-permute-start.50 = (bf16[78,8,128]{2,1,0:T(8,128)(2,1)}, bf16[78,8,128]{2,1,0:T(8,128)(2,1)S(1)}, u32[]{:S(2)}, u32[]{:S(2)}) collective-permute-start(bf16[78,8,128]{2,1,0:T(8,128)(2,1)} %get-tuple-element.239), channel_id=1, source_target_pairs={{0,16},{2,18},{4,20},{6,22},{8,24},{10,26},{12,28},{14,30},{16,0},... | collective-permute-start | bytes 479240 | tf_op jit(solution)/shard_map/ppermute | solution.py:631
  722.1 37.9 %collective-permute-start.49 = (bf16[78,8,128]{2,1,0:T(8,128)(2,1)S(1)}, bf16[78,8,128]{2,1,0:T(8,128)(2,1)S(1)}, u32[]{:S(2)}, u32[]{:S(2)}) collective-permute-start(bf16[78,8,128]{2,1,0:T(8,128)(2,1)S(1)} %get-tuple-element.240), channel_id=1, source_target_pairs={{0,8},{2,10},{4,12},{6,14},{8,0},{10,2},{12,4},{14,6},{16,24},{18,... | collective-permute-start | bytes 479240 | tf_op jit(solution)/shard_map/ppermute | solution.py:631
  758.5 41.4 %collective-permute-start.25 = (bf16[2,2,216,8,128]{4,3,2,0,1:T(8,128)(2,1)S(1)}, bf16[2,2,216,8,128]{4,3,2,0,1:T(8,128)(2,1)}, u32[]{:S(2)}, u32[]{:S(2)}) collective-permute-start(bf16[2,2,216,8,128]{4,3,2,0,1:T(8,128)(2,1)S(1)} %bitcast.357), channel_id=1, source_target_pairs={{0,6},{2,4},{4,2},{6,0},{8,14},{10,12},{12,10},{14,8},{16,22},{18,... | collective-permute-start | bytes 5308424 | tf_op jit(solution)/shard_map/ppermute | solution.py:631
  814.9 14.3 %collective-permute-start.26 = (bf16[1176,1024]{1,0:T(8,128)(2,1)}, bf16[1176,1024]{1,0:T(8,128)(2,1)}, u32[]{:S(2)}, u32[]{:S(2)}) collective-permute-start(bf16[1176,1024]{1,0:T(8,128)(2,1)} %convolution_convert_fusion.1), channel_id=1, source_target_pairs={{0,1},{1,0},{2,3},{3,2},{4,5},{5,4},{6,7},{7,6},{8,9},{9,8},{10,11... | collective-permute-start | bytes 7225352 | tf_op jit(solution)/shard_map/ppermute | solution.py:380
  820.7 45.9 %collective-permute-start.29 = (bf16[216,8,128]{2,1,0:T(8,128)(2,1)}, bf16[216,8,128]{2,1,0:T(8,128)(2,1)}, u32[]{:S(2)}, u32[]{:S(2)}) collective-permute-start(bf16[216,8,128]{2,1,0:T(8,128)(2,1)} %get-tuple-element.222), channel_id=1, source_target_pairs={{0,24},{2,26},{4,28},{6,30},{8,16},{10,18},{12,20},{14,22},{16,8},... | collective-permute-start | bytes 1327112 | tf_op jit(solution)/shard_map/ppermute | solution.py:631
  822.3 45.9 %collective-permute-start.28 = (bf16[216,8,128]{2,1,0:T(8,128)(2,1)}, bf16[216,8,128]{2,1,0:T(8,128)(2,1)}, u32[]{:S(2)}, u32[]{:S(2)}) collective-permute-start(bf16[216,8,128]{2,1,0:T(8,128)(2,1)} %get-tuple-element.223), channel_id=1, source_target_pairs={{0,16},{2,18},{4,20},{6,22},{8,24},{10,26},{12,28},{14,30},{16,0},... | collective-permute-start | bytes 1327112 | tf_op jit(solution)/shard_map/ppermute | solution.py:631
  822.5 33.3 %collective-permute-start.33 = (bf16[1,4,108,8,128]{4,3,2,1,0:T(8,128)(2,1)}, bf16[1,4,108,8,128]{4,3,2,1,0:T(8,128)(2,1)}, u32[]{:S(2)}, u32[]{:S(2)}) collective-permute-start(bf16[1,4,108,8,128]{4,3,2,1,0:T(8,128)(2,1)} %get-tuple-element.219), channel_id=1, source_target_pairs={{0,6},{2,4},{4,2},{6,0},{8,14},{10,12},{12,10},{14,8},{16,22},{18,... | collective-permute-start | bytes 2654216 | tf_op jit(solution)/shard_map/ppermute | solution.py:631
  824.0 40.2 %collective-permute-start.32 = (bf16[1,4,108,8,128]{4,3,2,1,0:T(8,128)(2,1)}, bf16[1,4,108,8,128]{4,3,2,1,0:T(8,128)(2,1)}, u32[]{:S(2)}, u32[]{:S(2)}) collective-permute-start(bf16[1,4,108,8,128]{4,3,2,1,0:T(8,128)(2,1)} %get-tuple-element.220), channel_id=1, source_target_pairs={{0,4},{2,6},{4,0},{6,2},{8,12},{10,14},{12,8},{14,10},{16,20},{18,... | collective-permute-start | bytes 2654216 | tf_op jit(solution)/shard_map/ppermute | solution.py:631
  829.2 36.5 %collective-permute-start.31 = (bf16[1,4,108,8,128]{4,3,2,1,0:T(8,128)(2,1)}, bf16[1,4,108,8,128]{4,3,2,1,0:T(8,128)(2,1)S(1)}, u32[]{:S(2)}, u32[]{:S(2)}) collective-permute-start(bf16[1,4,108,8,128]{4,3,2,1,0:T(8,128)(2,1)} %get-tuple-element.221), channel_id=1, source_target_pairs={{0,2},{2,0},{4,6},{6,4},{8,10},{10,8},{12,14},{14,12},{16,18},{18,... | collective-permute-start | bytes 2654216 | tf_op jit(solution)/shard_map/ppermute | solution.py:631
  856.1 15.1 %collective-permute-start.27 = (bf16[216,8,128]{2,1,0:T(8,128)(2,1)S(1)}, bf16[216,8,128]{2,1,0:T(8,128)(2,1)S(1)}, u32[]{:S(2)}, u32[]{:S(2)}) collective-permute-start(bf16[216,8,128]{2,1,0:T(8,128)(2,1)S(1)} %copy-done.94), channel_id=1, source_target_pairs={{0,8},{2,10},{4,12},{6,14},{8,0},{10,2},{12,4},{14,6},{16,24},{18,... | collective-permute-start | bytes 1327112 | tf_op jit(solution)/shard_map/ppermute | solution.py:631
  864.2 23.5 %collective-permute-start.39 = (bf16[1,4,108,8,128]{4,3,2,1,0:T(8,128)(2,1)S(1)}, bf16[1,4,108,8,128]{4,3,2,1,0:T(8,128)(2,1)S(1)}, u32[]{:S(2)}, u32[]{:S(2)}) collective-permute-start(bf16[1,4,108,8,128]{4,3,2,1,0:T(8,128)(2,1)S(1)} %get-tuple-element.216), channel_id=1, source_target_pairs={{0,6},{2,4},{4,2},{6,0},{8,14},{10,12},{12,10},{14,8},{16,22},{18,... | collective-permute-start | bytes 2654216 | tf_op jit(solution)/shard_map/ppermute | solution.py:631
  865.7 39.9 %collective-permute-start.38 = (bf16[1,4,108,8,128]{4,3,2,1,0:T(8,128)(2,1)S(1)}, bf16[1,4,108,8,128]{4,3,2,1,0:T(8,128)(2,1)S(1)}, u32[]{:S(2)}, u32[]{:S(2)}) collective-permute-start(bf16[1,4,108,8,128]{4,3,2,1,0:T(8,128)(2,1)S(1)} %get-tuple-element.217), channel_id=1, source_target_pairs={{0,4},{2,6},{4,0},{6,2},{8,12},{10,14},{12,8},{14,10},{16,20},{18,... | collective-permute-start | bytes 2654216 | tf_op jit(solution)/shard_map/ppermute | solution.py:631
  866.7 41.6 %collective-permute-start.37 = (bf16[1,4,108,8,128]{4,3,2,1,0:T(8,128)(2,1)S(1)}, bf16[1,4,108,8,128]{4,3,2,1,0:T(8,128)(2,1)S(1)}, u32[]{:S(2)}, u32[]{:S(2)}) collective-permute-start(bf16[1,4,108,8,128]{4,3,2,1,0:T(8,128)(2,1)S(1)} %get-tuple-element.218), channel_id=1, source_target_pairs={{0,2},{2,0},{4,6},{6,4},{8,10},{10,8},{12,14},{14,12},{16,18},{18,... | collective-permute-start | bytes 2654216 | tf_op jit(solution)/shard_map/ppermute | solution.py:631
  868.2 73.9 %collective-permute-start.59 = (f32[17920]{0:T(1024)S(1)}, f32[17920]{0:T(1024)S(1)}, u32[]{:S(2)}, u32[]{:S(2)}) collective-permute-start(f32[17920]{0:T(1024)S(1)} %constant_dynamic-update-slice_fusion.10), channel_id=1, source_target_pairs={{0,1},{1,0},{2,3},{3,2},{4,5},{5,4},{6,7},{7,6},{8,9},{9,8},{10,11... | collective-permute-start | bytes 215048 | tf_op jit(solution)/shard_map/ppermute | solution.py:400
  872.9 70.5 %collective-permute-start.30 = (bf16[216,8,128]{2,1,0:T(8,128)(2,1)S(1)}, bf16[216,8,128]{2,1,0:T(8,128)(2,1)S(1)}, u32[]{:S(2)}, u32[]{:S(2)}) collective-permute-start(bf16[216,8,128]{2,1,0:T(8,128)(2,1)S(1)} %fusion.70), channel_id=1, source_target_pairs={{0,16},{2,18},{4,20},{6,22},{8,24},{10,26},{12,28},{14,30},{1,17},... | collective-permute-start | bytes 1327112 | tf_op jit(solution)/shard_map/ppermute | solution.py:631
  887.7 21.4 %collective-permute-start.36 = (bf16[108,8,128]{2,1,0:T(8,128)(2,1)S(1)}, bf16[108,8,128]{2,1,0:T(8,128)(2,1)S(1)}, u32[]{:S(2)}, u32[]{:S(2)}) collective-permute-start(bf16[108,8,128]{2,1,0:T(8,128)(2,1)S(1)} %get-tuple-element.233), channel_id=1, source_target_pairs={{0,24},{2,26},{4,28},{6,30},{8,16},{10,18},{12,20},{14,22},{16,8},... | collective-permute-start | bytes 663560 | tf_op jit(solution)/shard_map/ppermute | solution.py:631
  905.7 13.9 %collective-permute-start.35 = (bf16[108,8,128]{2,1,0:T(8,128)(2,1)S(1)}, bf16[108,8,128]{2,1,0:T(8,128)(2,1)S(1)}, u32[]{:S(2)}, u32[]{:S(2)}) collective-permute-start(bf16[108,8,128]{2,1,0:T(8,128)(2,1)S(1)} %get-tuple-element.234), channel_id=1, source_target_pairs={{0,16},{2,18},{4,20},{6,22},{8,24},{10,26},{12,28},{14,30},{16,0},... | collective-permute-start | bytes 663560 | tf_op jit(solution)/shard_map/ppermute | solution.py:631
  908.3 11.3 %collective-permute-start.34 = (bf16[108,8,128]{2,1,0:T(8,128)(2,1)S(1)}, bf16[108,8,128]{2,1,0:T(8,128)(2,1)S(1)}, u32[]{:S(2)}, u32[]{:S(2)}) collective-permute-start(bf16[108,8,128]{2,1,0:T(8,128)(2,1)S(1)} %get-tuple-element.235), channel_id=1, source_target_pairs={{0,8},{2,10},{4,12},{6,14},{8,0},{10,2},{12,4},{14,6},{16,24},{18,... | collective-permute-start | bytes 663560 | tf_op jit(solution)/shard_map/ppermute | solution.py:631
  909.1 17.4 %collective-permute-start.45 = (bf16[108,8,128]{2,1,0:T(8,128)(2,1)S(1)}, bf16[108,8,128]{2,1,0:T(8,128)(2,1)S(1)}, u32[]{:S(2)}, u32[]{:S(2)}) collective-permute-start(bf16[108,8,128]{2,1,0:T(8,128)(2,1)S(1)} %get-tuple-element.230), channel_id=1, source_target_pairs={{0,24},{2,26},{4,28},{6,30},{8,16},{10,18},{12,20},{14,22},{16,8},... | collective-permute-start | bytes 663560 | tf_op jit(solution)/shard_map/ppermute | solution.py:631
  919.6 20.4 %collective-permute-start.44 = (bf16[108,8,128]{2,1,0:T(8,128)(2,1)S(1)}, bf16[108,8,128]{2,1,0:T(8,128)(2,1)S(1)}, u32[]{:S(2)}, u32[]{:S(2)}) collective-permute-start(bf16[108,8,128]{2,1,0:T(8,128)(2,1)S(1)} %get-tuple-element.231), channel_id=1, source_target_pairs={{0,16},{2,18},{4,20},{6,22},{8,24},{10,26},{12,28},{14,30},{16,0},... | collective-permute-start | bytes 663560 | tf_op jit(solution)/shard_map/ppermute | solution.py:631
  919.6 21.1 %collective-permute-start.43 = (bf16[108,8,128]{2,1,0:T(8,128)(2,1)S(1)}, bf16[108,8,128]{2,1,0:T(8,128)(2,1)S(1)}, u32[]{:S(2)}, u32[]{:S(2)}) collective-permute-start(bf16[108,8,128]{2,1,0:T(8,128)(2,1)S(1)} %get-tuple-element.232), channel_id=1, source_target_pairs={{0,8},{2,10},{4,12},{6,14},{8,0},{10,2},{12,4},{14,6},{16,24},{18,... | collective-permute-start | bytes 663560 | tf_op jit(solution)/shard_map/ppermute | solution.py:631
  926.5 18.2 %collective-permute-start.42 = (bf16[108,8,128]{2,1,0:T(8,128)(2,1)S(1)}, bf16[108,8,128]{2,1,0:T(8,128)(2,1)S(1)}, u32[]{:S(2)}, u32[]{:S(2)}) collective-permute-start(bf16[108,8,128]{2,1,0:T(8,128)(2,1)S(1)} %fusion.96), channel_id=1, source_target_pairs={{24,8},{26,10},{28,12},{30,14},{25,9},{27,11},{29,13},{31,15}} | collective-permute-start | bytes 663560 | tf_op jit(solution)/shard_map/ppermute | solution.py:631
  940.0 6.2 collective-permute-start.41
  940.7 7.1 collective-permute-start.40
  942.1 9.8 collective-permute-start.48
  943.4 13.4 %collective-permute-start.47 = (bf16[108,8,128]{2,1,0:T(8,128)(2,1)S(1)}, bf16[108,8,128]{2,1,0:T(8,128)(2,1)S(1)}, u32[]{:S(2)}, u32[]{:S(2)}) collective-permute-start(bf16[108,8,128]{2,1,0:T(8,128)(2,1)S(1)} %fusion.93), channel_id=1, source_target_pairs={{16,0},{18,2},{20,4},{22,6},{17,1},{19,3},{21,5},{23,7}} | collective-permute-start | bytes 663560 | tf_op jit(solution)/shard_map/ppermute | solution.py:631
  944.7 15.3 %collective-permute-start.46 = (bf16[108,8,128]{2,1,0:T(8,128)(2,1)S(1)}, bf16[108,8,128]{2,1,0:T(8,128)(2,1)S(1)}, u32[]{:S(2)}, u32[]{:S(2)}) collective-permute-start(bf16[108,8,128]{2,1,0:T(8,128)(2,1)S(1)} %fusion.93), channel_id=1, source_target_pairs={{8,0},{10,2},{12,4},{14,6},{9,1},{11,3},{13,5},{15,7}} | collective-permute-start | bytes 663560 | tf_op jit(solution)/shard_map/ppermute | solution.py:631
  946.2 21.4 %collective-permute-start.62 = (f32[17920]{0:T(1024)S(1)}, f32[17920]{0:T(1024)}, u32[]{:S(2)}, u32[]{:S(2)}) collective-permute-start(f32[17920]{0:T(1024)S(1)} %add.826), channel_id=1, source_target_pairs={{0,6},{2,4},{4,2},{6,0},{8,14},{10,12},{12,10},{14,8},{16,22},{18,... | collective-permute-start | bytes 215048 | tf_op jit(solution)/shard_map/ppermute | solution.py:400
  947.7 21.3 %collective-permute-start.61 = (f32[17920]{0:T(1024)S(1)}, f32[17920]{0:T(1024)}, u32[]{:S(2)}, u32[]{:S(2)}) collective-permute-start(f32[17920]{0:T(1024)S(1)} %add.826), channel_id=1, source_target_pairs={{0,4},{2,6},{4,0},{6,2},{8,12},{10,14},{12,8},{14,10},{16,20},{18,... | collective-permute-start | bytes 215048 | tf_op jit(solution)/shard_map/ppermute | solution.py:400
  951.9 17.1 %collective-permute-start.60 = (f32[17920]{0:T(1024)S(1)}, f32[17920]{0:T(1024)}, u32[]{:S(2)}, u32[]{:S(2)}) collective-permute-start(f32[17920]{0:T(1024)S(1)} %add.826), channel_id=1, source_target_pairs={{0,2},{2,0},{4,6},{6,4},{8,10},{10,8},{12,14},{14,12},{16,18},{18,... | collective-permute-start | bytes 215048 | tf_op jit(solution)/shard_map/ppermute | solution.py:400
  965.5 5.6 collective-permute-start.55
  967.0 7.4 collective-permute-start.54
  967.6 6.9 collective-permute-start.53
  970.0 7.0 collective-permute-start.65
  970.0 9.2 collective-permute-start.64
  971.0 8.2 collective-permute-start.63
  974.4 11.3 %collective-permute-start.58 = (f32[6272]{0:T(1024)S(1)}, f32[6272]{0:T(1024)}, u32[]{:S(2)}, u32[]{:S(2)}) collective-permute-start(f32[6272]{0:T(1024)S(1)} %add_add_fusion.22), channel_id=1, source_target_pairs={{0,24},{2,26},{4,28},{6,30},{8,16},{10,18},{12,20},{14,22},{16,8},... | collective-permute-start | bytes 75272 | tf_op jit(solution)/shard_map/ppermute | solution.py:400
  974.6 11.2 %collective-permute-start.57 = (f32[6272]{0:T(1024)S(1)}, f32[6272]{0:T(1024)}, u32[]{:S(2)}, u32[]{:S(2)}) collective-permute-start(f32[6272]{0:T(1024)S(1)} %add_add_fusion.22), channel_id=1, source_target_pairs={{0,16},{2,18},{4,20},{6,22},{8,24},{10,26},{12,28},{14,30},{16,0},... | collective-permute-start | bytes 75272 | tf_op jit(solution)/shard_map/ppermute | solution.py:400
  977.0 8.8 collective-permute-start.56
  (214 other events, 3057.7 us)
Sparse Core Ops, SparseCore 0:
  17.6 193.7 all-gather.2
  223.7 165.1 all-gather.4

commit v3 on v2

--- a/solution.py
+++ b/solution.py
@@ -229,11 +229,12 @@
             peak = jnp.max(s, axis=1, keepdims=True)
             p = jnp.exp2(s - peak)
             total = jnp.sum(p, axis=1, keepdims=True)
-            p_s[n % 2, r : r + step, :] = (p * (1.0 / total)).astype(jnp.bfloat16)
+            p_s[n % 2, r : r + step, :] = p.astype(jnp.bfloat16)
             peaks.append(peak)
             totals.append(total)
-        o = dot_nn(p_s[n % 2], v_s[...])
-        stat = jnp.concatenate(peaks, 0) + jnp.log2(jnp.concatenate(totals, 0))
+        total = jnp.concatenate(totals, 0)
+        o = dot_nn(p_s[n % 2], v_s[...]) * (1.0 / total)
+        stat = jnp.concatenate(peaks, 0) + jnp.log2(total)
         if h == 0:
             out = o
             stats = jnp.broadcast_to(stat, (QB, 128))
@@ -559,6 +560,45 @@
     return lax.all_gather(x, "dp", axis=0, tiled=True)
 
 
+def tree_gather(tiles):
+    place = lax.axis_index("dp")
+    z, y, x = place // 4, place // 2 % 2, place % 2
+    half = tiles.shape[0] // 2
+    over_x, over_y = ([(i, i ^ bit) for i in range(16)] for bit in (1, 2))
+    ring_up = [(i, (i + 4) % 16) for i in range(16)]
+    ring_down = [(j, i) for i, j in ring_up]
+    a, b = tiles[:half], tiles[half:]
+    arrived = []
+    waits = None
+    for k in range(4):
+        ax, by = permute(a, over_x), permute(b, over_y)
+        ay, bx = permute(a, over_y), permute(b, over_x)
+        axy, byx = permute(ax, over_y), permute(by, over_x)
+        za, zb = (z - k) % 4, (z + k) % 4
+        arrived.append([(0, za, y, x, a), (1, zb, y, x, b)])
+        arrived.append([(0, za, y, 1 - x, ax), (1, zb, 1 - y, x, by)])
+        arrived.append([(0, za, 1 - y, x, ay), (1, zb, y, 1 - x, bx)])
+        arrived.append([(0, za, 1 - y, 1 - x, axy), (1, zb, 1 - y, 1 - x, byx)])
+        if k == 1:
+            begun = (a, b)
+        if k == 2:
+            first = (ax, by, ay, bx) + last
+        if k == 3:
+            first = first + (a, b)
+        last = (axy, byx)
+        a, b = pin((a, b), waits)
+        waits = (ax, by, ay, bx) if k == 0 else (ax, by, ay, bx, axy, byx)
+        if k < 3:
+            a, b = permute(a, ring_up), permute(b, ring_down)
+    zero = pin(jnp.zeros((), tiles.dtype), first)
+    whole = jnp.broadcast_to(zero, (32, half) + tiles.shape[1:])
+    for n in sorted(range(16), key=lambda n: (n // 4 * 2 + n % 4, n)):
+        for side, pz, py, px, piece in arrived[n]:
+            slot = (pz * 4 + py * 2 + px) * 2 + side
+            whole = lax.dynamic_update_index_in_dim(whole, piece, slot, 0)
+    return whole.reshape((32 * half,) + tiles.shape[1:]), begun
+
+
 def split_gathered(gathered, sizes, part, first, total):
     results = []
     start = 0
@@ -786,6 +826,13 @@
     return (result, kept)
 
 
+def gelu_slope(x):
+    scale, cubic = math.sqrt(2 / math.pi), 0.044715
+    square = x * x
+    bend = jnp.tanh(scale * x * (1 + cubic * square))
+    return 0.5 * (1 + bend) + (0.5 * scale) * x * (1 - bend * bend) * (1 + 3 * cubic * square)
+
+
 def layer_backward(grad_out, kept, mats, vectors, tag, per_group, head_dim, sides, watch):
     (
         stream,
@@ -803,7 +850,7 @@
     grads["w_" + tag + "down"] = matmul_tn(activated, grad_low)
     grads["b_" + tag + "down"] = jnp.sum(grad_out, axis=0)
     grad_act = matmul_nt(grad_low, mats["w_" + tag + "down"])
-    grad_hidden = jax.vjp(jax.nn.gelu, hidden)[1](grad_act)[0].astype(jnp.bfloat16)
+    grad_hidden = (grad_act * gelu_slope(hidden)).astype(jnp.bfloat16)
     grads["w_" + tag + "up"] = matmul_tn(normed_two, grad_hidden)
     grads["b_" + tag + "up"] = jnp.sum(grad_hidden.astype(jnp.float32), axis=0)
     grad_hidden = pin(grad_hidden, watch(AT_HIDDEN, grads, grad_hidden))
@@ -908,6 +955,12 @@
     )
     vectors = split_vector(vecs, enc_vectors() + pred_vectors())
     target_vectors = split_vector(target_vecs, enc_vectors())
+    begun = None
+    if tiled:
+        pred_tiles = rows(pred_params).astype(jnp.bfloat16).reshape(-1, 8, 128)
+        own_tiles = jnp.concatenate([pack_tiles(rows(enc_params), place, spans), pred_tiles], 0)
+        enc_tiles, begun = tree_gather(own_tiles)
+    segment, target_local = pin((segment, target_params), begun)
     places = positions(segment)
     context_mask = context > 0
     padded = roundup(segment.shape[0], QB)
@@ -916,10 +969,7 @@
     embed_pos = sincos(places, D)
     pred_pos = sincos(places, PD)
     if tiled:
-        pred_tiles = rows(pred_params).astype(jnp.bfloat16).reshape(-1, 8, 128)
-        own_tiles = jnp.concatenate([pack_tiles(rows(enc_params), place, spans), pred_tiles], 0)
-        enc_tiles = gather_dp(own_tiles)
-        target_tiles = pack_tiles(rows(target_params), place, spans)
+        target_tiles = pack_tiles(rows(target_local), place, spans)
         enc_tiles, target_tiles, embed_pos, pred_pos, online_sides, all_sides = (
             lax.optimization_barrier(
                 (enc_tiles, target_tiles, embed_pos, pred_pos, online_sides, all_sides)

time: 1030 us -> 999 us (0.970)
  waiting for transfers between devices: 293 us -> 207 us
  starting transfers between devices: 67.9 us -> 105 us
  local copies, waits for them, and re-layouts: 106 us -> 128 us
    all_gather x2 -> x1, waiting for transfers between devices: 192 us -> 25.5 us  [gather_dp(): return lax.all_gather(x, 'dp', axis=0, tiled=True)]
    ppermute x31 -> x61, waiting for transfers between devices: 73.5 us -> 153 us  [permute(): return lax.ppermute(x, 'dp', pairs)]
    ppermute x31 -> x61, starting transfers between devices: 42.8 us -> 79.9 us  [permute(): return lax.ppermute(x, 'dp', pairs)]
    dynamic_update_slice x0 -> x32, local copies, waits for them, and re-layouts: none -> 14 us  [tree_gather(): whole = lax.dynamic_update_index_in_dim(whole, piece, slot, 0)]
    unnamed x416 -> x460, local copies, waits for them, and re-layouts: 49.5 us -> 54.6 us
  transfers between devices with their start and end apart: 68 -> 97, of which waited for: 30 -> 41; matrix products, arithmetic and copies ran while one was open for 21% -> 24% of each run, Pallas kernels for 13% -> 13%
where the time goes in v3:
time: 999 us; the launch traced here: 989 us
  waiting for transfers between devices  207 us (21%)
  Pallas kernels  199 us (20%)
  other arithmetic  165 us (17%)
  matrix products  160 us (16%)
  local copies, waits for them, and re-layouts  128 us (13%)
  starting transfers between devices  105 us (11%)
  between operations  24.7 us (2%)
    ppermute x61, waiting for transfers between devices, permute(): return lax.ppermute(x, 'dp', pairs)  153 us
    ppermute x61, starting transfers between devices, permute(): return lax.ppermute(x, 'dp', pairs)  79.9 us
    pallas_call x3, Pallas kernels, attn_bwd(): pl.pallas_call(functools.partial(attn_bwd_kernel, heads, e, T, TP, W, fir...  74.7 us
    dot_general x16, matrix products, matmul(): return jnp.dot(left, right, preferred_element_type=jnp.float32)  70.9 us
    pallas_call x3, Pallas kernels, attn_fwd(): pl.pallas_call(functools.partial(attn_fwd_kernel, heads, e, T, TP, W), gr...  62.4 us
    reduce_sum x13, other arithmetic, layer_norm(): centered = values - jnp.mean(values, axis=-1, keepdims=True)  55.2 us
    unnamed x460, local copies, waits for them, and re-layouts  54.6 us
    dot_general x11, matrix products, matmul_tn(): lax.dot_general(left, right, (((0,), (0,)), ((), ())), preferred_element_...  48.6 us
  transfers between devices with their start and end apart: 97, of which 41 were waited for; matrix products, arithmetic and copies ran while one was open for 24% of the time, Pallas kernels for 13%

profile of v3, /device:TPU:0, one launch (start us, length us, event | category | flops | bytes accessed | tf_op | source)
XLA Modules:
  0.0 988.9 jit_solution(11026090759502100)
XLA Ops:
  9.2 6.0 pack.2
  23.4 10.1 %collective-permute-done = bf16[255,8,128]{2,1,0:T(8,128)(2,1)} collective-permute-done((bf16[255,8,128]{2,1,0:T(8,128)(2,1)S(1)}, bf16[255,8,128]{2,1,0:T(8,128)(2,1)}, u32[]{:S(2)}, u32[]{:S(2)}) %collective-permute-start) | collective-permute-done | bytes 522272 | tf_op jit(solution)/shard_map/ppermute | solution.py:671
  35.3 11.3 %collective-permute-done.1 = bf16[255,8,128]{2,1,0:T(8,128)(2,1)S(1)} collective-permute-done((bf16[255,8,128]{2,1,0:T(8,128)(2,1)S(1)}, bf16[255,8,128]{2,1,0:T(8,128)(2,1)S(1)}, u32[]{:S(2)}, u32[]{:S(2)}) %collective-permute-start.1) | collective-permute-done | bytes 522272 | tf_op jit(solution)/shard_map/ppermute | solution.py:671
  51.3 9.8 multiply_sine_fusion
  67.9 8.2 collective-permute-done.16
  79.5 7.8 collective-permute-done.14
  93.1 5.4 collective-permute-done.13
  102.2 7.6 collective-permute-done.10
  111.5 6.3 pack.3
  118.5 5.2 pad_maximum_fusion
  151.5 8.2 collective-permute-done.24
  160.4 9.5 collective-permute-done.25
  171.5 4.0 collective-permute-done.28
  179.1 5.8 copy-done.38
  186.3 4.2 convolution_bitcast_fusion
  193.0 4.0 stack.31
  198.9 6.1 fusion.163
  208.7 4.6 fusion.24.packed_ref
  213.4 22.7 %attn_fwd.3 = (bf16[1176,512]{1,0:T(8,128)(2,1)S(1)}, f32[4,8,1280]{2,1,0:T(8,128)S(1)}) custom-call(bf16[1176,1536]{1,0:T(8,128)(2,1)S(1)} %fusion.24.packed_ref, bf16[1280,128]{1,0:T(8,128)(2,1)S(1)} %copy-done.24, bf16[1280,128]{1,0:T(8,128)(2,1)S(1)} %get-tuple-element.96.ka_ref), custom_call_target="tpu_custom_call" | custom-call | flops 11329339392 | bytes 5419008 | tf_op jit(solution)/shard_map/attn_fwd/pallas_call | solution.py:256
  239.8 4.4 stack.34
  244.2 4.3 stack.33
  248.5 5.1 fusion.162
  257.6 10.2 %fusion.7 = (bf16[1176,2048]{1,0:T(8,128)(2,1)S(1)}, f32[1176,2048]{1,0:T(8,128)}) fusion(f32[2048]{0:T(1024)S(1)} %dynamic_slice.133, bf16[1024,2048]{1,0:T(8,128)(2,1)S(1)} %bitcast.419, f32[1176,1024]{1,0:T(8,128)S(1)} %get-tuple-element.218, f32[1024]{0:T(1024)S(1)} %get-tuple-element.261, f32[1024]{0:T(1024)S(1)} %get-tuple-element.262, ...), kind=kOutput, calls=%fused_computation.11 | convolution fusion | flops 4962607104 | bytes 23487680 | tf_op jit(solution)/shard_map/dot_general | solution.py:144
  267.8 7.1 fusion.171
  283.3 6.0 fusion.161
  302.9 16.8 %attn_fwd.4 = (bf16[1176,256]{1,0:T(8,128)(2,1)S(1)}, f32[2,8,1280]{2,1,0:T(8,128)S(1)}) custom-call(bf16[1176,768]{1,0:T(8,128)(2,1)S(1)} %fusion.47.packed_ref, bf16[1280,128]{1,0:T(8,128)(2,1)S(1)} %copy-done.25, bf16[1280,128]{1,0:T(8,128)(2,1)S(1)} %get-tuple-element.100.ka_ref), custom_call_target="tpu_custom_call" | custom-call | flops 8497004544 | bytes 2709504 | tf_op jit(solution)/shard_map/attn_fwd/pallas_call | solution.py:256
  337.5 25.5 %all-gather.2.cloned.1.call-done.refs_0_ = bf16[6912,8,128]{2,1,0:T(8,128)(2,1)} async-done(((bf16[432,8,128]{2,1,0:T(8,128)(2,1)}), bf16[6912,8,128]{2,1,0:T(8,128)(2,1)}) %all-gather.2.cloned.1.call-update) | async-done | bytes 14155792 | tf_op jit(solution)/shard_map/all_gather | solution.py:560
  362.9 4.7 fusion.38
  384.4 4.3 fusion.174
  397.2 4.6 fusion.156
  405.5 4.7 fusion.25.packed_ref
  410.2 22.9 %attn_fwd.5 = (bf16[1176,512]{1,0:T(8,128)(2,1)S(1)}, f32[4,8,1280]{2,1,0:T(8,128)}) custom-call(bf16[1176,1536]{1,0:T(8,128)(2,1)S(1)} %fusion.25.packed_ref, bf16[1280,128]{1,0:T(8,128)(2,1)S(1)} %copy-done.26, bf16[1280,128]{1,0:T(8,128)(2,1)S(1)} %copy-done.23), custom_call_target="tpu_custom_call" | custom-call | flops 11329339392 | bytes 5419008 | tf_op jit(solution)/shard_map/attn_fwd/pallas_call | solution.py:256
  437.2 4.4 stack.40
  441.6 4.2 stack.39
  445.8 5.1 fusion.155
  454.9 8.8 fusion.23
  463.7 5.3 fusion.176
  470.0 7.1 collective-permute-done.38
  479.3 5.1 fusion.154
  508.2 4.7 fusion.147
  548.6 29.5 %attn_bwd.3 = bf16[1176,768]{1,0:T(8,128)(2,1)S(1)} custom-call(bf16[1176,768]{1,0:T(8,128)(2,1)S(1)} %copy-done.32, bf16[1176,256]{1,0:T(8,128)(2,1)S(1)} %convolution_convert_fusion.10.do_ref, bf16[1280,128]{1,0:T(8,128)(2,1)S(1)} %copy-done.26, bf16[1280,128]{1,0:T(8,128)(2,1)S(1)} %copy-done.23, f32[2,8,1280]{2,1,0:T(8,128)S(1)} %copy-done.37), custom_call_target="tpu_custom_call" | custom-call | flops 21242511360 | bytes 4515840 | tf_op jit(solution)/shard_map/attn_bwd/pallas_call | solution.py:350
  615.3 5.4 multiply_reduce_fusion
  620.7 4.3 fusion.151
  632.5 15.9 %convert_reduce_fusion = (f32[2048]{0:T(1024)S(1)}, bf16[1176,2048]{1,0:T(8,128)(2,1)}) fusion(f32[1176,2048]{1,0:T(8,128)} %get-tuple-element.297, f32[2048]{0:T(1024)S(1)} %copy-done.187, bf16[2048,1024]{1,0:T(8,128)(2,1)} %bitcast.421, f32[1176,1024]{1,0:T(8,128)} %broadcast_add_fusion), kind=kOutput, calls=%fused_computation.28 | convolution fusion | flops 4981872640 | bytes 23478272 | tf_op jit(solution)/shard_map/dot_general | solution.py:154
  648.4 9.6 convolution_convert_fusion.4
  658.1 8.5 convolution_convert_fusion.3
  678.4 7.9 convolution_convert_fusion.2
  696.0 4.0 fusion.150
  705.4 22.7 %attn_bwd.4.rest_0_ = bf16[1176,1536]{1,0:T(8,128)(2,1)S(1)} custom-call(bf16[1176,1536]{1,0:T(8,128)(2,1)} %copy-done.33, bf16[1176,512]{1,0:T(8,128)(2,1)S(1)} %convolution_convert_fusion.6.do_ref, bf16[1280,128]{1,0:T(8,128)(2,1)S(1)} %copy-done.26, bf16[1280,128]{1,0:T(8,128)(2,1)S(1)} %copy-done.21, f32[4,8,1280]{2,1,0:T(8,128)S(1)} %copy-done.35), custom_call_target="tpu_custom_call" | custom-call | flops 14161674240 | bytes 9031680 | tf_op jit(solution)/shard_map/attn_bwd/pallas_call | solution.py:350
  729.8 22.5 %attn_bwd.5 = bf16[1176,1536]{1,0:T(8,128)(2,1)S(1)} custom-call(bf16[1176,1536]{1,0:T(8,128)(2,1)} %copy-done.33, bf16[1176,512]{1,0:T(8,128)(2,1)S(1)} %convolution_convert_fusion.6.do_ref, bf16[1280,128]{1,0:T(8,128)(2,1)S(1)} %copy-done.26, bf16[1280,128]{1,0:T(8,128)(2,1)S(1)} %copy-done.21, ...), custom_call_target="tpu_custom_call", output_to_operand_aliasing={{}: (5, {})} | custom-call | flops 14161674240 | bytes 9031680 | tf_op jit(solution)/shard_map/attn_bwd/pallas_call | solution.py:350
  752.4 5.3 convolution_convert_fusion.11
  757.7 8.6 convolution_convert_fusion
  779.3 5.3 convolution_convert_fusion.1
  800.2 5.4 multiply_reduce_fusion.2
  805.7 4.6 fusion.149
  828.3 5.5 collective-permute-done.62
  846.8 10.4 %collective-permute-done.69 = bf16[1,4,108,8,128]{4,3,2,1,0:T(8,128)(2,1)S(1)} collective-permute-done((bf16[1,4,108,8,128]{4,3,2,1,0:T(8,128)(2,1)S(1)}, bf16[1,4,108,8,128]{4,3,2,1,0:T(8,128)(2,1)S(1)}, u32[]{:S(2)}, u32[]{:S(2)}) %collective-permute-start.69) | collective-permute-done | bytes 884768 | tf_op jit(solution)/shard_map/ppermute | solution.py:671
  859.6 15.6 %collective-permute-done.68 = bf16[1,4,108,8,128]{4,3,2,1,0:T(8,128)(2,1)S(1)} collective-permute-done((bf16[1,4,108,8,128]{4,3,2,1,0:T(8,128)(2,1)S(1)}, bf16[1,4,108,8,128]{4,3,2,1,0:T(8,128)(2,1)S(1)}, u32[]{:S(2)}, u32[]{:S(2)}) %collective-permute-start.68) | collective-permute-done | bytes 884768 | tf_op jit(solution)/shard_map/ppermute | solution.py:671
  880.9 8.3 collective-permute-done.65
  896.8 12.8 %collective-permute-done.74 = bf16[108,8,128]{2,1,0:T(8,128)(2,1)S(1)} collective-permute-done((bf16[108,8,128]{2,1,0:T(8,128)(2,1)S(1)}, bf16[108,8,128]{2,1,0:T(8,128)(2,1)S(1)}, u32[]{:S(2)}, u32[]{:S(2)}) %collective-permute-start.74) | collective-permute-done | bytes 221216 | tf_op jit(solution)/shard_map/ppermute | solution.py:671
  922.1 4.3 collective-permute-done.77
  949.4 6.0 unpack.1.g_ref
  970.8 5.5 adam.2
  976.3 4.2 convert_element_type.607
  (926 shorter events, 420.2 us)
Async XLA Ops:
  7.2 355.7 %all-gather.2.cloned.1.call-start = ((), (), s32[]{:S(2)}) async-start(), calls=%async_computation | async-start | bytes 15040512 | tf_op jit(solution)/shard_map/all_gather | solution.py:560
  16.5 17.1 %collective-permute-start = (bf16[255,8,128]{2,1,0:T(8,128)(2,1)S(1)}, bf16[255,8,128]{2,1,0:T(8,128)(2,1)}, u32[]{:S(2)}, u32[]{:S(2)}) collective-permute-start(bf16[255,8,128]{2,1,0:T(8,128)(2,1)S(1)} %get-tuple-element.256), channel_id=1, source_target_pairs={{0,8},{2,10},{4,12},{6,14},{8,16},{10,18},{12,20},{14,22},{16,24},... | collective-permute-start | bytes 1566728 | tf_op jit(solution)/shard_map/ppermute | solution.py:671
  19.3 27.3 %collective-permute-start.4 = (bf16[255,8,128]{2,1,0:T(8,128)(2,1)S(1)}, bf16[255,8,128]{2,1,0:T(8,128)(2,1)}, u32[]{:S(2)}, u32[]{:S(2)}) collective-permute-start(bf16[255,8,128]{2,1,0:T(8,128)(2,1)S(1)} %get-tuple-element.256), channel_id=1, source_target_pairs={{0,4},{2,6},{4,0},{6,2},{8,12},{10,14},{12,8},{14,10},{16,20},{18,... | collective-permute-start | bytes 1566728 | tf_op jit(solution)/shard_map/ppermute | solution.py:671
  21.1 25.5 %collective-permute-start.2 = (bf16[255,8,128]{2,1,0:T(8,128)(2,1)S(1)}, bf16[255,8,128]{2,1,0:T(8,128)(2,1)}, u32[]{:S(2)}, u32[]{:S(2)}) collective-permute-start(bf16[255,8,128]{2,1,0:T(8,128)(2,1)S(1)} %get-tuple-element.256), channel_id=1, source_target_pairs={{0,2},{2,0},{4,6},{6,4},{8,10},{10,8},{12,14},{14,12},{16,18},{18,... | collective-permute-start | bytes 1566728 | tf_op jit(solution)/shard_map/ppermute | solution.py:671
  22.6 24.0 %collective-permute-start.5 = (bf16[255,8,128]{2,1,0:T(8,128)(2,1)S(1)}, bf16[255,8,128]{2,1,0:T(8,128)(2,1)}, u32[]{:S(2)}, u32[]{:S(2)}) collective-permute-start(bf16[255,8,128]{2,1,0:T(8,128)(2,1)S(1)} %get-tuple-element.255), channel_id=1, source_target_pairs={{0,2},{2,0},{4,6},{6,4},{8,10},{10,8},{12,14},{14,12},{16,18},{18,... | collective-permute-start | bytes 1566728 | tf_op jit(solution)/shard_map/ppermute | solution.py:671
  23.1 23.5 %collective-permute-start.3 = (bf16[255,8,128]{2,1,0:T(8,128)(2,1)S(1)}, bf16[255,8,128]{2,1,0:T(8,128)(2,1)S(1)}, u32[]{:S(2)}, u32[]{:S(2)}) collective-permute-start(bf16[255,8,128]{2,1,0:T(8,128)(2,1)S(1)} %get-tuple-element.255), channel_id=1, source_target_pairs={{0,4},{2,6},{4,0},{6,2},{8,12},{10,14},{12,8},{14,10},{16,20},{18,... | collective-permute-start | bytes 1566728 | tf_op jit(solution)/shard_map/ppermute | solution.py:671
  33.5 13.1 %collective-permute-start.1 = (bf16[255,8,128]{2,1,0:T(8,128)(2,1)S(1)}, bf16[255,8,128]{2,1,0:T(8,128)(2,1)S(1)}, u32[]{:S(2)}, u32[]{:S(2)}) collective-permute-start(bf16[255,8,128]{2,1,0:T(8,128)(2,1)S(1)} %get-tuple-element.255), channel_id=1, source_target_pairs={{8,0},{10,2},{12,4},{14,6},{16,8},{18,10},{20,12},{22,14},{24,16},... | collective-permute-start | bytes 1566728 | tf_op jit(solution)/shard_map/ppermute | solution.py:671
  47.4 31.7 %collective-permute-start.6 = (bf16[255,8,128]{2,1,0:T(8,128)(2,1)}, bf16[255,8,128]{2,1,0:T(8,128)(2,1)}, u32[]{:S(2)}, u32[]{:S(2)}) collective-permute-start(bf16[255,8,128]{2,1,0:T(8,128)(2,1)} %collective-permute-done), channel_id=1, source_target_pairs={{0,8},{2,10},{4,12},{6,14},{8,16},{10,18},{12,20},{14,22},{16,24},... | collective-permute-start | bytes 1566728 | tf_op jit(solution)/shard_map/ppermute | solution.py:671
  47.9 43.1 %collective-permute-start.8 = (bf16[255,8,128]{2,1,0:T(8,128)(2,1)S(1)}, bf16[255,8,128]{2,1,0:T(8,128)(2,1)}, u32[]{:S(2)}, u32[]{:S(2)}) collective-permute-start(bf16[255,8,128]{2,1,0:T(8,128)(2,1)S(1)} %collective-permute-done.1), channel_id=1, source_target_pairs={{8,0},{10,2},{12,4},{14,6},{16,8},{18,10},{20,12},{22,14},{24,16},... | collective-permute-start | bytes 1566728 | tf_op jit(solution)/shard_map/ppermute | solution.py:671
  61.1 15.0 %collective-permute-start.16 = (bf16[255,8,128]{2,1,0:T(8,128)(2,1)}, bf16[255,8,128]{2,1,0:T(8,128)(2,1)S(1)}, u32[]{:S(2)}, u32[]{:S(2)}) collective-permute-start(bf16[255,8,128]{2,1,0:T(8,128)(2,1)} %collective-permute-done), channel_id=1, source_target_pairs={{0,4},{2,6},{4,0},{6,2},{8,12},{10,14},{12,8},{14,10},{16,20},{18,... | collective-permute-start | bytes 1566728 | tf_op jit(solution)/shard_map/ppermute | solution.py:671
  62.6 14.8 %collective-permute-start.12 = (bf16[255,8,128]{2,1,0:T(8,128)(2,1)}, bf16[255,8,128]{2,1,0:T(8,128)(2,1)S(1)}, u32[]{:S(2)}, u32[]{:S(2)}) collective-permute-start(bf16[255,8,128]{2,1,0:T(8,128)(2,1)} %collective-permute-done), channel_id=1, source_target_pairs={{0,2},{2,0},{4,6},{6,4},{8,10},{10,8},{12,14},{14,12},{16,18},{18,... | collective-permute-start | bytes 1566728 | tf_op jit(solution)/shard_map/ppermute | solution.py:671
  64.1 23.2 %collective-permute-start.14 = (bf16[255,8,128]{2,1,0:T(8,128)(2,1)S(1)}, bf16[255,8,128]{2,1,0:T(8,128)(2,1)S(1)}, u32[]{:S(2)}, u32[]{:S(2)}) collective-permute-start(bf16[255,8,128]{2,1,0:T(8,128)(2,1)S(1)} %collective-permute-done.1), channel_id=1, source_target_pairs={{0,4},{2,6},{4,0},{6,2},{8,12},{10,14},{12,8},{14,10},{16,20},{18,... | collective-permute-start | bytes 1566728 | tf_op jit(solution)/shard_map/ppermute | solution.py:671
  76.2 15.6 %collective-permute-start.17 = (bf16[255,8,128]{2,1,0:T(8,128)(2,1)S(1)}, bf16[255,8,128]{2,1,0:T(8,128)(2,1)S(1)}, u32[]{:S(2)}, u32[]{:S(2)}) collective-permute-start(bf16[255,8,128]{2,1,0:T(8,128)(2,1)S(1)} %collective-permute-done.1), channel_id=1, source_target_pairs={{0,2},{2,0},{4,6},{6,4},{8,10},{10,8},{12,14},{14,12},{16,18},{18,... | collective-permute-start | bytes 1566728 | tf_op jit(solution)/shard_map/ppermute | solution.py:671
  77.5 21.1 %collective-permute-start.13 = (bf16[255,8,128]{2,1,0:T(8,128)(2,1)S(1)}, bf16[255,8,128]{2,1,0:T(8,128)(2,1)S(1)}, u32[]{:S(2)}, u32[]{:S(2)}) collective-permute-start(bf16[255,8,128]{2,1,0:T(8,128)(2,1)S(1)} %collective-permute-done.12), channel_id=1, source_target_pairs={{0,4},{2,6},{4,0},{6,2},{8,12},{10,14},{12,8},{14,10},{16,20},{18,... | collective-permute-start | bytes 1566728 | tf_op jit(solution)/shard_map/ppermute | solution.py:671
  79.2 30.6 %collective-permute-start.10 = (bf16[255,8,128]{2,1,0:T(8,128)(2,1)}, bf16[255,8,128]{2,1,0:T(8,128)(2,1)S(1)}, u32[]{:S(2)}, u32[]{:S(2)}) collective-permute-start(bf16[255,8,128]{2,1,0:T(8,128)(2,1)} %collective-permute-done.6), channel_id=1, source_target_pairs={{0,4},{2,6},{4,0},{6,2},{8,12},{10,14},{12,8},{14,10},{16,20},{18,... | collective-permute-start | bytes 1566728 | tf_op jit(solution)/shard_map/ppermute | solution.py:671
  87.4 14.8 %collective-permute-start.15 = (bf16[255,8,128]{2,1,0:T(8,128)(2,1)S(1)}, bf16[255,8,128]{2,1,0:T(8,128)(2,1)S(1)}, u32[]{:S(2)}, u32[]{:S(2)}) collective-permute-start(bf16[255,8,128]{2,1,0:T(8,128)(2,1)S(1)} %collective-permute-done.14), channel_id=1, source_target_pairs={{0,2},{2,0},{4,6},{6,4},{8,10},{10,8},{12,14},{14,12},{16,18},{18,... | collective-permute-start | bytes 1566728 | tf_op jit(solution)/shard_map/ppermute | solution.py:671
  91.0 32.7 %collective-permute-start.7 = (bf16[255,8,128]{2,1,0:T(8,128)(2,1)}, bf16[255,8,128]{2,1,0:T(8,128)(2,1)}, u32[]{:S(2)}, u32[]{:S(2)}) collective-permute-start(bf16[255,8,128]{2,1,0:T(8,128)(2,1)} %collective-permute-done.6), channel_id=1, source_target_pairs={{0,2},{2,0},{4,6},{6,4},{8,10},{10,8},{12,14},{14,12},{16,18},{18,... | collective-permute-start | bytes 1566728 | tf_op jit(solution)/shard_map/ppermute | solution.py:671
  91.8 33.2 %collective-permute-start.11 = (bf16[255,8,128]{2,1,0:T(8,128)(2,1)}, bf16[255,8,128]{2,1,0:T(8,128)(2,1)}, u32[]{:S(2)}, u32[]{:S(2)}) collective-permute-start(bf16[255,8,128]{2,1,0:T(8,128)(2,1)} %collective-permute-done.8), channel_id=1, source_target_pairs={{0,2},{2,0},{4,6},{6,4},{8,10},{10,8},{12,14},{14,12},{16,18},{18,... | collective-permute-start | bytes 1566728 | tf_op jit(solution)/shard_map/ppermute | solution.py:671
  98.5 28.0 %collective-permute-start.9 = (bf16[255,8,128]{2,1,0:T(8,128)(2,1)}, bf16[255,8,128]{2,1,0:T(8,128)(2,1)}, u32[]{:S(2)}, u32[]{:S(2)}) collective-permute-start(bf16[255,8,128]{2,1,0:T(8,128)(2,1)} %collective-permute-done.8), channel_id=1, source_target_pairs={{0,4},{2,6},{4,0},{6,2},{8,12},{10,14},{12,8},{14,10},{16,20},{18,... | collective-permute-start | bytes 1566728 | tf_op jit(solution)/shard_map/ppermute | solution.py:671
  102.2 25.0 %collective-permute-start.18 = (bf16[255,8,128]{2,1,0:T(8,128)(2,1)}, bf16[255,8,128]{2,1,0:T(8,128)(2,1)}, u32[]{:S(2)}, u32[]{:S(2)}) collective-permute-start(bf16[255,8,128]{2,1,0:T(8,128)(2,1)} %collective-permute-done.6), channel_id=1, source_target_pairs={{0,8},{2,10},{4,12},{6,14},{8,16},{10,18},{12,20},{14,22},{16,24},... | collective-permute-start | bytes 1566728 | tf_op jit(solution)/shard_map/ppermute | solution.py:671
  109.7 18.0 %collective-permute-start.19 = (bf16[255,8,128]{2,1,0:T(8,128)(2,1)}, bf16[255,8,128]{2,1,0:T(8,128)(2,1)}, u32[]{:S(2)}, u32[]{:S(2)}) collective-permute-start(bf16[255,8,128]{2,1,0:T(8,128)(2,1)} %collective-permute-done.8), channel_id=1, source_target_pairs={{8,0},{10,2},{12,4},{14,6},{16,8},{18,10},{20,12},{22,14},{24,16},... | collective-permute-start | bytes 1566728 | tf_op jit(solution)/shard_map/ppermute | solution.py:671
  123.7 15.0 %collective-permute-start.20 = (bf16[255,8,128]{2,1,0:T(8,128)(2,1)}, bf16[255,8,128]{2,1,0:T(8,128)(2,1)S(1)}, u32[]{:S(2)}, u32[]{:S(2)}) collective-permute-start(bf16[255,8,128]{2,1,0:T(8,128)(2,1)} %collective-permute-done.2), channel_id=1, source_target_pairs={{0,4},{2,6},{4,0},{6,2},{8,12},{10,14},{12,8},{14,10},{16,20},{18,... | collective-permute-start | bytes 1566728 | tf_op jit(solution)/shard_map/ppermute | solution.py:671
  125.0 15.2 %collective-permute-start.21 = (bf16[255,8,128]{2,1,0:T(8,128)(2,1)S(1)}, bf16[255,8,128]{2,1,0:T(8,128)(2,1)S(1)}, u32[]{:S(2)}, u32[]{:S(2)}) collective-permute-start(bf16[255,8,128]{2,1,0:T(8,128)(2,1)S(1)} %copy-done.97), channel_id=1, source_target_pairs={{0,2},{2,0},{4,6},{6,4},{8,10},{10,8},{12,14},{14,12},{16,18},{18,... | collective-permute-start | bytes 1566728 | tf_op jit(solution)/shard_map/ppermute | solution.py:671
  126.5 23.8 %collective-permute-start.22 = (bf16[255,8,128]{2,1,0:T(8,128)(2,1)}, bf16[255,8,128]{2,1,0:T(8,128)(2,1)S(1)}, u32[]{:S(2)}, u32[]{:S(2)}) collective-permute-start(bf16[255,8,128]{2,1,0:T(8,128)(2,1)} %collective-permute-done.7), channel_id=1, source_target_pairs={{0,4},{2,6},{4,0},{6,2},{8,12},{10,14},{12,8},{14,10},{16,20},{18,... | collective-permute-start | bytes 1566728 | tf_op jit(solution)/shard_map/ppermute | solution.py:671
  127.2 24.3 %collective-permute-start.23 = (bf16[255,8,128]{2,1,0:T(8,128)(2,1)}, bf16[255,8,128]{2,1,0:T(8,128)(2,1)S(1)}, u32[]{:S(2)}, u32[]{:S(2)}) collective-permute-start(bf16[255,8,128]{2,1,0:T(8,128)(2,1)} %collective-permute-done.9), channel_id=1, source_target_pairs={{0,2},{2,0},{4,6},{6,4},{8,10},{10,8},{12,14},{14,12},{16,18},{18,... | collective-permute-start | bytes 1566728 | tf_op jit(solution)/shard_map/ppermute | solution.py:671
  130.2 41.1 %collective-permute-start.26 = (bf16[255,8,128]{2,1,0:T(8,128)(2,1)}, bf16[255,8,128]{2,1,0:T(8,128)(2,1)S(1)}, u32[]{:S(2)}, u32[]{:S(2)}) collective-permute-start(bf16[255,8,128]{2,1,0:T(8,128)(2,1)} %collective-permute-done.18), channel_id=1, source_target_pairs={{0,4},{2,6},{4,0},{6,2},{8,12},{10,14},{12,8},{14,10},{16,20},{18,... | collective-permute-start | bytes 1566728 | tf_op jit(solution)/shard_map/ppermute | solution.py:671
  138.7 21.0 %collective-permute-start.24 = (bf16[255,8,128]{2,1,0:T(8,128)(2,1)}, bf16[255,8,128]{2,1,0:T(8,128)(2,1)S(1)}, u32[]{:S(2)}, u32[]{:S(2)}) collective-permute-start(bf16[255,8,128]{2,1,0:T(8,128)(2,1)} %collective-permute-done.18), channel_id=1, source_target_pairs={{0,2},{2,0},{4,6},{6,4},{8,10},{10,8},{12,14},{14,12},{16,18},{18,... | collective-permute-start | bytes 1566728 | tf_op jit(solution)/shard_map/ppermute | solution.py:671
  140.2 29.6 %collective-permute-start.25 = (bf16[255,8,128]{2,1,0:T(8,128)(2,1)}, bf16[255,8,128]{2,1,0:T(8,128)(2,1)S(1)}, u32[]{:S(2)}, u32[]{:S(2)}) collective-permute-start(bf16[255,8,128]{2,1,0:T(8,128)(2,1)} %collective-permute-done.19), channel_id=1, source_target_pairs={{0,4},{2,6},{4,0},{6,2},{8,12},{10,14},{12,8},{14,10},{16,20},{18,... | collective-permute-start | bytes 1566728 | tf_op jit(solution)/shard_map/ppermute | solution.py:671
  150.3 21.1 %collective-permute-start.27 = (bf16[255,8,128]{2,1,0:T(8,128)(2,1)}, bf16[255,8,128]{2,1,0:T(8,128)(2,1)S(1)}, u32[]{:S(2)}, u32[]{:S(2)}) collective-permute-start(bf16[255,8,128]{2,1,0:T(8,128)(2,1)} %collective-permute-done.19), channel_id=1, source_target_pairs={{0,2},{2,0},{4,6},{6,4},{8,10},{10,8},{12,14},{14,12},{16,18},{18,... | collective-permute-start | bytes 1566728 | tf_op jit(solution)/shard_map/ppermute | solution.py:671
  159.7 15.7 %collective-permute-start.28 = (bf16[255,8,128]{2,1,0:T(8,128)(2,1)S(1)}, bf16[255,8,128]{2,1,0:T(8,128)(2,1)S(1)}, u32[]{:S(2)}, u32[]{:S(2)}) collective-permute-start(bf16[255,8,128]{2,1,0:T(8,128)(2,1)S(1)} %collective-permute-done.24), channel_id=1, source_target_pairs={{0,4},{2,6},{4,0},{6,2},{8,12},{10,14},{12,8},{14,10},{16,20},{18,... | collective-permute-start | bytes 1566728 | tf_op jit(solution)/shard_map/ppermute | solution.py:671
  597.4 17.3 %collective-permute-start.48 = (bf16[1176,1024]{1,0:T(8,128)(2,1)}, bf16[1176,1024]{1,0:T(8,128)(2,1)}, u32[]{:S(2)}, u32[]{:S(2)}) collective-permute-start(bf16[1176,1024]{1,0:T(8,128)(2,1)} %convolution_convert_fusion.5), channel_id=1, source_target_pairs={{0,1},{1,0},{2,3},{3,2},{4,5},{5,4},{6,7},{7,6},{8,9},{9,8},{10,11... | collective-permute-start | bytes 7225352 | tf_op jit(solution)/shard_map/ppermute | solution.py:381
  629.0 45.9 %collective-permute-start.51 = (bf16[4,1,78,8,128]{4,3,2,1,0:T(8,128)(2,1)}, bf16[4,1,78,8,128]{4,3,2,1,0:T(8,128)(2,1)S(1)}, u32[]{:S(2)}, u32[]{:S(2)}) collective-permute-start(bf16[4,1,78,8,128]{4,3,2,1,0:T(8,128)(2,1)} %get-tuple-element.225), channel_id=1, source_target_pairs={{0,6},{2,4},{4,2},{6,0},{8,14},{10,12},{12,10},{14,8},{16,22},{18,... | collective-permute-start | bytes 1916936 | tf_op jit(solution)/shard_map/ppermute | solution.py:671
  630.5 44.4 %collective-permute-start.50 = (bf16[4,1,78,8,128]{4,3,2,1,0:T(8,128)(2,1)}, bf16[4,1,78,8,128]{4,3,2,1,0:T(8,128)(2,1)}, u32[]{:S(2)}, u32[]{:S(2)}) collective-permute-start(bf16[4,1,78,8,128]{4,3,2,1,0:T(8,128)(2,1)} %get-tuple-element.226), channel_id=1, source_target_pairs={{0,4},{2,6},{4,0},{6,2},{8,12},{10,14},{12,8},{14,10},{16,20},{18,... | collective-permute-start | bytes 1916936 | tf_op jit(solution)/shard_map/ppermute | solution.py:671
  631.0 44.7 %collective-permute-start.49 = (bf16[4,1,78,8,128]{4,3,2,1,0:T(8,128)(2,1)S(1)}, bf16[4,1,78,8,128]{4,3,2,1,0:T(8,128)(2,1)}, u32[]{:S(2)}, u32[]{:S(2)}) collective-permute-start(bf16[4,1,78,8,128]{4,3,2,1,0:T(8,128)(2,1)S(1)} %get-tuple-element.227), channel_id=1, source_target_pairs={{0,2},{2,0},{4,6},{6,4},{8,10},{10,8},{12,14},{14,12},{16,18},{18,... | collective-permute-start | bytes 1916936 | tf_op jit(solution)/shard_map/ppermute | solution.py:671
  686.4 79.9 %collective-permute-start.53 = (bf16[2,2,216,8,128]{4,3,2,0,1:T(8,128)(2,1)}, bf16[2,2,216,8,128]{4,3,2,0,1:T(8,128)(2,1)}, u32[]{:S(2)}, u32[]{:S(2)}) collective-permute-start(bf16[2,2,216,8,128]{4,3,2,0,1:T(8,128)(2,1)} %bitcast.355), channel_id=1, source_target_pairs={{0,2},{2,0},{4,6},{6,4},{8,10},{10,8},{12,14},{14,12},{16,18},{18,... | collective-permute-start | bytes 5308424 | tf_op jit(solution)/shard_map/ppermute | solution.py:671
  687.1 79.3 %collective-permute-start.54 = (bf16[2,2,216,8,128]{4,3,2,0,1:T(8,128)(2,1)}, bf16[2,2,216,8,128]{4,3,2,0,1:T(8,128)(2,1)}, u32[]{:S(2)}, u32[]{:S(2)}) collective-permute-start(bf16[2,2,216,8,128]{4,3,2,0,1:T(8,128)(2,1)} %bitcast.354), channel_id=1, source_target_pairs={{0,4},{2,6},{4,0},{6,2},{8,12},{10,14},{12,8},{14,10},{16,20},{18,... | collective-permute-start | bytes 5308424 | tf_op jit(solution)/shard_map/ppermute | solution.py:671
  688.5 39.7 %collective-permute-start.81 = (bf16[78,8,128]{2,1,0:T(8,128)(2,1)}, bf16[78,8,128]{2,1,0:T(8,128)(2,1)S(1)}, u32[]{:S(2)}, u32[]{:S(2)}) collective-permute-start(bf16[78,8,128]{2,1,0:T(8,128)(2,1)} %get-tuple-element.252), channel_id=1, source_target_pairs={{0,24},{2,26},{4,28},{6,30},{8,16},{10,18},{12,20},{14,22},{16,8},... | collective-permute-start | bytes 479240 | tf_op jit(solution)/shard_map/ppermute | solution.py:671
  690.9 38.9 %collective-permute-start.80 = (bf16[78,8,128]{2,1,0:T(8,128)(2,1)}, bf16[78,8,128]{2,1,0:T(8,128)(2,1)S(1)}, u32[]{:S(2)}, u32[]{:S(2)}) collective-permute-start(bf16[78,8,128]{2,1,0:T(8,128)(2,1)} %get-tuple-element.253), channel_id=1, source_target_pairs={{0,16},{2,18},{4,20},{6,22},{8,24},{10,26},{12,28},{14,30},{16,0},... | collective-permute-start | bytes 479240 | tf_op jit(solution)/shard_map/ppermute | solution.py:671
  692.0 37.8 %collective-permute-start.79 = (bf16[78,8,128]{2,1,0:T(8,128)(2,1)S(1)}, bf16[78,8,128]{2,1,0:T(8,128)(2,1)S(1)}, u32[]{:S(2)}, u32[]{:S(2)}) collective-permute-start(bf16[78,8,128]{2,1,0:T(8,128)(2,1)S(1)} %get-tuple-element.254), channel_id=1, source_target_pairs={{0,8},{2,10},{4,12},{6,14},{8,0},{10,2},{12,4},{14,6},{16,24},{18,... | collective-permute-start | bytes 479240 | tf_op jit(solution)/shard_map/ppermute | solution.py:671
  728.2 41.4 %collective-permute-start.55 = (bf16[2,2,216,8,128]{4,3,2,0,1:T(8,128)(2,1)S(1)}, bf16[2,2,216,8,128]{4,3,2,0,1:T(8,128)(2,1)}, u32[]{:S(2)}, u32[]{:S(2)}) collective-permute-start(bf16[2,2,216,8,128]{4,3,2,0,1:T(8,128)(2,1)S(1)} %bitcast.429), channel_id=1, source_target_pairs={{0,6},{2,4},{4,2},{6,0},{8,14},{10,12},{12,10},{14,8},{16,22},{18,... | collective-permute-start | bytes 5308424 | tf_op jit(solution)/shard_map/ppermute | solution.py:671
  784.6 14.2 %collective-permute-start.56 = (bf16[1176,1024]{1,0:T(8,128)(2,1)}, bf16[1176,1024]{1,0:T(8,128)(2,1)}, u32[]{:S(2)}, u32[]{:S(2)}) collective-permute-start(bf16[1176,1024]{1,0:T(8,128)(2,1)} %convolution_convert_fusion.1), channel_id=1, source_target_pairs={{0,1},{1,0},{2,3},{3,2},{4,5},{5,4},{6,7},{7,6},{8,9},{9,8},{10,11... | collective-permute-start | bytes 7225352 | tf_op jit(solution)/shard_map/ppermute | solution.py:381
  790.3 45.9 %collective-permute-start.59 = (bf16[216,8,128]{2,1,0:T(8,128)(2,1)}, bf16[216,8,128]{2,1,0:T(8,128)(2,1)}, u32[]{:S(2)}, u32[]{:S(2)}) collective-permute-start(bf16[216,8,128]{2,1,0:T(8,128)(2,1)} %get-tuple-element.236), channel_id=1, source_target_pairs={{0,24},{2,26},{4,28},{6,30},{8,16},{10,18},{12,20},{14,22},{16,8},... | collective-permute-start | bytes 1327112 | tf_op jit(solution)/shard_map/ppermute | solution.py:671
  791.8 45.9 %collective-permute-start.58 = (bf16[216,8,128]{2,1,0:T(8,128)(2,1)}, bf16[216,8,128]{2,1,0:T(8,128)(2,1)}, u32[]{:S(2)}, u32[]{:S(2)}) collective-permute-start(bf16[216,8,128]{2,1,0:T(8,128)(2,1)} %get-tuple-element.237), channel_id=1, source_target_pairs={{0,16},{2,18},{4,20},{6,22},{8,24},{10,26},{12,28},{14,30},{16,0},... | collective-permute-start | bytes 1327112 | tf_op jit(solution)/shard_map/ppermute | solution.py:671
  792.1 33.3 %collective-permute-start.63 = (bf16[1,4,108,8,128]{4,3,2,1,0:T(8,128)(2,1)}, bf16[1,4,108,8,128]{4,3,2,1,0:T(8,128)(2,1)}, u32[]{:S(2)}, u32[]{:S(2)}) collective-permute-start(bf16[1,4,108,8,128]{4,3,2,1,0:T(8,128)(2,1)} %get-tuple-element.233), channel_id=1, source_target_pairs={{0,6},{2,4},{4,2},{6,0},{8,14},{10,12},{12,10},{14,8},{16,22},{18,... | collective-permute-start | bytes 2654216 | tf_op jit(solution)/shard_map/ppermute | solution.py:671
  793.7 40.2 %collective-permute-start.62 = (bf16[1,4,108,8,128]{4,3,2,1,0:T(8,128)(2,1)}, bf16[1,4,108,8,128]{4,3,2,1,0:T(8,128)(2,1)}, u32[]{:S(2)}, u32[]{:S(2)}) collective-permute-start(bf16[1,4,108,8,128]{4,3,2,1,0:T(8,128)(2,1)} %get-tuple-element.234), channel_id=1, source_target_pairs={{0,4},{2,6},{4,0},{6,2},{8,12},{10,14},{12,8},{14,10},{16,20},{18,... | collective-permute-start | bytes 2654216 | tf_op jit(solution)/shard_map/ppermute | solution.py:671
  798.8 36.5 %collective-permute-start.61 = (bf16[1,4,108,8,128]{4,3,2,1,0:T(8,128)(2,1)}, bf16[1,4,108,8,128]{4,3,2,1,0:T(8,128)(2,1)S(1)}, u32[]{:S(2)}, u32[]{:S(2)}) collective-permute-start(bf16[1,4,108,8,128]{4,3,2,1,0:T(8,128)(2,1)} %get-tuple-element.235), channel_id=1, source_target_pairs={{0,2},{2,0},{4,6},{6,4},{8,10},{10,8},{12,14},{14,12},{16,18},{18,... | collective-permute-start | bytes 2654216 | tf_op jit(solution)/shard_map/ppermute | solution.py:671
  825.7 15.2 %collective-permute-start.57 = (bf16[216,8,128]{2,1,0:T(8,128)(2,1)S(1)}, bf16[216,8,128]{2,1,0:T(8,128)(2,1)S(1)}, u32[]{:S(2)}, u32[]{:S(2)}) collective-permute-start(bf16[216,8,128]{2,1,0:T(8,128)(2,1)S(1)} %copy-done.114), channel_id=1, source_target_pairs={{0,8},{2,10},{4,12},{6,14},{8,0},{10,2},{12,4},{14,6},{16,24},{18,... | collective-permute-start | bytes 1327112 | tf_op jit(solution)/shard_map/ppermute | solution.py:671
  833.8 23.5 %collective-permute-start.69 = (bf16[1,4,108,8,128]{4,3,2,1,0:T(8,128)(2,1)S(1)}, bf16[1,4,108,8,128]{4,3,2,1,0:T(8,128)(2,1)S(1)}, u32[]{:S(2)}, u32[]{:S(2)}) collective-permute-start(bf16[1,4,108,8,128]{4,3,2,1,0:T(8,128)(2,1)S(1)} %get-tuple-element.230), channel_id=1, source_target_pairs={{0,6},{2,4},{4,2},{6,0},{8,14},{10,12},{12,10},{14,8},{16,22},{18,... | collective-permute-start | bytes 2654216 | tf_op jit(solution)/shard_map/ppermute | solution.py:671
  835.3 39.9 %collective-permute-start.68 = (bf16[1,4,108,8,128]{4,3,2,1,0:T(8,128)(2,1)S(1)}, bf16[1,4,108,8,128]{4,3,2,1,0:T(8,128)(2,1)S(1)}, u32[]{:S(2)}, u32[]{:S(2)}) collective-permute-start(bf16[1,4,108,8,128]{4,3,2,1,0:T(8,128)(2,1)S(1)} %get-tuple-element.231), channel_id=1, source_target_pairs={{0,4},{2,6},{4,0},{6,2},{8,12},{10,14},{12,8},{14,10},{16,20},{18,... | collective-permute-start | bytes 2654216 | tf_op jit(solution)/shard_map/ppermute | solution.py:671
  836.3 41.6 %collective-permute-start.67 = (bf16[1,4,108,8,128]{4,3,2,1,0:T(8,128)(2,1)S(1)}, bf16[1,4,108,8,128]{4,3,2,1,0:T(8,128)(2,1)S(1)}, u32[]{:S(2)}, u32[]{:S(2)}) collective-permute-start(bf16[1,4,108,8,128]{4,3,2,1,0:T(8,128)(2,1)S(1)} %get-tuple-element.232), channel_id=1, source_target_pairs={{0,2},{2,0},{4,6},{6,4},{8,10},{10,8},{12,14},{14,12},{16,18},{18,... | collective-permute-start | bytes 2654216 | tf_op jit(solution)/shard_map/ppermute | solution.py:671
  837.8 73.9 %collective-permute-start.89 = (f32[17920]{0:T(1024)S(1)}, f32[17920]{0:T(1024)S(1)}, u32[]{:S(2)}, u32[]{:S(2)}) collective-permute-start(f32[17920]{0:T(1024)S(1)} %constant_dynamic-update-slice_fusion.10), channel_id=1, source_target_pairs={{0,1},{1,0},{2,3},{3,2},{4,5},{5,4},{6,7},{7,6},{8,9},{9,8},{10,11... | collective-permute-start | bytes 215048 | tf_op jit(solution)/shard_map/ppermute | solution.py:401
  842.5 70.5 %collective-permute-start.60 = (bf16[216,8,128]{2,1,0:T(8,128)(2,1)S(1)}, bf16[216,8,128]{2,1,0:T(8,128)(2,1)S(1)}, u32[]{:S(2)}, u32[]{:S(2)}) collective-permute-start(bf16[216,8,128]{2,1,0:T(8,128)(2,1)S(1)} %fusion.84), channel_id=1, source_target_pairs={{0,16},{2,18},{4,20},{6,22},{8,24},{10,26},{12,28},{14,30},{1,17},... | collective-permute-start | bytes 1327112 | tf_op jit(solution)/shard_map/ppermute | solution.py:671
  857.3 21.4 %collective-permute-start.66 = (bf16[108,8,128]{2,1,0:T(8,128)(2,1)S(1)}, bf16[108,8,128]{2,1,0:T(8,128)(2,1)S(1)}, u32[]{:S(2)}, u32[]{:S(2)}) collective-permute-start(bf16[108,8,128]{2,1,0:T(8,128)(2,1)S(1)} %get-tuple-element.247), channel_id=1, source_target_pairs={{0,24},{2,26},{4,28},{6,30},{8,16},{10,18},{12,20},{14,22},{16,8},... | collective-permute-start | bytes 663560 | tf_op jit(solution)/shard_map/ppermute | solution.py:671
  875.3 13.9 %collective-permute-start.65 = (bf16[108,8,128]{2,1,0:T(8,128)(2,1)S(1)}, bf16[108,8,128]{2,1,0:T(8,128)(2,1)S(1)}, u32[]{:S(2)}, u32[]{:S(2)}) collective-permute-start(bf16[108,8,128]{2,1,0:T(8,128)(2,1)S(1)} %get-tuple-element.248), channel_id=1, source_target_pairs={{0,16},{2,18},{4,20},{6,22},{8,24},{10,26},{12,28},{14,30},{16,0},... | collective-permute-start | bytes 663560 | tf_op jit(solution)/shard_map/ppermute | solution.py:671
  878.7 17.4 %collective-permute-start.75 = (bf16[108,8,128]{2,1,0:T(8,128)(2,1)S(1)}, bf16[108,8,128]{2,1,0:T(8,128)(2,1)S(1)}, u32[]{:S(2)}, u32[]{:S(2)}) collective-permute-start(bf16[108,8,128]{2,1,0:T(8,128)(2,1)S(1)} %get-tuple-element.244), channel_id=1, source_target_pairs={{0,24},{2,26},{4,28},{6,30},{8,16},{10,18},{12,20},{14,22},{16,8},... | collective-permute-start | bytes 663560 | tf_op jit(solution)/shard_map/ppermute | solution.py:671
  889.2 20.4 %collective-permute-start.74 = (bf16[108,8,128]{2,1,0:T(8,128)(2,1)S(1)}, bf16[108,8,128]{2,1,0:T(8,128)(2,1)S(1)}, u32[]{:S(2)}, u32[]{:S(2)}) collective-permute-start(bf16[108,8,128]{2,1,0:T(8,128)(2,1)S(1)} %get-tuple-element.245), channel_id=1, source_target_pairs={{0,16},{2,18},{4,20},{6,22},{8,24},{10,26},{12,28},{14,30},{16,0},... | collective-permute-start | bytes 663560 | tf_op jit(solution)/shard_map/ppermute | solution.py:671
  889.2 21.1 %collective-permute-start.73 = (bf16[108,8,128]{2,1,0:T(8,128)(2,1)S(1)}, bf16[108,8,128]{2,1,0:T(8,128)(2,1)S(1)}, u32[]{:S(2)}, u32[]{:S(2)}) collective-permute-start(bf16[108,8,128]{2,1,0:T(8,128)(2,1)S(1)} %get-tuple-element.246), channel_id=1, source_target_pairs={{0,8},{2,10},{4,12},{6,14},{8,0},{10,2},{12,4},{14,6},{16,24},{18,... | collective-permute-start | bytes 663560 | tf_op jit(solution)/shard_map/ppermute | solution.py:671
  896.1 18.2 %collective-permute-start.72 = (bf16[108,8,128]{2,1,0:T(8,128)(2,1)S(1)}, bf16[108,8,128]{2,1,0:T(8,128)(2,1)S(1)}, u32[]{:S(2)}, u32[]{:S(2)}) collective-permute-start(bf16[108,8,128]{2,1,0:T(8,128)(2,1)S(1)} %fusion.110), channel_id=1, source_target_pairs={{24,8},{26,10},{28,12},{30,14},{25,9},{27,11},{29,13},{31,15}} | collective-permute-start | bytes 663560 | tf_op jit(solution)/shard_map/ppermute | solution.py:671
  913.0 13.4 %collective-permute-start.77 = (bf16[108,8,128]{2,1,0:T(8,128)(2,1)S(1)}, bf16[108,8,128]{2,1,0:T(8,128)(2,1)S(1)}, u32[]{:S(2)}, u32[]{:S(2)}) collective-permute-start(bf16[108,8,128]{2,1,0:T(8,128)(2,1)S(1)} %fusion.107), channel_id=1, source_target_pairs={{16,0},{18,2},{20,4},{22,6},{17,1},{19,3},{21,5},{23,7}} | collective-permute-start | bytes 663560 | tf_op jit(solution)/shard_map/ppermute | solution.py:671
  914.3 15.3 %collective-permute-start.76 = (bf16[108,8,128]{2,1,0:T(8,128)(2,1)S(1)}, bf16[108,8,128]{2,1,0:T(8,128)(2,1)S(1)}, u32[]{:S(2)}, u32[]{:S(2)}) collective-permute-start(bf16[108,8,128]{2,1,0:T(8,128)(2,1)S(1)} %fusion.107), channel_id=1, source_target_pairs={{8,0},{10,2},{12,4},{14,6},{9,1},{11,3},{13,5},{15,7}} | collective-permute-start | bytes 663560 | tf_op jit(solution)/shard_map/ppermute | solution.py:671
  915.8 21.4 %collective-permute-start.92 = (f32[17920]{0:T(1024)S(1)}, f32[17920]{0:T(1024)}, u32[]{:S(2)}, u32[]{:S(2)}) collective-permute-start(f32[17920]{0:T(1024)S(1)} %add.1320), channel_id=1, source_target_pairs={{0,6},{2,4},{4,2},{6,0},{8,14},{10,12},{12,10},{14,8},{16,22},{18,... | collective-permute-start | bytes 215048 | tf_op jit(solution)/shard_map/ppermute | solution.py:401
  917.3 21.3 %collective-permute-start.91 = (f32[17920]{0:T(1024)S(1)}, f32[17920]{0:T(1024)}, u32[]{:S(2)}, u32[]{:S(2)}) collective-permute-start(f32[17920]{0:T(1024)S(1)} %add.1320), channel_id=1, source_target_pairs={{0,4},{2,6},{4,0},{6,2},{8,12},{10,14},{12,8},{14,10},{16,20},{18,... | collective-permute-start | bytes 215048 | tf_op jit(solution)/shard_map/ppermute | solution.py:401
  921.5 17.1 %collective-permute-start.90 = (f32[17920]{0:T(1024)S(1)}, f32[17920]{0:T(1024)}, u32[]{:S(2)}, u32[]{:S(2)}) collective-permute-start(f32[17920]{0:T(1024)S(1)} %add.1320), channel_id=1, source_target_pairs={{0,2},{2,0},{4,6},{6,4},{8,10},{10,8},{12,14},{14,12},{16,18},{18,... | collective-permute-start | bytes 215048 | tf_op jit(solution)/shard_map/ppermute | solution.py:401
  944.1 11.3 %collective-permute-start.88 = (f32[6272]{0:T(1024)S(1)}, f32[6272]{0:T(1024)}, u32[]{:S(2)}, u32[]{:S(2)}) collective-permute-start(f32[6272]{0:T(1024)S(1)} %add_add_fusion.22), channel_id=1, source_target_pairs={{0,24},{2,26},{4,28},{6,30},{8,16},{10,18},{12,20},{14,22},{16,8},... | collective-permute-start | bytes 75272 | tf_op jit(solution)/shard_map/ppermute | solution.py:401
  (265 other events, 3308.4 us)
Sparse Core Ops, SparseCore 0:
  197.1 165.7 all-gather.1

commit v4 on v3

--- a/solution.py
+++ b/solution.py
@@ -534,7 +534,7 @@
         in_specs=[pl.BlockSpec(memory_space=pltpu.SMEM)] + [spec] * len(arrays),
         out_specs=[spec] * n_out,
         out_shape=[jax.ShapeDtypeStruct((rows, 128), jnp.float32)] * n_out,
-        compiler_params=pltpu.CompilerParams(vmem_limit_bytes=32 << 20),
+        compiler_params=pltpu.CompilerParams(vmem_limit_bytes=60 << 20),
         name="adam",
     )(scalars, *arrays)
 
@@ -585,6 +585,7 @@
             first = (ax, by, ay, bx) + last
         if k == 3:
             first = first + (a, b)
+            nearly = (ax, by, ay, bx)
         last = (axy, byx)
         a, b = pin((a, b), waits)
         waits = (ax, by, ay, bx) if k == 0 else (ax, by, ay, bx, axy, byx)
@@ -596,7 +597,7 @@
         for side, pz, py, px, piece in arrived[n]:
             slot = (pz * 4 + py * 2 + px) * 2 + side
             whole = lax.dynamic_update_index_in_dim(whole, piece, slot, 0)
-    return whole.reshape((32 * half,) + tiles.shape[1:]), begun
+    return whole.reshape((32 * half,) + tiles.shape[1:]), begun, nearly
 
 
 def split_gathered(gathered, sizes, part, first, total):
@@ -805,12 +806,12 @@
     normed_two = layer_norm(middle, vectors[tag + "ln2_g"], vectors[tag + "ln2_b"]).astype(
         jnp.bfloat16
     )
-    normed_two = pin(normed_two, watch(normed_two))
     hidden = matmul(normed_two, mats["w_" + tag + "up"]) + local_columns(
         vectors["b_" + tag + "up"], False, ways, member
     )
     activated = lax.optimization_barrier(jax.nn.gelu(hidden).astype(jnp.bfloat16))
     down_part = matmul(activated, mats["w_" + tag + "down"])
+    down_part = pin(down_part, watch(down_part))
     result = middle + tensor_total(down_part) + vectors["b_" + tag + "down"]
     kept = (
         stream,
@@ -959,7 +960,7 @@
     if tiled:
         pred_tiles = rows(pred_params).astype(jnp.bfloat16).reshape(-1, 8, 128)
         own_tiles = jnp.concatenate([pack_tiles(rows(enc_params), place, spans), pred_tiles], 0)
-        enc_tiles, begun = tree_gather(own_tiles)
+        enc_tiles, begun, nearly = tree_gather(own_tiles)
     segment, target_local = pin((segment, target_params), begun)
     places = positions(segment)
     context_mask = context > 0
@@ -970,11 +971,10 @@
     pred_pos = sincos(places, PD)
     if tiled:
         target_tiles = pack_tiles(rows(target_local), place, spans)
-        enc_tiles, target_tiles, embed_pos, pred_pos, online_sides, all_sides = (
-            lax.optimization_barrier(
-                (enc_tiles, target_tiles, embed_pos, pred_pos, online_sides, all_sides)
-            )
+        enc_tiles, embed_pos, pred_pos, online_sides, all_sides = pin(
+            (enc_tiles, embed_pos, pred_pos, online_sides, all_sides), target_tiles
         )
+        target_tiles = pin(target_tiles, nearly)
         sizes = [size for _, size in ENC_TILES]
         shard, both = sum(sizes) // 16, own_tiles.shape[0]
         mats = from_tiles(split_gathered(enc_tiles, sizes, shard, 0, both), ways)

time: 999 us -> 989 us (0.990)
  waiting for transfers between devices: 207 us -> 188 us
    all_gather x1, waiting for transfers between devices: 25.5 us -> 11.5 us  [gather_dp(): return lax.all_gather(x, 'dp', axis=0, tiled=True)]
    unnamed x460 -> x414, local copies, waits for them, and re-layouts: 54.6 us -> 46.1 us
  transfers between devices with their start and end apart: 97 -> 97, of which waited for: 41 -> 39; matrix products, arithmetic and copies ran while one was open for 24% -> 25% of each run, Pallas kernels for 13% -> 13%
where the time goes in v4:
time: 989 us; the launch traced here: 979 us
  Pallas kernels  205 us (21%)
  waiting for transfers between devices  188 us (19%)
  other arithmetic  166 us (17%)
  matrix products  160 us (16%)
  local copies, waits for them, and re-layouts  122 us (12%)
  starting transfers between devices  114 us (12%)
  between operations  24.6 us (2%)
    ppermute x61, waiting for transfers between devices, permute(): return lax.ppermute(x, 'dp', pairs)  147 us
    ppermute x61, starting transfers between devices, permute(): return lax.ppermute(x, 'dp', pairs)  87.6 us
    pallas_call x3, Pallas kernels, attn_bwd(): pl.pallas_call(functools.partial(attn_bwd_kernel, heads, e, T, TP, W, fir...  74.7 us
    dot_general x16, matrix products, matmul(): return jnp.dot(left, right, preferred_element_type=jnp.float32)  70 us
    pallas_call x3, Pallas kernels, attn_fwd(): pl.pallas_call(functools.partial(attn_fwd_kernel, heads, e, T, TP, W), gr...  62.5 us
    reduce_sum x13, other arithmetic, layer_norm(): centered = values - jnp.mean(values, axis=-1, keepdims=True)  56.3 us
    dot_general x11, matrix products, matmul_tn(): lax.dot_general(left, right, (((0,), (0,)), ((), ())), preferred_element_...  48 us
    unnamed x414, local copies, waits for them, and re-layouts  46.1 us
  transfers between devices with their start and end apart: 97, of which 39 were waited for; matrix products, arithmetic and copies ran while one was open for 25% of the time, Pallas kernels for 13%

profile of v4, /device:TPU:0, one launch (start us, length us, event | category | flops | bytes accessed | tf_op | source)
XLA Modules:
  0.0 979.2 jit_solution(4608086011684079874)
XLA Ops:
  9.2 6.0 pack.2
  16.5 5.1 collective-permute-start.1
  25.1 8.7 collective-permute-done.1
  35.4 9.5 collective-permute-done
  52.8 9.8 %multiply_sine_fusion = (f32[1176,512]{1,0:T(8,128)}, f32[1176,512]{1,0:T(8,128)}) fusion(f32[512]{0:T(512)S(1)} %multiply_exponential_fusion, f32[1176]{0:T(1024)S(1)} %subtract_convert_fusion.1), kind=kLoop, calls=%fused_computation.110 | loop fusion | flops 602112 | bytes 4823648 | tf_op jit(solution)/shard_map/sin | solution.py:125
  70.3 7.4 collective-permute-done.14
  84.2 5.2 collective-permute-done.17
  91.4 9.2 collective-permute-done.15
  102.1 9.7 collective-permute-done.7
  113.9 6.3 pack.3
  121.1 5.1 pad_maximum_fusion
  154.1 10.9 %collective-permute-done.24 = bf16[255,8,128]{2,1,0:T(8,128)(2,1)S(1)} collective-permute-done((bf16[255,8,128]{2,1,0:T(8,128)(2,1)}, bf16[255,8,128]{2,1,0:T(8,128)(2,1)S(1)}, u32[]{:S(2)}, u32[]{:S(2)}) %collective-permute-start.24) | collective-permute-done | bytes 522272 | tf_op jit(solution)/shard_map/ppermute | solution.py:672
  167.3 4.5 collective-permute-done.26
  172.9 4.5 collective-permute-done.28
  178.5 5.7 copy-done.27
  185.7 4.2 convolution_bitcast_fusion
  198.3 6.0 fusion.164
  207.9 4.6 fusion.24.packed_ref
  212.6 22.7 %attn_fwd.3 = (bf16[1176,512]{1,0:T(8,128)(2,1)S(1)}, f32[4,8,1280]{2,1,0:T(8,128)S(1)}) custom-call(bf16[1176,1536]{1,0:T(8,128)(2,1)S(1)} %fusion.24.packed_ref, bf16[1280,128]{1,0:T(8,128)(2,1)S(1)} %concatenate.50.qa_ref, bf16[1280,128]{1,0:T(8,128)(2,1)S(1)} %get-tuple-element.96.ka_ref), custom_call_target="tpu_custom_call" | custom-call | flops 11329339392 | bytes 5419008 | tf_op jit(solution)/shard_map/attn_fwd/pallas_call | solution.py:256
  239.2 4.3 stack.33
  243.5 4.3 stack.34
  247.9 5.1 fusion.163
  256.9 10.1 %fusion.7 = (bf16[1176,2048]{1,0:T(8,128)(2,1)S(1)}, f32[1176,2048]{1,0:T(8,128)}) fusion(f32[2048]{0:T(1024)S(1)} %dynamic_slice.133, bf16[1024,2048]{1,0:T(8,128)(2,1)S(1)} %bitcast.408, f32[1176,1024]{1,0:T(8,128)S(1)} %get-tuple-element.218, f32[1024]{0:T(1024)S(1)} %get-tuple-element.261, f32[1024]{0:T(1024)S(1)} %get-tuple-element.262, ...), kind=kOutput, calls=%fused_computation.11 | convolution fusion | flops 4962607104 | bytes 23487680 | tf_op jit(solution)/shard_map/dot_general | solution.py:144
  267.1 7.2 fusion.172
  282.7 6.0 fusion.162
  303.5 16.8 %attn_fwd.4 = (bf16[1176,256]{1,0:T(8,128)(2,1)S(1)}, f32[2,8,1280]{2,1,0:T(8,128)S(1)}) custom-call(bf16[1176,768]{1,0:T(8,128)(2,1)S(1)} %fusion.47.packed_ref, bf16[1280,128]{1,0:T(8,128)(2,1)S(1)} %concatenate.50.qa_ref, bf16[1280,128]{1,0:T(8,128)(2,1)S(1)} %get-tuple-element.100.ka_ref), custom_call_target="tpu_custom_call" | custom-call | flops 8497004544 | bytes 2709504 | tf_op jit(solution)/shard_map/attn_fwd/pallas_call | solution.py:256
  343.5 11.5 %all-gather.2.cloned.1.call-done.refs_0_ = bf16[6912,8,128]{2,1,0:T(8,128)(2,1)} async-done(((bf16[432,8,128]{2,1,0:T(8,128)(2,1)}), bf16[6912,8,128]{2,1,0:T(8,128)(2,1)}) %all-gather.2.cloned.1.call-update) | async-done | bytes 14155792 | tf_op jit(solution)/shard_map/all_gather | solution.py:560
  369.2 4.3 fusion.175
  382.0 6.0 fusion.157
  389.8 4.6 fusion.25.packed_ref
  394.5 22.9 %attn_fwd.5 = (bf16[1176,512]{1,0:T(8,128)(2,1)S(1)}, f32[4,8,1280]{2,1,0:T(8,128)}) custom-call(bf16[1176,1536]{1,0:T(8,128)(2,1)S(1)} %fusion.25.packed_ref, bf16[1280,128]{1,0:T(8,128)(2,1)S(1)} %copy-done.19, bf16[1280,128]{1,0:T(8,128)(2,1)S(1)} %copy-done.17), custom_call_target="tpu_custom_call" | custom-call | flops 11329339392 | bytes 5419008 | tf_op jit(solution)/shard_map/attn_fwd/pallas_call | solution.py:256
  425.7 4.2 stack.40
  429.9 5.1 fusion.156
  438.9 8.8 fusion.23
  447.8 5.3 fusion.177
  454.1 7.1 collective-permute-done.38
  463.3 5.1 fusion.155
  493.6 4.7 fusion.148
  535.2 29.5 %attn_bwd.3 = bf16[1176,768]{1,0:T(8,128)(2,1)S(1)} custom-call(bf16[1176,768]{1,0:T(8,128)(2,1)S(1)} %copy-done.23, bf16[1176,256]{1,0:T(8,128)(2,1)S(1)} %convolution_convert_fusion.10.do_ref, bf16[1280,128]{1,0:T(8,128)(2,1)S(1)} %copy-done.19, bf16[1280,128]{1,0:T(8,128)(2,1)S(1)} %copy-done.17, f32[2,8,1280]{2,1,0:T(8,128)S(1)} %get-tuple-element.107.lse_ref), custom_call_target="tpu_custom_call" | custom-call | flops 21242511360 | bytes 4515840 | tf_op jit(solution)/shard_map/attn_bwd/pallas_call | solution.py:350
  601.8 5.4 multiply_reduce_fusion
  607.2 4.3 fusion.152
  619.4 16.0 %convert_reduce_fusion = (f32[2048]{0:T(1024)S(1)}, bf16[1176,2048]{1,0:T(8,128)(2,1)}) fusion(f32[1176,2048]{1,0:T(8,128)} %get-tuple-element.297, f32[2048]{0:T(1024)S(1)} %copy-done.168, bf16[2048,1024]{1,0:T(8,128)(2,1)} %bitcast.410, f32[1176,1024]{1,0:T(8,128)} %broadcast_add_fusion), kind=kOutput, calls=%fused_computation.28 | convolution fusion | flops 4981872640 | bytes 23478272 | tf_op jit(solution)/shard_map/dot_general | solution.py:154
  635.4 9.0 convolution_convert_fusion.4
  644.4 8.5 convolution_convert_fusion.3
  665.6 7.8 convolution_convert_fusion.2
  693.0 22.7 %attn_bwd.4.rest_0_ = bf16[1176,1536]{1,0:T(8,128)(2,1)S(1)} custom-call(bf16[1176,1536]{1,0:T(8,128)(2,1)} %copy-done.24, bf16[1176,512]{1,0:T(8,128)(2,1)S(1)} %convolution_convert_fusion.6.do_ref, bf16[1280,128]{1,0:T(8,128)(2,1)S(1)} %copy-done.19, bf16[1280,128]{1,0:T(8,128)(2,1)S(1)} %copy-done.15, f32[4,8,1280]{2,1,0:T(8,128)S(1)} %copy-done.26), custom_call_target="tpu_custom_call" | custom-call | flops 14161674240 | bytes 9031680 | tf_op jit(solution)/shard_map/attn_bwd/pallas_call | solution.py:350
  717.3 22.5 %attn_bwd.5 = bf16[1176,1536]{1,0:T(8,128)(2,1)S(1)} custom-call(bf16[1176,1536]{1,0:T(8,128)(2,1)} %copy-done.24, bf16[1176,512]{1,0:T(8,128)(2,1)S(1)} %convolution_convert_fusion.6.do_ref, bf16[1280,128]{1,0:T(8,128)(2,1)S(1)} %copy-done.19, bf16[1280,128]{1,0:T(8,128)(2,1)S(1)} %copy-done.15, ...), custom_call_target="tpu_custom_call", output_to_operand_aliasing={{}: (5, {})} | custom-call | flops 14161674240 | bytes 9031680 | tf_op jit(solution)/shard_map/attn_bwd/pallas_call | solution.py:350
  739.8 5.3 convolution_convert_fusion.11
  745.1 8.5 convolution_convert_fusion
  763.2 5.4 convolution_convert_fusion.1
  785.7 5.4 multiply_reduce_fusion.2
  791.2 4.6 fusion.150
  811.3 5.3 collective-permute-done.62
  825.0 7.9 collective-permute-start.64
  834.5 4.7 collective-permute-done.67
  839.3 17.6 %collective-permute-done.68 = bf16[1,4,108,8,128]{4,3,2,1,0:T(8,128)(2,1)S(1)} collective-permute-done((bf16[1,4,108,8,128]{4,3,2,1,0:T(8,128)(2,1)S(1)}, bf16[1,4,108,8,128]{4,3,2,1,0:T(8,128)(2,1)S(1)}, u32[]{:S(2)}, u32[]{:S(2)}) %collective-permute-start.68) | collective-permute-done | bytes 884768 | tf_op jit(solution)/shard_map/ppermute | solution.py:672
  869.1 9.8 collective-permute-done.73
  878.9 4.4 collective-permute-start.70
  894.8 15.6 %collective-permute-done.76 = bf16[108,8,128]{2,1,0:T(8,128)(2,1)S(1)} collective-permute-done((bf16[108,8,128]{2,1,0:T(8,128)(2,1)S(1)}, bf16[108,8,128]{2,1,0:T(8,128)(2,1)S(1)}, u32[]{:S(2)}, u32[]{:S(2)}) %collective-permute-start.76) | collective-permute-done | bytes 221216 | tf_op jit(solution)/shard_map/ppermute | solution.py:672
  912.0 9.6 collective-permute-done.77
  939.8 6.0 unpack.1.g_ref
  950.5 4.3 adam.3
  956.6 10.0 %adam.2 = (f32[3456,128]{1,0:T(8,128)}, f32[3456,128]{1,0:T(8,128)}, f32[3456,128]{1,0:T(8,128)}, f32[3456,128]{1,0:T(8,128)}) custom-call(f32[3]{0:T(128)} %pad_maximum_fusion.7.scalars, f32[3456,128]{1,0:T(8,128)} %bitcast.403, f32[3456,128]{1,0:T(8,128)} %bitcast.423, f32[3456,128]{1,0:T(8,128)} %bitcast.424, f32[3456,128]{1,0:T(8,128)} %unpack.1.g_ref, ...), custom_call_target="tpu_custom_call" | custom-call | tf_op jit(solution)/shard_map/adam/pallas_call | solution.py:531
  966.6 4.2 convert_element_type.607
  (877 shorter events, 411.7 us)
Async XLA Ops:
  7.2 347.8 %all-gather.2.cloned.1.call-start = ((), (), s32[]{:S(2)}) async-start(), calls=%async_computation | async-start | bytes 15040512 | tf_op jit(solution)/shard_map/all_gather | solution.py:560
  16.5 17.4 %collective-permute-start.1 = (bf16[255,8,128]{2,1,0:T(8,128)(2,1)S(1)}, bf16[255,8,128]{2,1,0:T(8,128)(2,1)}, u32[]{:S(2)}, u32[]{:S(2)}) collective-permute-start(bf16[255,8,128]{2,1,0:T(8,128)(2,1)S(1)} %get-tuple-element.255), channel_id=1, source_target_pairs={{8,0},{10,2},{12,4},{14,6},{16,8},{18,10},{20,12},{22,14},{24,16},... | collective-permute-start | bytes 1566728 | tf_op jit(solution)/shard_map/ppermute | solution.py:672
  21.6 23.4 %collective-permute-start.3 = (bf16[255,8,128]{2,1,0:T(8,128)(2,1)S(1)}, bf16[255,8,128]{2,1,0:T(8,128)(2,1)}, u32[]{:S(2)}, u32[]{:S(2)}) collective-permute-start(bf16[255,8,128]{2,1,0:T(8,128)(2,1)S(1)} %get-tuple-element.255), channel_id=1, source_target_pairs={{0,4},{2,6},{4,0},{6,2},{8,12},{10,14},{12,8},{14,10},{16,20},{18,... | collective-permute-start | bytes 1566728 | tf_op jit(solution)/shard_map/ppermute | solution.py:672
  23.1 21.9 %collective-permute-start = (bf16[255,8,128]{2,1,0:T(8,128)(2,1)S(1)}, bf16[255,8,128]{2,1,0:T(8,128)(2,1)}, u32[]{:S(2)}, u32[]{:S(2)}) collective-permute-start(bf16[255,8,128]{2,1,0:T(8,128)(2,1)S(1)} %get-tuple-element.256), channel_id=1, source_target_pairs={{0,8},{2,10},{4,12},{6,14},{8,16},{10,18},{12,20},{14,22},{16,24},... | collective-permute-start | bytes 1566728 | tf_op jit(solution)/shard_map/ppermute | solution.py:672
  23.1 21.9 %collective-permute-start.2 = (bf16[255,8,128]{2,1,0:T(8,128)(2,1)S(1)}, bf16[255,8,128]{2,1,0:T(8,128)(2,1)}, u32[]{:S(2)}, u32[]{:S(2)}) collective-permute-start(bf16[255,8,128]{2,1,0:T(8,128)(2,1)S(1)} %get-tuple-element.256), channel_id=1, source_target_pairs={{0,2},{2,0},{4,6},{6,4},{8,10},{10,8},{12,14},{14,12},{16,18},{18,... | collective-permute-start | bytes 1566728 | tf_op jit(solution)/shard_map/ppermute | solution.py:672
  24.6 22.9 %collective-permute-start.5 = (bf16[255,8,128]{2,1,0:T(8,128)(2,1)S(1)}, bf16[255,8,128]{2,1,0:T(8,128)(2,1)}, u32[]{:S(2)}, u32[]{:S(2)}) collective-permute-start(bf16[255,8,128]{2,1,0:T(8,128)(2,1)S(1)} %get-tuple-element.255), channel_id=1, source_target_pairs={{0,2},{2,0},{4,6},{6,4},{8,10},{10,8},{12,14},{14,12},{16,18},{18,... | collective-permute-start | bytes 1566728 | tf_op jit(solution)/shard_map/ppermute | solution.py:672
  33.9 13.6 %collective-permute-start.4 = (bf16[255,8,128]{2,1,0:T(8,128)(2,1)S(1)}, bf16[255,8,128]{2,1,0:T(8,128)(2,1)S(1)}, u32[]{:S(2)}, u32[]{:S(2)}) collective-permute-start(bf16[255,8,128]{2,1,0:T(8,128)(2,1)S(1)} %get-tuple-element.256), channel_id=1, source_target_pairs={{0,4},{2,6},{4,0},{6,2},{8,12},{10,14},{12,8},{14,10},{16,20},{18,... | collective-permute-start | bytes 1566728 | tf_op jit(solution)/shard_map/ppermute | solution.py:672
  48.2 20.4 %collective-permute-start.6 = (bf16[255,8,128]{2,1,0:T(8,128)(2,1)}, bf16[255,8,128]{2,1,0:T(8,128)(2,1)}, u32[]{:S(2)}, u32[]{:S(2)}) collective-permute-start(bf16[255,8,128]{2,1,0:T(8,128)(2,1)} %collective-permute-done), channel_id=1, source_target_pairs={{0,8},{2,10},{4,12},{6,14},{8,16},{10,18},{12,20},{14,22},{16,24},... | collective-permute-start | bytes 1566728 | tf_op jit(solution)/shard_map/ppermute | solution.py:672
  48.2 31.5 %collective-permute-start.8 = (bf16[255,8,128]{2,1,0:T(8,128)(2,1)}, bf16[255,8,128]{2,1,0:T(8,128)(2,1)}, u32[]{:S(2)}, u32[]{:S(2)}) collective-permute-start(bf16[255,8,128]{2,1,0:T(8,128)(2,1)} %collective-permute-done.1), channel_id=1, source_target_pairs={{8,0},{10,2},{12,4},{14,6},{16,8},{18,10},{20,12},{22,14},{24,16},... | collective-permute-start | bytes 1566728 | tf_op jit(solution)/shard_map/ppermute | solution.py:672
  62.7 15.0 %collective-permute-start.14 = (bf16[255,8,128]{2,1,0:T(8,128)(2,1)}, bf16[255,8,128]{2,1,0:T(8,128)(2,1)S(1)}, u32[]{:S(2)}, u32[]{:S(2)}) collective-permute-start(bf16[255,8,128]{2,1,0:T(8,128)(2,1)} %collective-permute-done.1), channel_id=1, source_target_pairs={{0,4},{2,6},{4,0},{6,2},{8,12},{10,14},{12,8},{14,10},{16,20},{18,... | collective-permute-start | bytes 1566728 | tf_op jit(solution)/shard_map/ppermute | solution.py:672
  63.2 16.0 %collective-permute-start.12 = (bf16[255,8,128]{2,1,0:T(8,128)(2,1)}, bf16[255,8,128]{2,1,0:T(8,128)(2,1)S(1)}, u32[]{:S(2)}, u32[]{:S(2)}) collective-permute-start(bf16[255,8,128]{2,1,0:T(8,128)(2,1)} %collective-permute-done), channel_id=1, source_target_pairs={{0,2},{2,0},{4,6},{6,4},{8,10},{10,8},{12,14},{14,12},{16,18},{18,... | collective-permute-start | bytes 1566728 | tf_op jit(solution)/shard_map/ppermute | solution.py:672
  64.7 24.7 %collective-permute-start.17 = (bf16[255,8,128]{2,1,0:T(8,128)(2,1)}, bf16[255,8,128]{2,1,0:T(8,128)(2,1)S(1)}, u32[]{:S(2)}, u32[]{:S(2)}) collective-permute-start(bf16[255,8,128]{2,1,0:T(8,128)(2,1)} %collective-permute-done.1), channel_id=1, source_target_pairs={{0,2},{2,0},{4,6},{6,4},{8,10},{10,8},{12,14},{14,12},{16,18},{18,... | collective-permute-start | bytes 1566728 | tf_op jit(solution)/shard_map/ppermute | solution.py:672
  68.7 22.2 %collective-permute-start.16 = (bf16[255,8,128]{2,1,0:T(8,128)(2,1)}, bf16[255,8,128]{2,1,0:T(8,128)(2,1)S(1)}, u32[]{:S(2)}, u32[]{:S(2)}) collective-permute-start(bf16[255,8,128]{2,1,0:T(8,128)(2,1)} %collective-permute-done), channel_id=1, source_target_pairs={{0,4},{2,6},{4,0},{6,2},{8,12},{10,14},{12,8},{14,10},{16,20},{18,... | collective-permute-start | bytes 1566728 | tf_op jit(solution)/shard_map/ppermute | solution.py:672
  77.7 22.9 %collective-permute-start.15 = (bf16[255,8,128]{2,1,0:T(8,128)(2,1)S(1)}, bf16[255,8,128]{2,1,0:T(8,128)(2,1)S(1)}, u32[]{:S(2)}, u32[]{:S(2)}) collective-permute-start(bf16[255,8,128]{2,1,0:T(8,128)(2,1)S(1)} %collective-permute-done.14), channel_id=1, source_target_pairs={{0,2},{2,0},{4,6},{6,4},{8,10},{10,8},{12,14},{14,12},{16,18},{18,... | collective-permute-start | bytes 1566728 | tf_op jit(solution)/shard_map/ppermute | solution.py:672
  79.2 22.9 %collective-permute-start.13 = (bf16[255,8,128]{2,1,0:T(8,128)(2,1)S(1)}, bf16[255,8,128]{2,1,0:T(8,128)(2,1)S(1)}, u32[]{:S(2)}, u32[]{:S(2)}) collective-permute-start(bf16[255,8,128]{2,1,0:T(8,128)(2,1)S(1)} %collective-permute-done.12), channel_id=1, source_target_pairs={{0,4},{2,6},{4,0},{6,2},{8,12},{10,14},{12,8},{14,10},{16,20},{18,... | collective-permute-start | bytes 1566728 | tf_op jit(solution)/shard_map/ppermute | solution.py:672
  79.7 32.0 %collective-permute-start.7 = (bf16[255,8,128]{2,1,0:T(8,128)(2,1)}, bf16[255,8,128]{2,1,0:T(8,128)(2,1)S(1)}, u32[]{:S(2)}, u32[]{:S(2)}) collective-permute-start(bf16[255,8,128]{2,1,0:T(8,128)(2,1)} %collective-permute-done.6), channel_id=1, source_target_pairs={{0,2},{2,0},{4,6},{6,4},{8,10},{10,8},{12,14},{14,12},{16,18},{18,... | collective-permute-start | bytes 1566728 | tf_op jit(solution)/shard_map/ppermute | solution.py:672
  89.4 38.2 %collective-permute-start.10 = (bf16[255,8,128]{2,1,0:T(8,128)(2,1)}, bf16[255,8,128]{2,1,0:T(8,128)(2,1)}, u32[]{:S(2)}, u32[]{:S(2)}) collective-permute-start(bf16[255,8,128]{2,1,0:T(8,128)(2,1)} %collective-permute-done.6), channel_id=1, source_target_pairs={{0,4},{2,6},{4,0},{6,2},{8,12},{10,14},{12,8},{14,10},{16,20},{18,... | collective-permute-start | bytes 1566728 | tf_op jit(solution)/shard_map/ppermute | solution.py:672
  90.9 35.4 %collective-permute-start.9 = (bf16[255,8,128]{2,1,0:T(8,128)(2,1)}, bf16[255,8,128]{2,1,0:T(8,128)(2,1)}, u32[]{:S(2)}, u32[]{:S(2)}) collective-permute-start(bf16[255,8,128]{2,1,0:T(8,128)(2,1)} %collective-permute-done.8), channel_id=1, source_target_pairs={{0,4},{2,6},{4,0},{6,2},{8,12},{10,14},{12,8},{14,10},{16,20},{18,... | collective-permute-start | bytes 1566728 | tf_op jit(solution)/shard_map/ppermute | solution.py:672
  100.6 28.5 %collective-permute-start.11 = (bf16[255,8,128]{2,1,0:T(8,128)(2,1)}, bf16[255,8,128]{2,1,0:T(8,128)(2,1)}, u32[]{:S(2)}, u32[]{:S(2)}) collective-permute-start(bf16[255,8,128]{2,1,0:T(8,128)(2,1)} %collective-permute-done.8), channel_id=1, source_target_pairs={{0,2},{2,0},{4,6},{6,4},{8,10},{10,8},{12,14},{14,12},{16,18},{18,... | collective-permute-start | bytes 1566728 | tf_op jit(solution)/shard_map/ppermute | solution.py:672
  102.1 27.7 %collective-permute-start.18 = (bf16[255,8,128]{2,1,0:T(8,128)(2,1)}, bf16[255,8,128]{2,1,0:T(8,128)(2,1)}, u32[]{:S(2)}, u32[]{:S(2)}) collective-permute-start(bf16[255,8,128]{2,1,0:T(8,128)(2,1)} %collective-permute-done.6), channel_id=1, source_target_pairs={{0,8},{2,10},{4,12},{6,14},{8,16},{10,18},{12,20},{14,22},{16,24},... | collective-permute-start | bytes 1566728 | tf_op jit(solution)/shard_map/ppermute | solution.py:672
  111.8 18.6 %collective-permute-start.19 = (bf16[255,8,128]{2,1,0:T(8,128)(2,1)}, bf16[255,8,128]{2,1,0:T(8,128)(2,1)}, u32[]{:S(2)}, u32[]{:S(2)}) collective-permute-start(bf16[255,8,128]{2,1,0:T(8,128)(2,1)} %collective-permute-done.8), channel_id=1, source_target_pairs={{8,0},{10,2},{12,4},{14,6},{16,8},{18,10},{20,12},{22,14},{24,16},... | collective-permute-start | bytes 1566728 | tf_op jit(solution)/shard_map/ppermute | solution.py:672
  126.3 15.0 %collective-permute-start.20 = (bf16[255,8,128]{2,1,0:T(8,128)(2,1)}, bf16[255,8,128]{2,1,0:T(8,128)(2,1)S(1)}, u32[]{:S(2)}, u32[]{:S(2)}) collective-permute-start(bf16[255,8,128]{2,1,0:T(8,128)(2,1)} %collective-permute-done.2), channel_id=1, source_target_pairs={{0,4},{2,6},{4,0},{6,2},{8,12},{10,14},{12,8},{14,10},{16,20},{18,... | collective-permute-start | bytes 1566728 | tf_op jit(solution)/shard_map/ppermute | solution.py:672
  127.6 15.1 %collective-permute-start.21 = (bf16[255,8,128]{2,1,0:T(8,128)(2,1)}, bf16[255,8,128]{2,1,0:T(8,128)(2,1)S(1)}, u32[]{:S(2)}, u32[]{:S(2)}) collective-permute-start(bf16[255,8,128]{2,1,0:T(8,128)(2,1)} %collective-permute-done.3), channel_id=1, source_target_pairs={{0,2},{2,0},{4,6},{6,4},{8,10},{10,8},{12,14},{14,12},{16,18},{18,... | collective-permute-start | bytes 1566728 | tf_op jit(solution)/shard_map/ppermute | solution.py:672
  129.1 23.4 %collective-permute-start.22 = (bf16[255,8,128]{2,1,0:T(8,128)(2,1)S(1)}, bf16[255,8,128]{2,1,0:T(8,128)(2,1)S(1)}, u32[]{:S(2)}, u32[]{:S(2)}) collective-permute-start(bf16[255,8,128]{2,1,0:T(8,128)(2,1)S(1)} %copy-done.89), channel_id=1, source_target_pairs={{0,4},{2,6},{4,0},{6,2},{8,12},{10,14},{12,8},{14,10},{16,20},{18,... | collective-permute-start | bytes 1566728 | tf_op jit(solution)/shard_map/ppermute | solution.py:672
  129.8 24.3 %collective-permute-start.23 = (bf16[255,8,128]{2,1,0:T(8,128)(2,1)}, bf16[255,8,128]{2,1,0:T(8,128)(2,1)S(1)}, u32[]{:S(2)}, u32[]{:S(2)}) collective-permute-start(bf16[255,8,128]{2,1,0:T(8,128)(2,1)} %collective-permute-done.9), channel_id=1, source_target_pairs={{0,2},{2,0},{4,6},{6,4},{8,10},{10,8},{12,14},{14,12},{16,18},{18,... | collective-permute-start | bytes 1566728 | tf_op jit(solution)/shard_map/ppermute | solution.py:672
  132.8 32.2 %collective-permute-start.24 = (bf16[255,8,128]{2,1,0:T(8,128)(2,1)}, bf16[255,8,128]{2,1,0:T(8,128)(2,1)S(1)}, u32[]{:S(2)}, u32[]{:S(2)}) collective-permute-start(bf16[255,8,128]{2,1,0:T(8,128)(2,1)} %collective-permute-done.18), channel_id=1, source_target_pairs={{0,2},{2,0},{4,6},{6,4},{8,10},{10,8},{12,14},{14,12},{16,18},{18,... | collective-permute-start | bytes 1566728 | tf_op jit(solution)/shard_map/ppermute | solution.py:672
  141.3 24.4 %collective-permute-start.25 = (bf16[255,8,128]{2,1,0:T(8,128)(2,1)}, bf16[255,8,128]{2,1,0:T(8,128)(2,1)S(1)}, u32[]{:S(2)}, u32[]{:S(2)}) collective-permute-start(bf16[255,8,128]{2,1,0:T(8,128)(2,1)} %collective-permute-done.19), channel_id=1, source_target_pairs={{0,4},{2,6},{4,0},{6,2},{8,12},{10,14},{12,8},{14,10},{16,20},{18,... | collective-permute-start | bytes 1566728 | tf_op jit(solution)/shard_map/ppermute | solution.py:672
  142.7 29.1 %collective-permute-start.26 = (bf16[255,8,128]{2,1,0:T(8,128)(2,1)}, bf16[255,8,128]{2,1,0:T(8,128)(2,1)S(1)}, u32[]{:S(2)}, u32[]{:S(2)}) collective-permute-start(bf16[255,8,128]{2,1,0:T(8,128)(2,1)} %collective-permute-done.18), channel_id=1, source_target_pairs={{0,4},{2,6},{4,0},{6,2},{8,12},{10,14},{12,8},{14,10},{16,20},{18,... | collective-permute-start | bytes 1566728 | tf_op jit(solution)/shard_map/ppermute | solution.py:672
  152.5 20.3 %collective-permute-start.27 = (bf16[255,8,128]{2,1,0:T(8,128)(2,1)}, bf16[255,8,128]{2,1,0:T(8,128)(2,1)S(1)}, u32[]{:S(2)}, u32[]{:S(2)}) collective-permute-start(bf16[255,8,128]{2,1,0:T(8,128)(2,1)} %collective-permute-done.19), channel_id=1, source_target_pairs={{0,2},{2,0},{4,6},{6,4},{8,10},{10,8},{12,14},{14,12},{16,18},{18,... | collective-permute-start | bytes 1566728 | tf_op jit(solution)/shard_map/ppermute | solution.py:672
  165.7 12.7 %collective-permute-start.29 = (bf16[255,8,128]{2,1,0:T(8,128)(2,1)S(1)}, bf16[255,8,128]{2,1,0:T(8,128)(2,1)S(1)}, u32[]{:S(2)}, u32[]{:S(2)}) collective-permute-start(bf16[255,8,128]{2,1,0:T(8,128)(2,1)S(1)} %collective-permute-done.25), channel_id=1, source_target_pairs={{0,2},{2,0},{4,6},{6,4},{8,10},{10,8},{12,14},{14,12},{16,18},{18,... | collective-permute-start | bytes 1566728 | tf_op jit(solution)/shard_map/ppermute | solution.py:672
  584.1 17.1 %collective-permute-start.48 = (bf16[1176,1024]{1,0:T(8,128)(2,1)}, bf16[1176,1024]{1,0:T(8,128)(2,1)}, u32[]{:S(2)}, u32[]{:S(2)}) collective-permute-start(bf16[1176,1024]{1,0:T(8,128)(2,1)} %convolution_convert_fusion.5), channel_id=1, source_target_pairs={{0,1},{1,0},{2,3},{3,2},{4,5},{5,4},{6,7},{7,6},{8,9},{9,8},{10,11... | collective-permute-start | bytes 7225352 | tf_op jit(solution)/shard_map/ppermute | solution.py:381
  615.8 46.3 %collective-permute-start.49 = (bf16[4,1,78,8,128]{4,3,2,1,0:T(8,128)(2,1)}, bf16[4,1,78,8,128]{4,3,2,1,0:T(8,128)(2,1)}, u32[]{:S(2)}, u32[]{:S(2)}) collective-permute-start(bf16[4,1,78,8,128]{4,3,2,1,0:T(8,128)(2,1)} %get-tuple-element.227), channel_id=1, source_target_pairs={{0,2},{2,0},{4,6},{6,4},{8,10},{10,8},{12,14},{14,12},{16,18},{18,... | collective-permute-start | bytes 1916936 | tf_op jit(solution)/shard_map/ppermute | solution.py:672
  617.3 44.8 %collective-permute-start.50 = (bf16[4,1,78,8,128]{4,3,2,1,0:T(8,128)(2,1)}, bf16[4,1,78,8,128]{4,3,2,1,0:T(8,128)(2,1)}, u32[]{:S(2)}, u32[]{:S(2)}) collective-permute-start(bf16[4,1,78,8,128]{4,3,2,1,0:T(8,128)(2,1)} %get-tuple-element.226), channel_id=1, source_target_pairs={{0,4},{2,6},{4,0},{6,2},{8,12},{10,14},{12,8},{14,10},{16,20},{18,... | collective-permute-start | bytes 1916936 | tf_op jit(solution)/shard_map/ppermute | solution.py:672
  617.9 44.2 %collective-permute-start.51 = (bf16[4,1,78,8,128]{4,3,2,1,0:T(8,128)(2,1)}, bf16[4,1,78,8,128]{4,3,2,1,0:T(8,128)(2,1)}, u32[]{:S(2)}, u32[]{:S(2)}) collective-permute-start(bf16[4,1,78,8,128]{4,3,2,1,0:T(8,128)(2,1)} %get-tuple-element.225), channel_id=1, source_target_pairs={{0,6},{2,4},{4,2},{6,0},{8,14},{10,12},{12,10},{14,8},{16,22},{18,... | collective-permute-start | bytes 1916936 | tf_op jit(solution)/shard_map/ppermute | solution.py:672
  673.5 85.2 %collective-permute-start.53 = (bf16[2,2,216,8,128]{4,3,2,0,1:T(8,128)(2,1)}, bf16[2,2,216,8,128]{4,3,2,0,1:T(8,128)(2,1)}, u32[]{:S(2)}, u32[]{:S(2)}) collective-permute-start(bf16[2,2,216,8,128]{4,3,2,0,1:T(8,128)(2,1)} %bitcast.353), channel_id=1, source_target_pairs={{0,2},{2,0},{4,6},{6,4},{8,10},{10,8},{12,14},{14,12},{16,18},{18,... | collective-permute-start | bytes 5308424 | tf_op jit(solution)/shard_map/ppermute | solution.py:672
  675.0 83.6 %collective-permute-start.54 = (bf16[2,2,216,8,128]{4,3,2,0,1:T(8,128)(2,1)}, bf16[2,2,216,8,128]{4,3,2,0,1:T(8,128)(2,1)}, u32[]{:S(2)}, u32[]{:S(2)}) collective-permute-start(bf16[2,2,216,8,128]{4,3,2,0,1:T(8,128)(2,1)} %bitcast.352), channel_id=1, source_target_pairs={{0,4},{2,6},{4,0},{6,2},{8,12},{10,14},{12,8},{14,10},{16,20},{18,... | collective-permute-start | bytes 5308424 | tf_op jit(solution)/shard_map/ppermute | solution.py:672
  675.6 40.1 %collective-permute-start.79 = (bf16[78,8,128]{2,1,0:T(8,128)(2,1)S(1)}, bf16[78,8,128]{2,1,0:T(8,128)(2,1)}, u32[]{:S(2)}, u32[]{:S(2)}) collective-permute-start(bf16[78,8,128]{2,1,0:T(8,128)(2,1)S(1)} %get-tuple-element.254), channel_id=1, source_target_pairs={{0,8},{2,10},{4,12},{6,14},{8,0},{10,2},{12,4},{14,6},{16,24},{18,... | collective-permute-start | bytes 479240 | tf_op jit(solution)/shard_map/ppermute | solution.py:672
  675.6 41.7 %collective-permute-start.80 = (bf16[78,8,128]{2,1,0:T(8,128)(2,1)}, bf16[78,8,128]{2,1,0:T(8,128)(2,1)}, u32[]{:S(2)}, u32[]{:S(2)}) collective-permute-start(bf16[78,8,128]{2,1,0:T(8,128)(2,1)} %get-tuple-element.253), channel_id=1, source_target_pairs={{0,16},{2,18},{4,20},{6,22},{8,24},{10,26},{12,28},{14,30},{16,0},... | collective-permute-start | bytes 479240 | tf_op jit(solution)/shard_map/ppermute | solution.py:672
  678.6 38.7 %collective-permute-start.81 = (bf16[78,8,128]{2,1,0:T(8,128)(2,1)}, bf16[78,8,128]{2,1,0:T(8,128)(2,1)}, u32[]{:S(2)}, u32[]{:S(2)}) collective-permute-start(bf16[78,8,128]{2,1,0:T(8,128)(2,1)} %get-tuple-element.252), channel_id=1, source_target_pairs={{0,24},{2,26},{4,28},{6,30},{8,16},{10,18},{12,20},{14,22},{16,8},... | collective-permute-start | bytes 479240 | tf_op jit(solution)/shard_map/ppermute | solution.py:672
  715.7 42.9 %collective-permute-start.55 = (bf16[2,2,216,8,128]{4,3,2,0,1:T(8,128)(2,1)S(1)}, bf16[2,2,216,8,128]{4,3,2,0,1:T(8,128)(2,1)S(1)}, u32[]{:S(2)}, u32[]{:S(2)}) collective-permute-start(bf16[2,2,216,8,128]{4,3,2,0,1:T(8,128)(2,1)S(1)} %bitcast.418), channel_id=1, source_target_pairs={{0,6},{2,4},{4,2},{6,0},{8,14},{10,12},{12,10},{14,8},{16,22},{18,... | collective-permute-start | bytes 5308424 | tf_op jit(solution)/shard_map/ppermute | solution.py:672
  768.5 14.8 %collective-permute-start.56 = (bf16[1176,1024]{1,0:T(8,128)(2,1)}, bf16[1176,1024]{1,0:T(8,128)(2,1)}, u32[]{:S(2)}, u32[]{:S(2)}) collective-permute-start(bf16[1176,1024]{1,0:T(8,128)(2,1)} %convolution_convert_fusion.1), channel_id=1, source_target_pairs={{0,1},{1,0},{2,3},{3,2},{4,5},{5,4},{6,7},{7,6},{8,9},{9,8},{10,11... | collective-permute-start | bytes 7225352 | tf_op jit(solution)/shard_map/ppermute | solution.py:381
  774.3 34.8 %collective-permute-start.61 = (bf16[1,4,108,8,128]{4,3,2,1,0:T(8,128)(2,1)}, bf16[1,4,108,8,128]{4,3,2,1,0:T(8,128)(2,1)}, u32[]{:S(2)}, u32[]{:S(2)}) collective-permute-start(bf16[1,4,108,8,128]{4,3,2,1,0:T(8,128)(2,1)} %get-tuple-element.235), channel_id=1, source_target_pairs={{0,2},{2,0},{4,6},{6,4},{8,10},{10,8},{12,14},{14,12},{16,18},{18,... | collective-permute-start | bytes 2654216 | tf_op jit(solution)/shard_map/ppermute | solution.py:672
  775.8 40.9 %collective-permute-start.62 = (bf16[1,4,108,8,128]{4,3,2,1,0:T(8,128)(2,1)}, bf16[1,4,108,8,128]{4,3,2,1,0:T(8,128)(2,1)}, u32[]{:S(2)}, u32[]{:S(2)}) collective-permute-start(bf16[1,4,108,8,128]{4,3,2,1,0:T(8,128)(2,1)} %get-tuple-element.234), channel_id=1, source_target_pairs={{0,4},{2,6},{4,0},{6,2},{8,12},{10,14},{12,8},{14,10},{16,20},{18,... | collective-permute-start | bytes 2654216 | tf_op jit(solution)/shard_map/ppermute | solution.py:672
  776.4 40.9 %collective-permute-start.63 = (bf16[1,4,108,8,128]{4,3,2,1,0:T(8,128)(2,1)}, bf16[1,4,108,8,128]{4,3,2,1,0:T(8,128)(2,1)}, u32[]{:S(2)}, u32[]{:S(2)}) collective-permute-start(bf16[1,4,108,8,128]{4,3,2,1,0:T(8,128)(2,1)} %get-tuple-element.233), channel_id=1, source_target_pairs={{0,6},{2,4},{4,2},{6,0},{8,14},{10,12},{12,10},{14,8},{16,22},{18,... | collective-permute-start | bytes 2654216 | tf_op jit(solution)/shard_map/ppermute | solution.py:672
  777.9 41.3 %collective-permute-start.57 = (bf16[216,8,128]{2,1,0:T(8,128)(2,1)}, bf16[216,8,128]{2,1,0:T(8,128)(2,1)}, u32[]{:S(2)}, u32[]{:S(2)}) collective-permute-start(bf16[216,8,128]{2,1,0:T(8,128)(2,1)} %get-tuple-element.238), channel_id=1, source_target_pairs={{0,8},{2,10},{4,12},{6,14},{8,0},{10,2},{12,4},{14,6},{16,24},{18,... | collective-permute-start | bytes 1327112 | tf_op jit(solution)/shard_map/ppermute | solution.py:672
  783.3 37.3 %collective-permute-start.58 = (bf16[216,8,128]{2,1,0:T(8,128)(2,1)}, bf16[216,8,128]{2,1,0:T(8,128)(2,1)}, u32[]{:S(2)}, u32[]{:S(2)}) collective-permute-start(bf16[216,8,128]{2,1,0:T(8,128)(2,1)} %get-tuple-element.237), channel_id=1, source_target_pairs={{0,16},{2,18},{4,20},{6,22},{8,24},{10,26},{12,28},{14,30},{16,0},... | collective-permute-start | bytes 1327112 | tf_op jit(solution)/shard_map/ppermute | solution.py:672
  809.4 13.1 %collective-permute-start.59 = (bf16[216,8,128]{2,1,0:T(8,128)(2,1)S(1)}, bf16[216,8,128]{2,1,0:T(8,128)(2,1)S(1)}, u32[]{:S(2)}, u32[]{:S(2)}) collective-permute-start(bf16[216,8,128]{2,1,0:T(8,128)(2,1)S(1)} %copy-done.104), channel_id=1, source_target_pairs={{0,24},{2,26},{4,28},{6,30},{8,16},{10,18},{12,20},{14,22},{16,8},... | collective-permute-start | bytes 1327112 | tf_op jit(solution)/shard_map/ppermute | solution.py:672
  816.7 22.6 %collective-permute-start.67 = (bf16[1,4,108,8,128]{4,3,2,1,0:T(8,128)(2,1)S(1)}, bf16[1,4,108,8,128]{4,3,2,1,0:T(8,128)(2,1)S(1)}, u32[]{:S(2)}, u32[]{:S(2)}) collective-permute-start(bf16[1,4,108,8,128]{4,3,2,1,0:T(8,128)(2,1)S(1)} %get-tuple-element.232), channel_id=1, source_target_pairs={{0,2},{2,0},{4,6},{6,4},{8,10},{10,8},{12,14},{14,12},{16,18},{18,... | collective-permute-start | bytes 2654216 | tf_op jit(solution)/shard_map/ppermute | solution.py:672
  817.3 39.6 %collective-permute-start.68 = (bf16[1,4,108,8,128]{4,3,2,1,0:T(8,128)(2,1)S(1)}, bf16[1,4,108,8,128]{4,3,2,1,0:T(8,128)(2,1)S(1)}, u32[]{:S(2)}, u32[]{:S(2)}) collective-permute-start(bf16[1,4,108,8,128]{4,3,2,1,0:T(8,128)(2,1)S(1)} %get-tuple-element.231), channel_id=1, source_target_pairs={{0,4},{2,6},{4,0},{6,2},{8,12},{10,14},{12,8},{14,10},{16,20},{18,... | collective-permute-start | bytes 2654216 | tf_op jit(solution)/shard_map/ppermute | solution.py:672
  819.2 39.6 %collective-permute-start.69 = (bf16[1,4,108,8,128]{4,3,2,1,0:T(8,128)(2,1)S(1)}, bf16[1,4,108,8,128]{4,3,2,1,0:T(8,128)(2,1)S(1)}, u32[]{:S(2)}, u32[]{:S(2)}) collective-permute-start(bf16[1,4,108,8,128]{4,3,2,1,0:T(8,128)(2,1)S(1)} %get-tuple-element.230), channel_id=1, source_target_pairs={{0,6},{2,4},{4,2},{6,0},{8,14},{10,12},{12,10},{14,8},{16,22},{18,... | collective-permute-start | bytes 2654216 | tf_op jit(solution)/shard_map/ppermute | solution.py:672
  820.6 68.1 %collective-permute-start.89 = (f32[17920]{0:T(1024)S(1)}, f32[17920]{0:T(1024)S(1)}, u32[]{:S(2)}, u32[]{:S(2)}) collective-permute-start(f32[17920]{0:T(1024)S(1)} %constant_dynamic-update-slice_fusion.10), channel_id=1, source_target_pairs={{0,1},{1,0},{2,3},{3,2},{4,5},{5,4},{6,7},{7,6},{8,9},{9,8},{10,11... | collective-permute-start | bytes 215048 | tf_op jit(solution)/shard_map/ppermute | solution.py:401
  825.0 35.6 %collective-permute-start.64 = (bf16[108,8,128]{2,1,0:T(8,128)(2,1)S(1)}, bf16[108,8,128]{2,1,0:T(8,128)(2,1)S(1)}, u32[]{:S(2)}, u32[]{:S(2)}) collective-permute-start(bf16[108,8,128]{2,1,0:T(8,128)(2,1)S(1)} %get-tuple-element.249), channel_id=1, source_target_pairs={{0,8},{2,10},{4,12},{6,14},{8,0},{10,2},{12,4},{14,6},{16,24},{18,... | collective-permute-start | bytes 663560 | tf_op jit(solution)/shard_map/ppermute | solution.py:672
  839.3 24.6 %collective-permute-start.65 = (bf16[108,8,128]{2,1,0:T(8,128)(2,1)S(1)}, bf16[108,8,128]{2,1,0:T(8,128)(2,1)S(1)}, u32[]{:S(2)}, u32[]{:S(2)}) collective-permute-start(bf16[108,8,128]{2,1,0:T(8,128)(2,1)S(1)} %get-tuple-element.248), channel_id=1, source_target_pairs={{0,16},{2,18},{4,20},{6,22},{8,24},{10,26},{12,28},{14,30},{16,0},... | collective-permute-start | bytes 663560 | tf_op jit(solution)/shard_map/ppermute | solution.py:672
  858.8 31.2 %collective-permute-start.60 = (bf16[216,8,128]{2,1,0:T(8,128)(2,1)S(1)}, bf16[216,8,128]{2,1,0:T(8,128)(2,1)S(1)}, u32[]{:S(2)}, u32[]{:S(2)}) collective-permute-start(bf16[216,8,128]{2,1,0:T(8,128)(2,1)S(1)} %fusion.84), channel_id=1, source_target_pairs={{0,16},{2,18},{4,20},{6,22},{8,24},{10,26},{12,28},{14,30},{1,17},... | collective-permute-start | bytes 1327112 | tf_op jit(solution)/shard_map/ppermute | solution.py:672
  860.6 18.3 %collective-permute-start.73 = (bf16[108,8,128]{2,1,0:T(8,128)(2,1)S(1)}, bf16[108,8,128]{2,1,0:T(8,128)(2,1)S(1)}, u32[]{:S(2)}, u32[]{:S(2)}) collective-permute-start(bf16[108,8,128]{2,1,0:T(8,128)(2,1)S(1)} %get-tuple-element.246), channel_id=1, source_target_pairs={{0,8},{2,10},{4,12},{6,14},{8,0},{10,2},{12,4},{14,6},{16,24},{18,... | collective-permute-start | bytes 663560 | tf_op jit(solution)/shard_map/ppermute | solution.py:672
  863.8 19.8 %collective-permute-start.74 = (bf16[108,8,128]{2,1,0:T(8,128)(2,1)S(1)}, bf16[108,8,128]{2,1,0:T(8,128)(2,1)S(1)}, u32[]{:S(2)}, u32[]{:S(2)}) collective-permute-start(bf16[108,8,128]{2,1,0:T(8,128)(2,1)S(1)} %get-tuple-element.245), channel_id=1, source_target_pairs={{0,16},{2,18},{4,20},{6,22},{8,24},{10,26},{12,28},{14,30},{16,0},... | collective-permute-start | bytes 663560 | tf_op jit(solution)/shard_map/ppermute | solution.py:672
  867.1 20.8 %collective-permute-start.75 = (bf16[108,8,128]{2,1,0:T(8,128)(2,1)S(1)}, bf16[108,8,128]{2,1,0:T(8,128)(2,1)S(1)}, u32[]{:S(2)}, u32[]{:S(2)}) collective-permute-start(bf16[108,8,128]{2,1,0:T(8,128)(2,1)S(1)} %get-tuple-element.244), channel_id=1, source_target_pairs={{0,24},{2,26},{4,28},{6,30},{8,16},{10,18},{12,20},{14,22},{16,8},... | collective-permute-start | bytes 663560 | tf_op jit(solution)/shard_map/ppermute | solution.py:672
  878.9 12.4 %collective-permute-start.70 = (bf16[108,8,128]{2,1,0:T(8,128)(2,1)S(1)}, bf16[108,8,128]{2,1,0:T(8,128)(2,1)S(1)}, u32[]{:S(2)}, u32[]{:S(2)}) collective-permute-start(bf16[108,8,128]{2,1,0:T(8,128)(2,1)S(1)} %fusion.110), channel_id=1, source_target_pairs={{0,8},{2,10},{4,12},{6,14},{1,9},{3,11},{5,13},{7,15}} | collective-permute-start | bytes 663560 | tf_op jit(solution)/shard_map/ppermute | solution.py:672
  888.7 21.7 %collective-permute-start.76 = (bf16[108,8,128]{2,1,0:T(8,128)(2,1)S(1)}, bf16[108,8,128]{2,1,0:T(8,128)(2,1)S(1)}, u32[]{:S(2)}, u32[]{:S(2)}) collective-permute-start(bf16[108,8,128]{2,1,0:T(8,128)(2,1)S(1)} %fusion.107), channel_id=1, source_target_pairs={{8,0},{10,2},{12,4},{14,6},{9,1},{11,3},{13,5},{15,7}} | collective-permute-start | bytes 663560 | tf_op jit(solution)/shard_map/ppermute | solution.py:672
  890.0 31.5 %collective-permute-start.77 = (bf16[108,8,128]{2,1,0:T(8,128)(2,1)S(1)}, bf16[108,8,128]{2,1,0:T(8,128)(2,1)S(1)}, u32[]{:S(2)}, u32[]{:S(2)}) collective-permute-start(bf16[108,8,128]{2,1,0:T(8,128)(2,1)S(1)} %fusion.107), channel_id=1, source_target_pairs={{16,0},{18,2},{20,4},{22,6},{17,1},{19,3},{21,5},{23,7}} | collective-permute-start | bytes 663560 | tf_op jit(solution)/shard_map/ppermute | solution.py:672
  891.3 30.2 %collective-permute-start.78 = (bf16[108,8,128]{2,1,0:T(8,128)(2,1)S(1)}, bf16[108,8,128]{2,1,0:T(8,128)(2,1)S(1)}, u32[]{:S(2)}, u32[]{:S(2)}) collective-permute-start(bf16[108,8,128]{2,1,0:T(8,128)(2,1)S(1)} %fusion.107), channel_id=1, source_target_pairs={{24,0},{26,2},{28,4},{30,6},{25,1},{27,3},{29,5},{31,7}} | collective-permute-start | bytes 663560 | tf_op jit(solution)/shard_map/ppermute | solution.py:672
  892.7 35.5 %collective-permute-start.90 = (f32[17920]{0:T(1024)S(1)}, f32[17920]{0:T(1024)S(1)}, u32[]{:S(2)}, u32[]{:S(2)}) collective-permute-start(f32[17920]{0:T(1024)S(1)} %add.1320), channel_id=1, source_target_pairs={{0,2},{2,0},{4,6},{6,4},{8,10},{10,8},{12,14},{14,12},{16,18},{18,... | collective-permute-start | bytes 215048 | tf_op jit(solution)/shard_map/ppermute | solution.py:401
  892.8 36.8 %collective-permute-start.91 = (f32[17920]{0:T(1024)S(1)}, f32[17920]{0:T(1024)S(1)}, u32[]{:S(2)}, u32[]{:S(2)}) collective-permute-start(f32[17920]{0:T(1024)S(1)} %add.1320), channel_id=1, source_target_pairs={{0,4},{2,6},{4,0},{6,2},{8,12},{10,14},{12,8},{14,10},{16,20},{18,... | collective-permute-start | bytes 215048 | tf_op jit(solution)/shard_map/ppermute | solution.py:401
  910.4 19.2 %collective-permute-start.92 = (f32[17920]{0:T(1024)S(1)}, f32[17920]{0:T(1024)S(1)}, u32[]{:S(2)}, u32[]{:S(2)}) collective-permute-start(f32[17920]{0:T(1024)S(1)} %add.1320), channel_id=1, source_target_pairs={{0,6},{2,4},{4,2},{6,0},{8,14},{10,12},{12,10},{14,8},{16,22},{18,... | collective-permute-start | bytes 215048 | tf_op jit(solution)/shard_map/ppermute | solution.py:401
  (242 other events, 3384.4 us)
Sparse Core Ops, SparseCore 0:
  190.1 164.8 all-gather.1
